TPU v7x, 256 devices: a whole 4x4x8 slice. The times are simulated.
256 devices in a mesh: segment: 4 (over y), rows: 64 (over x, z, core).
Axes of the slice: x: 4, y: 4, z: 8, core: 2. Of those that a mesh axis runs over, the one named last changes fastest.
Arguments:
- hidden_in: bfloat16 [4096, 8192], P('rows'), may hold values from -6 to 6
- request_adapter: int32 [4096, 1], P('rows'), may hold values from 0 to 63; in each aligned block of 64 rows (0 to 63, 64 to 127, ...) at most 2 rows name the same one
- home_slot: int32 [64], replicated, may hold values from 0 to 63, each once
- gains: float32 [4, 8192], P('segment'), may hold values from 0.5 to 1.5
- shrink_tiles: bfloat16 [4, 64, 8192, 64], P('segment', 'rows'), may hold values from -0.0625 to 0.0625
- expand_tiles: bfloat16 [4, 64, 64, 8192], P('segment', 'rows'), may hold values from -0.75 to 0.75
Outputs:
- section_out: bfloat16 [4, 4096, 8192], P('segment', 'rows')
Inputs may be any that keep to these rules, and one draw needn't show every extreme that they name: `request_adapter`: no adapter is used by more than 2 requests of one index of rows (the requests of one device); some adapter is used by exactly 2 of them. Every adapter is used by some request. A permutation: adapter a's factors stand at index home_slot[a] of the adapter dimension of shrink_tiles and expand_tiles.
All inputs are finite; a program needn't handle non-finite values.
Results may differ from a plain program's by a relative error of at most 0.0095.
Values may be sent and summed in bfloat16 or wider, within the bound.
No kernel may reach another device: no remote copies, remote signals or barrier semaphores. Data moves between devices by JAX's collectives and lax.ppermute only.
A program may use at most 64 MiB of HBM per device.

v0:
```python
import jax
import jax.numpy as jnp
from jax import lax
from jax.sharding import PartitionSpec as P


def from_behind(value, axis, steps):
    count = lax.axis_size(axis)
    initial, last = (max(0, -steps), min(count, count - steps))
    return lax.ppermute(value, axis, [(source, source + steps) for source in range(initial, last)])


def normalize(rows, gain):
    values = rows.astype(jnp.float32)
    scale = lax.rsqrt(jnp.mean(values * values, axis=-1, keepdims=True) + 1e-05)
    return (values * scale * gain).astype(jnp.bfloat16)


def shrink_expand(normed, shrink, expand):
    lower = jnp.einsum("sajd,adr->sajr", normed, shrink, preferred_element_type=jnp.float32).astype(
        jnp.bfloat16
    )
    return jnp.einsum("sajr,ard->sajd", lower, expand, preferred_element_type=jnp.float32).astype(
        jnp.bfloat16
    )


def local(hidden_in, request_adapter, home_slot, gains, shrink_tiles, expand_tiles):
    peers = lax.axis_size("rows")
    sections = lax.axis_size("segment")
    segment_index = lax.axis_index("segment")
    owned = shrink_tiles.shape[1]
    width = hidden_in.shape[1]
    gain = gains[0]
    shrink = shrink_tiles[0]
    expand = expand_tiles[0]
    adapter_ids = request_adapter[:, 0]
    count = adapter_ids.shape[0]
    total = home_slot.shape[0]
    depth = max(2, 2 * count // total)
    catalog = jnp.arange(total, dtype=jnp.int32)
    storage = jnp.sum(
        jnp.where(adapter_ids[:, None] == catalog[None, :], home_slot[None, :], 0), axis=1
    )
    order = jnp.arange(count, dtype=jnp.int32)
    same_adapter = adapter_ids[:, None] == adapter_ids[None, :]
    earlier = jnp.sum((same_adapter & (order[None, :] < order[:, None])).astype(jnp.int32), axis=1)
    target = storage * depth + earlier
    places = jnp.arange(total * depth, dtype=jnp.int32)
    packing = (places[:, None] == target[None, :]).astype(jnp.bfloat16)
    unpacking = packing.T
    current = hidden_in
    kept = hidden_in
    for section in range(sections):
        normed = (
            jnp.dot(packing, normalize(current, gain), preferred_element_type=jnp.float32)
            .astype(jnp.bfloat16)
            .reshape(peers, owned, depth, width)
        )
        returned = lax.all_to_all(
            shrink_expand(
                lax.all_to_all(normed, "rows", split_axis=0, concat_axis=0, tiled=True),
                shrink,
                expand,
            ),
            "rows",
            split_axis=0,
            concat_axis=0,
            tiled=True,
        )
        updated = (
            current.astype(jnp.float32)
            + jnp.dot(
                unpacking,
                returned.reshape(total * depth, width),
                preferred_element_type=jnp.float32,
            )
        ).astype(jnp.bfloat16)
        kept = jnp.where(segment_index == section, updated, kept)
        if section + 1 < sections:
            current = from_behind(updated, "segment", 1)
    return kept[None]


def solution(mesh):
    return jax.shard_map(
        local,
        mesh=mesh,
        in_specs=(
            P("rows", None),
            P("rows", None),
            P(),
            P("segment", None),
            P("segment", "rows", None, None),
            P("segment", "rows", None, None),
        ),
        out_specs=P("segment", "rows", None),
        check_vma=False,
    )
```

profile of v0, /device:TPU:1, one launch (start us, length us, event | category | flops | bytes accessed | tf_op | source)
XLA Modules:
  0.0 638.5 jit_solution(9207534827622171612)
XLA Ops:
  4.6 2.7 reshape.116
  7.2 64.5 %all_to_all.40 = bf16[64,1,2,8192]{3,2,1,0:T(2,128)(2,1)} all-to-all(bf16[64,1,2,8192]{3,2,1,0:T(2,128)(2,1)} %bitcast.94), channel_id=1, replica_groups=mesh['segment'=4,'rows'=64] {'rows'}, dimensions={0} | all-to-all | bytes 4194304 | tf_op jit(solution)/shard_map/all_to_all | solution.py:62
  71.7 5.4 fusion
  77.1 3.8 copy.25
  80.9 57.0 %all_to_all.41 = bf16[64,1,2,8192]{3,2,1,0:T(2,128)(2,1)} all-to-all(bf16[64,1,2,8192]{3,2,1,0:T(2,128)(2,1)S(1)} %copy.25), channel_id=1, replica_groups=mesh['segment'=4,'rows'=64] {'rows'}, dimensions={0} | all-to-all | bytes 4194304 | tf_op jit(solution)/shard_map/all_to_all | solution.py:60
  137.8 4.2 reshape.120
  144.2 3.3 collective-permute-start
  147.4 22.1 %collective-permute-done = bf16[64,8192]{1,0:T(8,128)(2,1)S(1)} collective-permute-done((bf16[64,8192]{1,0:T(8,128)(2,1)S(1)}, bf16[64,8192]{1,0:T(8,128)(2,1)S(1)}, u32[]{:S(2)}, u32[]{:S(2)}) %collective-permute-start) | collective-permute-done | bytes 1048608 | tf_op jit(solution)/shard_map/ppermute | solution.py:10
  172.5 4.4 reshape.121
  176.9 57.8 %all_to_all.42 = bf16[64,1,2,8192]{3,2,1,0:T(2,128)(2,1)} all-to-all(bf16[64,1,2,8192]{3,2,1,0:T(2,128)(2,1)} %bitcast.95), channel_id=1, replica_groups=mesh['segment'=4,'rows'=64] {'rows'}, dimensions={0} | all-to-all | bytes 4194304 | tf_op jit(solution)/shard_map/all_to_all | solution.py:62
  234.7 5.5 fusion.1
  240.2 3.8 copy.28
  244.0 57.0 %all_to_all.43 = bf16[64,1,2,8192]{3,2,1,0:T(2,128)(2,1)} all-to-all(bf16[64,1,2,8192]{3,2,1,0:T(2,128)(2,1)S(1)} %copy.28), channel_id=1, replica_groups=mesh['segment'=4,'rows'=64] {'rows'}, dimensions={0} | all-to-all | bytes 4194304 | tf_op jit(solution)/shard_map/all_to_all | solution.py:60
  300.9 4.1 reshape.123
  307.4 4.2 collective-permute-start.1
  311.6 22.1 %collective-permute-done.1 = bf16[64,8192]{1,0:T(8,128)(2,1)S(1)} collective-permute-done((bf16[64,8192]{1,0:T(8,128)(2,1)S(1)}, bf16[64,8192]{1,0:T(8,128)(2,1)S(1)}, u32[]{:S(2)}, u32[]{:S(2)}) %collective-permute-start.1) | collective-permute-done | bytes 1048608 | tf_op jit(solution)/shard_map/ppermute | solution.py:10
  336.7 4.4 reshape.124
  341.1 57.8 %all_to_all.44 = bf16[64,1,2,8192]{3,2,1,0:T(2,128)(2,1)} all-to-all(bf16[64,1,2,8192]{3,2,1,0:T(2,128)(2,1)} %bitcast.96), channel_id=1, replica_groups=mesh['segment'=4,'rows'=64] {'rows'}, dimensions={0} | all-to-all | bytes 4194304 | tf_op jit(solution)/shard_map/all_to_all | solution.py:62
  398.9 5.5 fusion.2
  404.3 3.8 copy.31
  408.1 57.0 %all_to_all.45 = bf16[64,1,2,8192]{3,2,1,0:T(2,128)(2,1)} all-to-all(bf16[64,1,2,8192]{3,2,1,0:T(2,128)(2,1)S(1)} %copy.31), channel_id=1, replica_groups=mesh['segment'=4,'rows'=64] {'rows'}, dimensions={0} | all-to-all | bytes 4194304 | tf_op jit(solution)/shard_map/all_to_all | solution.py:60
  465.1 4.1 reshape.126
  471.5 4.2 collective-permute-start.2
  475.7 22.1 %collective-permute-done.2 = bf16[64,8192]{1,0:T(8,128)(2,1)S(1)} collective-permute-done((bf16[64,8192]{1,0:T(8,128)(2,1)S(1)}, bf16[64,8192]{1,0:T(8,128)(2,1)S(1)}, u32[]{:S(2)}, u32[]{:S(2)}) %collective-permute-start.2) | collective-permute-done | bytes 1048608 | tf_op jit(solution)/shard_map/ppermute | solution.py:10
  500.8 4.4 reshape.127
  505.2 57.8 %all_to_all.46 = bf16[64,1,2,8192]{3,2,1,0:T(2,128)(2,1)} all-to-all(bf16[64,1,2,8192]{3,2,1,0:T(2,128)(2,1)} %bitcast.97), channel_id=1, replica_groups=mesh['segment'=4,'rows'=64] {'rows'}, dimensions={0} | all-to-all | bytes 4194304 | tf_op jit(solution)/shard_map/all_to_all | solution.py:62
  563.0 5.5 fusion.3
  568.5 5.1 copy.34
  573.6 6.0 all-to-all-start.7
  579.6 51.1 %all-to-all-done.7 = bf16[64,1,2,8192]{3,2,1,0:T(2,128)(2,1)} async-done(((bf16[64,1,2,8192]{3,2,1,0:T(2,128)(2,1)}), bf16[64,1,2,8192]{3,2,1,0:T(2,128)(2,1)}, u32[]{:S(2)}, u32[]{:S(2)}) %all-to-all-start.7) | async-done | bytes 2097184 | tf_op jit(solution)/shard_map/all_to_all | solution.py:60
  630.7 4.1 reshape.129
  634.9 3.6 fusion.9
  (39 shorter events, 20.4 us)
Async XLA Ops:
  0.0 71.7 %copy-start = (bf16[1,1,64,8192]{3,2,1,0:T(8,128)(2,1)S(1)}, bf16[1,1,64,8192]{3,2,1,0:T(8,128)(2,1)}, u32[]{:S(2)}) copy-start(bf16[1,1,64,8192]{3,2,1,0:T(8,128)(2,1)} %param.11) | copy-start | bytes 3145732
  7.2 64.5 %copy-start.2 = (bf16[1,1,8192,64]{2,3,1,0:T(8,128)(2,1)S(1)}, bf16[1,1,8192,64]{2,3,1,0:T(8,128)(2,1)}, u32[]{:S(2)}) copy-start(bf16[1,1,8192,64]{2,3,1,0:T(8,128)(2,1)} %param.10) | copy-start | bytes 3145732
  137.8 4.2 copy-start.1
  142.1 28.4 %copy-start.10 = (f32[1,8192]{1,0:T(1,128)S(1)}, f32[1,8192]{1,0:T(1,128)}, u32[]{:S(2)}) copy-start(f32[1,8192]{1,0:T(1,128)} %param.9) | copy-start | bytes 98308
  144.2 25.4 %copy-start.7 = (bf16[64,8192]{1,0:T(8,128)(2,1)}, bf16[64,8192]{1,0:T(8,128)(2,1)S(1)}, u32[]{:S(2)}) copy-start(bf16[64,8192]{1,0:T(8,128)(2,1)S(1)} %fusion.4) | copy-start | bytes 3145732
  144.2 25.3 %collective-permute-start = (bf16[64,8192]{1,0:T(8,128)(2,1)S(1)}, bf16[64,8192]{1,0:T(8,128)(2,1)S(1)}, u32[]{:S(2)}, u32[]{:S(2)}) collective-permute-start(bf16[64,8192]{1,0:T(8,128)(2,1)S(1)} %fusion.4), channel_id=1, source_target_pairs={{0,64},{64,128},{128,192},{1,65},{65,129},{129,193},{2,66},{66,130... | collective-permute-start | bytes 3145736 | tf_op jit(solution)/shard_map/ppermute | solution.py:10
  169.5 1.0 copy-start.5
  307.4 26.3 %copy-start.8 = (bf16[64,8192]{1,0:T(8,128)(2,1)}, bf16[64,8192]{1,0:T(8,128)(2,1)S(1)}, u32[]{:S(2)}) copy-start(bf16[64,8192]{1,0:T(8,128)(2,1)S(1)} %fusion.5) | copy-start | bytes 3145732
  307.4 26.2 %collective-permute-start.1 = (bf16[64,8192]{1,0:T(8,128)(2,1)S(1)}, bf16[64,8192]{1,0:T(8,128)(2,1)S(1)}, u32[]{:S(2)}, u32[]{:S(2)}) collective-permute-start(bf16[64,8192]{1,0:T(8,128)(2,1)S(1)} %fusion.5), channel_id=1, source_target_pairs={{0,64},{64,128},{128,192},{1,65},{65,129},{129,193},{2,66},{66,130... | collective-permute-start | bytes 3145736 | tf_op jit(solution)/shard_map/ppermute | solution.py:10
  333.6 1.0 copy-start.6
  471.5 26.2 %copy-start.9 = (bf16[64,8192]{1,0:T(8,128)(2,1)}, bf16[64,8192]{1,0:T(8,128)(2,1)S(1)}, u32[]{:S(2)}) copy-start(bf16[64,8192]{1,0:T(8,128)(2,1)S(1)} %fusion.6) | copy-start | bytes 3145732
  471.5 26.2 %collective-permute-start.2 = (bf16[64,8192]{1,0:T(8,128)(2,1)S(1)}, bf16[64,8192]{1,0:T(8,128)(2,1)S(1)}, u32[]{:S(2)}, u32[]{:S(2)}) collective-permute-start(bf16[64,8192]{1,0:T(8,128)(2,1)S(1)} %fusion.6), channel_id=1, source_target_pairs={{0,64},{64,128},{128,192},{1,65},{65,129},{129,193},{2,66},{66,130... | collective-permute-start | bytes 3145736 | tf_op jit(solution)/shard_map/ppermute | solution.py:10
  497.8 1.0 copy-start.3
  573.6 57.2 %all-to-all-start.7 = ((bf16[64,1,2,8192]{3,2,1,0:T(2,128)(2,1)}), bf16[64,1,2,8192]{3,2,1,0:T(2,128)(2,1)}, u32[]{:S(2)}, u32[]{:S(2)}) async-start(bf16[64,1,2,8192]{3,2,1,0:T(2,128)(2,1)} %copy.34), calls=%async_computation.7 | async-start | bytes 4194304 | tf_op jit(solution)/shard_map/all_to_all | solution.py:60
  579.6 55.3 %copy-start.4 = (bf16[64,8192]{1,0:T(8,128)(2,1)S(1)}, bf16[64,8192]{1,0:T(8,128)(2,1)}, u32[]{:S(2)}) copy-start(bf16[64,8192]{1,0:T(8,128)(2,1)} %copy-done.3) | copy-start | bytes 3145732
where the time goes:
time: 640 us; the launch traced here: 638 us
  blocking collectives  409 us (64%)
  waiting for transfers between devices  117 us (18%)
  local copies, waits for them, and re-layouts  50.8 us (8%)
  matrix products  40.3 us (6%)
  starting transfers between devices  17.6 us (3%)
    all_to_all x4, blocking collectives, local(): lax.all_to_all(normed, 'rows', split_axis=0, concat_axis=0, tiled=True)  238 us
    all_to_all x3, blocking collectives, local(): lax.all_to_all(shrink_expand(lax.all_to_all(normed, 'rows', split_axis=0,...  171 us
    ppermute x3, waiting for transfers between devices, from_behind(): lax.ppermute(value, axis, [(source, source + steps) for source in range(i...  66.2 us
    all_to_all x1, waiting for transfers between devices, local(): lax.all_to_all(shrink_expand(lax.all_to_all(normed, 'rows', split_axis=0,...  51.1 us
    dot_general x4, matrix products, shrink_expand(): jnp.einsum('sajr,ard->sajd', lower, expand, preferred_element_type=jnp.fl...  21.8 us
    reshape x4, local copies, waits for them, and re-layouts, local(): returned.reshape(total * depth, width)  16.6 us
    convert_element_type x4, local copies, waits for them, and re-layouts, shrink_expand(): jnp.einsum('sajr,ard->sajd', lower, expand, preferred_element_type=jnp.fl...  16.4 us
    reshape x4, local copies, waits for them, and re-layouts, local(): normed = jnp.dot(packing, normalize(current, gain), preferred_element_typ...  15.8 us
  transfers between devices with their start and end apart: 4, of which 4 were waited for; matrix products, arithmetic and copies ran while one was open for 0% of the time, Pallas kernels for 0%

commit v1 on v0

v1 whole, which is shorter than its diff:
```python
import jax
import jax.numpy as jnp
from jax import lax
from jax.sharding import PartitionSpec as P


def shifted(value, axis, steps):
    count = lax.axis_size(axis)
    return lax.ppermute(value, axis, [(source, (source + steps) % count) for source in range(count)])


def local(hidden_in, request_adapter, home_slot, gains, shrink_tiles, expand_tiles):
    peers = lax.axis_size("rows")
    sections = lax.axis_size("segment")
    plane = lax.axis_index("segment")
    count, width = hidden_in.shape
    part = width // sections
    total = home_slot.shape[0]
    rank = expand_tiles.shape[2]
    depth = max(2, 2 * count // total)
    adapter_ids = request_adapter[:, 0]
    catalog = jnp.arange(total, dtype=jnp.int32)
    storage = jnp.sum(
        jnp.where(adapter_ids[:, None] == catalog[None, :], home_slot[None, :], 0), axis=1
    )
    order = jnp.arange(count, dtype=jnp.int32)
    same_adapter = adapter_ids[:, None] == adapter_ids[None, :]
    earlier = jnp.sum((same_adapter & (order[None, :] < order[:, None])).astype(jnp.int32), axis=1)
    target = storage * depth + earlier
    places = jnp.arange(total * depth, dtype=jnp.int32)
    packing = (places[:, None] == target[None, :]).astype(jnp.bfloat16)
    unpacking = packing.T

    mine = lax.dynamic_slice(hidden_in, (0, plane * part), (count, part))
    packed = jnp.dot(packing, mine, preferred_element_type=jnp.float32).astype(jnp.bfloat16)
    held = lax.all_to_all(
        packed.reshape(peers, depth, part), "rows", split_axis=0, concat_axis=0, tiled=True
    ).reshape(peers * depth, part)

    scaled = (shrink_tiles[0, 0].astype(jnp.float32) * gains[0][:, None]).astype(jnp.bfloat16)
    factors = jnp.concatenate([scaled.T, expand_tiles[0, 0]], axis=0)

    def quarter(steps):
        start = ((plane + steps) % sections) * part
        return lax.dynamic_slice(factors, (0, start), (2 * rank, part))

    arrived = jnp.stack(
        [quarter(0)] + [shifted(quarter(steps), "segment", steps) for steps in range(1, sections)]
    )

    current = held
    results = []
    for section in range(sections):
        own = lax.dynamic_index_in_dim(arrived, (plane - section) % sections, 0, keepdims=False)
        values = current.astype(jnp.float32)
        squares = jnp.sum(values * values, axis=1, keepdims=True)
        product = lax.dot_general(
            current, own[:rank], (((1,), (1,)), ((), ())), preferred_element_type=jnp.float32
        )
        partial = jnp.concatenate([product, jnp.broadcast_to(squares, product.shape)], axis=1)
        summed = partial
        for steps in range(1, sections):
            summed = summed + shifted(partial, "segment", steps)
        scale = lax.rsqrt(summed[:, rank:] / width + 1e-05)
        lower = (summed[:, :rank] * scale).astype(jnp.bfloat16)
        delta = jnp.dot(lower, own[rank:], preferred_element_type=jnp.float32)
        current = (values + delta).astype(jnp.bfloat16)
        results.append(current.reshape(peers, depth, part))

    back = lax.all_to_all(
        jnp.concatenate(results, axis=0),
        ("segment", "rows"),
        split_axis=0,
        concat_axis=0,
        tiled=True,
    ).reshape(sections, total * depth, part)
    rows = [
        jnp.dot(unpacking, back[piece], preferred_element_type=jnp.float32).astype(jnp.bfloat16)
        for piece in range(sections)
    ]
    return jnp.concatenate(rows, axis=1)[None]


def solution(mesh):
    return jax.shard_map(
        local,
        mesh=mesh,
        in_specs=(
            P("rows", None),
            P("rows", None),
            P(),
            P("segment", None),
            P("segment", "rows", None, None),
            P("segment", "rows", None, None),
        ),
        out_specs=P("segment", "rows", None),
        check_vma=False,
    )
```

time: 640 us -> 178 us (0.28)
  blocking collectives: 409 us -> 72.2 us
  waiting for transfers between devices: 117 us -> 33.1 us
  local copies, waits for them, and re-layouts: 50.8 us -> 19.2 us
  matrix products: 40.3 us -> 10.2 us
  starting transfers between devices: 17.6 us -> 30.8 us
  other arithmetic: 3.47 us -> 11.2 us
    all_to_all x7 -> x1, blocking collectives: 409 us -> 72.2 us  [local(): lax.all_to_all(jnp.concatenate(results, axis=0), ('segment', 'rows'), spl...]
    all_to_all x1, waiting for transfers between devices: 51.1 us -> 0.01 us  [local(): lax.all_to_all(packed.reshape(peers, depth, part), 'rows', split_axis=0,...]
    ppermute x3 -> x15, waiting for transfers between devices: 66.2 us -> 33.1 us  [shifted(): lax.ppermute(value, axis, [(source, (source + steps) % count) for source...]
    dot_general x12 -> x13, matrix products: 40.3 us -> 10.2 us  [the longest x4 6.6 us: local(): delta = jnp.dot(lower, own[rank:], preferred_element_type=jnp.float32)]
    reshape x8 -> x6, local copies, waits for them, and re-layouts: 32.4 us -> 11.1 us  [the longest x4 7.94 us: local(): results.append(current.reshape(peers, depth, part))]
    convert_element_type x4 -> x0, local copies, waits for them, and re-layouts: 16.4 us -> none  [shrink_expand(): jnp.einsum('sajr,ard->sajd', lower, expand, preferred_element_type=jnp.fl...]
    all_to_all x1, starting transfers between devices: 6 us -> 13.2 us  [local(): lax.all_to_all(packed.reshape(peers, depth, part), 'rows', split_axis=0,...]
    ppermute x3 -> x15, starting transfers between devices: 11.6 us -> 17.6 us  [shifted(): lax.ppermute(value, axis, [(source, (source + steps) % count) for source...]
  transfers between devices with their start and end apart: 4 -> 16, of which waited for: 4 -> 10; matrix products, arithmetic and copies ran while one was open for 0% -> 5% of each run, Pallas kernels for 0% -> 0%
where the time goes in v1:
time: 178 us; the launch traced here: 177 us
  blocking collectives  72.2 us (41%)
  waiting for transfers between devices  33.1 us (19%)
  starting transfers between devices  30.8 us (17%)
  local copies, waits for them, and re-layouts  19.2 us (11%)
  other arithmetic  11.2 us (6%)
  matrix products  10.2 us (6%)
    all_to_all x1, blocking collectives, local(): lax.all_to_all(jnp.concatenate(results, axis=0), ('segment', 'rows'), spl...  72.2 us
    ppermute x15, waiting for transfers between devices, shifted(): lax.ppermute(value, axis, [(source, (source + steps) % count) for source...  33.1 us
    ppermute x15, starting transfers between devices, shifted(): lax.ppermute(value, axis, [(source, (source + steps) % count) for source...  17.6 us
    all_to_all x1, starting transfers between devices, local(): lax.all_to_all(packed.reshape(peers, depth, part), 'rows', split_axis=0,...  13.2 us
    reshape x4, local copies, waits for them, and re-layouts, local(): results.append(current.reshape(peers, depth, part))  7.94 us
    dot_general x4, matrix products, local(): delta = jnp.dot(lower, own[rank:], preferred_element_type=jnp.float32)  6.6 us
    concatenate x1, other arithmetic, local(): jnp.concatenate(results, axis=0)  4.45 us
    unnamed x16, local copies, waits for them, and re-layouts  3.65 us
  transfers between devices with their start and end apart: 16, of which 10 were waited for; matrix products, arithmetic and copies ran while one was open for 5% of the time, Pallas kernels for 0%

profile of v1, /device:TPU:1, one launch (start us, length us, event | category | flops | bytes accessed | tf_op | source)
XLA Modules:
  0.0 177.1 jit_solution(1154461442224921725)
XLA Ops:
  1.6 1.1 reshape.52
  2.7 13.2 %all-to-all-start = ((bf16[64,2,2048]{2,1,0:T(2,128)(2,1)}), bf16[64,2,2048]{2,1,0:T(2,128)(2,1)}, u32[]{:S(2)}, u32[]{:S(2)}) async-start(bf16[64,2,2048]{2,1,0:T(2,128)(2,1)} %reshape.52), calls=%async_computation | async-start | bytes 1048576 | tf_op jit(solution)/shard_map/all_to_all | solution.py:36
  18.1 1.3 collective-permute-start
  19.4 2.6 %collective-permute-start.1 = (bf16[128,2048]{1,0:T(8,128)(2,1)S(1)}, bf16[128,2048]{1,0:T(8,128)(2,1)}, u32[]{:S(2)}, u32[]{:S(2)}) collective-permute-start(bf16[128,2048]{1,0:T(8,128)(2,1)S(1)} %get-tuple-element.13), channel_id=1, source_target_pairs={{0,128},{64,192},{128,0},{192,64},{1,129},{65,193},{129,1},{193,65... | collective-permute-start | bytes 1572872 | tf_op jit(solution)/shard_map/ppermute | solution.py:9
  23.1 9.4 %collective-permute-done = bf16[128,2048]{1,0:T(8,128)(2,1)S(1)} collective-permute-done((bf16[128,2048]{1,0:T(8,128)(2,1)S(1)}, bf16[128,2048]{1,0:T(8,128)(2,1)S(1)}, u32[]{:S(2)}, u32[]{:S(2)}) %collective-permute-start) | collective-permute-done | bytes 524320 | tf_op jit(solution)/shard_map/ppermute | solution.py:9
  32.5 12.3 %collective-permute-done.1 = bf16[128,2048]{1,0:T(8,128)(2,1)} collective-permute-done((bf16[128,2048]{1,0:T(8,128)(2,1)S(1)}, bf16[128,2048]{1,0:T(8,128)(2,1)}, u32[]{:S(2)}, u32[]{:S(2)}) %collective-permute-start.1) | collective-permute-done | bytes 524320 | tf_op jit(solution)/shard_map/ppermute | solution.py:9
  44.9 1.8 %pad_maximum_fusion = bf16[4,128,2048]{2,1,0:T(8,128)(2,1)S(1)} fusion(bf16[1,128,2048]{2,1,0:T(8,128)(2,1)} %bitcast.8, bf16[1,128,2048]{2,1,0:T(8,128)(2,1)} %bitcast.7, bf16[1,128,2048]{2,1,0:T(8,128)(2,1)} %bitcast.54, bf16[1,128,2048]{2,1,0:T(8,128)(2,1)} %get-tuple-element.11), kind=kLoop, calls=%fused_computation.21 | loop fusion | flops 3145728 | bytes 4194304 | tf_op jit(solution)/shard_map/stack | solution.py:47
  46.6 1.7 multiply_reduce_fusion
  48.4 2.0 %reshape.53 = bf16[128,2048]{1,0:T(8,128)(2,1)} reshape(bf16[64,2,2048]{2,1,0:T(2,128)(2,1)} %all-to-all-done) | data formatting | bytes 1048576 | tf_op jit(solution)/shard_map/reshape | solution.py:38
  50.5 1.3 fusion.17
  52.8 3.0 %collective-permute-start.4 = (f32[128,128]{0,1:T(8,128)S(1)}, f32[128,128]{0,1:T(8,128)S(1)}, u32[]{:S(2)}, u32[]{:S(2)}) collective-permute-start(f32[128,128]{0,1:T(8,128)S(1)} %pad_maximum_fusion.2), channel_id=1, source_target_pairs={{0,128},{64,192},{128,0},{192,64},{1,129},{65,193},{129,1},{193,65... | collective-permute-start | bytes 196616 | tf_op jit(solution)/shard_map/ppermute | solution.py:9
  56.3 2.3 %collective-permute-done.4 = f32[128,128]{0,1:T(8,128)S(1)} collective-permute-done((f32[128,128]{0,1:T(8,128)S(1)}, f32[128,128]{0,1:T(8,128)S(1)}, u32[]{:S(2)}, u32[]{:S(2)}) %collective-permute-start.4) | collective-permute-done | bytes 65568 | tf_op jit(solution)/shard_map/ppermute | solution.py:9
  58.6 1.2 collective-permute-done.5
  59.9 1.5 fusion.5
  62.6 1.7 collective-permute-start.7
  65.2 2.3 %collective-permute-done.6 = f32[128,128]{0,1:T(8,128)S(1)} collective-permute-done((f32[128,128]{0,1:T(8,128)S(1)}, f32[128,128]{0,1:T(8,128)S(1)}, u32[]{:S(2)}, u32[]{:S(2)}) %collective-permute-start.6) | collective-permute-done | bytes 65568 | tf_op jit(solution)/shard_map/ppermute | solution.py:9
  68.5 1.5 fusion.6
  71.8 2.3 %collective-permute-start.11 = (f32[128,128]{0,1:T(8,128)S(1)}, f32[128,128]{0,1:T(8,128)S(1)}, u32[]{:S(2)}, u32[]{:S(2)}) collective-permute-start(f32[128,128]{0,1:T(8,128)S(1)} %pad_maximum_fusion.4), channel_id=1, source_target_pairs={{0,192},{64,0},{128,64},{192,128},{1,193},{65,1},{129,65},{193,129... | collective-permute-start | bytes 196616 | tf_op jit(solution)/shard_map/ppermute | solution.py:9
  74.0 1.8 collective-permute-done.10
  75.9 2.5 %collective-permute-done.9 = f32[128,128]{0,1:T(8,128)S(1)} collective-permute-done((f32[128,128]{0,1:T(8,128)S(1)}, f32[128,128]{0,1:T(8,128)S(1)}, u32[]{:S(2)}, u32[]{:S(2)}) %collective-permute-start.9) | collective-permute-done | bytes 65568 | tf_op jit(solution)/shard_map/ppermute | solution.py:9
  78.4 1.5 fusion.7
  81.1 1.2 collective-permute-start.13
  82.3 1.5 collective-permute-start.14
  83.8 2.2 %reshape.54 = bf16[64,2,2048]{2,1,0:T(2,128)(2,1)} reshape(bf16[128,2048]{1,0:T(8,128)(2,1)} %copy-done.1) | data formatting | bytes 1048576 | tf_op jit(solution)/shard_map/reshape | solution.py:68
  86.0 2.2 %reshape.55 = bf16[64,2,2048]{2,1,0:T(2,128)(2,1)} reshape(bf16[128,2048]{1,0:T(8,128)(2,1)} %copy-done.2) | data formatting | bytes 1048576 | tf_op jit(solution)/shard_map/reshape | solution.py:68
  88.1 2.2 %reshape.56 = bf16[64,2,2048]{2,1,0:T(2,128)(2,1)} reshape(bf16[128,2048]{1,0:T(8,128)(2,1)} %copy-done.3) | data formatting | bytes 1048576 | tf_op jit(solution)/shard_map/reshape | solution.py:68
  90.4 2.2 %fusion.3 = bf16[128,2048]{1,0:T(8,128)(2,1)} fusion(bf16[128,2048]{1,0:T(8,128)(2,1)} %copy-done.3, bf16[4,128,2048]{2,1,0:T(8,128)(2,1)S(1)} %pad_maximum_fusion, s32[]{:T(128)S(6)} %select_n.81, s32[]{:T(128)S(6)} %add.170, f32[128,128]{0,1:T(8,128)S(1)} %add_add_fusion), kind=kOutput, calls=%fused_computation.15 | convolution fusion | flops 34373632 | bytes 1376264 | tf_op jit(solution)/shard_map/dot_general | solution.py:66
  92.5 1.4 reshape.57
  93.9 4.4 %pad_maximum_fusion.1 = bf16[256,2,2048]{2,1,0:T(2,128)(2,1)S(1)} fusion(bf16[64,2,2048]{2,1,0:T(2,128)(2,1)S(1)} %reshape.57, bf16[64,2,2048]{2,1,0:T(2,128)(2,1)} %reshape.56, bf16[64,2,2048]{2,1,0:T(2,128)(2,1)} %reshape.55, bf16[64,2,2048]{2,1,0:T(2,128)(2,1)} %reshape.54), kind=kLoop, calls=%fused_computation.22 | loop fusion | flops 3145728 | bytes 4194304 | tf_op jit(solution)/shard_map/concatenate | solution.py:71
  98.4 72.2 %all_to_all.10 = bf16[256,2,2048]{2,1,0:T(2,128)(2,1)S(1)} all-to-all(bf16[256,2,2048]{2,1,0:T(2,128)(2,1)S(1)} %pad_maximum_fusion.1), channel_id=1, replica_groups=mesh['segment'=4,'rows'=64] {'segment','rows'}, dimensions={0} | all-to-all | bytes 4194304 | tf_op jit(solution)/shard_map/all_to_all | solution.py:70
  170.6 2.5 %fusion.70 = (bf16[64,2,2048]{2,1,0:T(2,128)(2,1)S(1)}, bf16[64,2,2048]{2,1,0:T(2,128)(2,1)S(1)}, bf16[64,2,2048]{2,1,0:T(2,128)(2,1)}, bf16[64,2,2048]{2,1,0:T(2,128)(2,1)S(1)}) fusion(bf16[256,2,2048]{2,1,0:T(2,128)(2,1)S(1)} %all_to_all.10), kind=kLoop, calls=%fused_computation.117 | loop fusion | bytes 4194304 | tf_op jit(solution)/shard_map/slice | solution.py:78
  173.1 1.2 squeeze.24
  (62 shorter events, 15.3 us)
Async XLA Ops:
  0.0 1.3 copy-start
  0.0 15.9 %copy-start.7 = (f32[1,8192]{1,0:T(1,128)S(1)}, f32[1,8192]{1,0:T(1,128)}, u32[]{:S(2)}) copy-start(f32[1,8192]{1,0:T(1,128)} %param.9) | copy-start | bytes 98308
  0.0 16.0 %copy-start.4 = (bf16[1,1,8192,64]{2,3,1,0:T(8,128)(2,1)S(1)}, bf16[1,1,8192,64]{2,3,1,0:T(8,128)(2,1)}, u32[]{:S(2)}) copy-start(bf16[1,1,8192,64]{2,3,1,0:T(8,128)(2,1)} %param.10) | copy-start | bytes 3145732
  2.7 43.9 %all-to-all-start = ((bf16[64,2,2048]{2,1,0:T(2,128)(2,1)}), bf16[64,2,2048]{2,1,0:T(2,128)(2,1)}, u32[]{:S(2)}, u32[]{:S(2)}) async-start(bf16[64,2,2048]{2,1,0:T(2,128)(2,1)} %reshape.52), calls=%async_computation | async-start | bytes 1048576 | tf_op jit(solution)/shard_map/all_to_all | solution.py:36
  15.9 1.2 copy-start.5
  18.1 14.4 %collective-permute-start = (bf16[128,2048]{1,0:T(8,128)(2,1)S(1)}, bf16[128,2048]{1,0:T(8,128)(2,1)S(1)}, u32[]{:S(2)}, u32[]{:S(2)}) collective-permute-start(bf16[128,2048]{1,0:T(8,128)(2,1)S(1)} %get-tuple-element.12), channel_id=1, source_target_pairs={{0,64},{64,128},{128,192},{192,0},{1,65},{65,129},{129,193},{193,1... | collective-permute-start | bytes 1572872 | tf_op jit(solution)/shard_map/ppermute | solution.py:9
  19.4 25.5 %collective-permute-start.1 = (bf16[128,2048]{1,0:T(8,128)(2,1)S(1)}, bf16[128,2048]{1,0:T(8,128)(2,1)}, u32[]{:S(2)}, u32[]{:S(2)}) collective-permute-start(bf16[128,2048]{1,0:T(8,128)(2,1)S(1)} %get-tuple-element.13), channel_id=1, source_target_pairs={{0,128},{64,192},{128,0},{192,64},{1,129},{65,193},{129,1},{193,65... | collective-permute-start | bytes 1572872 | tf_op jit(solution)/shard_map/ppermute | solution.py:9
  22.0 22.8 %collective-permute-start.2 = (bf16[128,2048]{1,0:T(8,128)(2,1)S(1)}, bf16[128,2048]{1,0:T(8,128)(2,1)}, u32[]{:S(2)}, u32[]{:S(2)}) collective-permute-start(bf16[128,2048]{1,0:T(8,128)(2,1)S(1)} %get-tuple-element.14), channel_id=1, source_target_pairs={{0,192},{64,0},{128,64},{192,128},{1,193},{65,1},{129,65},{193,129... | collective-permute-start | bytes 1572872 | tf_op jit(solution)/shard_map/ppermute | solution.py:9
  32.5 12.3 %copy-start.6 = (bf16[128,2048]{1,0:T(8,128)(2,1)}, bf16[128,2048]{1,0:T(8,128)(2,1)S(1)}, u32[]{:S(2)}) copy-start(bf16[128,2048]{1,0:T(8,128)(2,1)S(1)} %collective-permute-done) | copy-start | bytes 1572868
  51.9 4.4 %collective-permute-start.3 = (f32[128,128]{0,1:T(8,128)S(1)}, f32[128,128]{0,1:T(8,128)S(1)}, u32[]{:S(2)}, u32[]{:S(2)}) collective-permute-start(f32[128,128]{0,1:T(8,128)S(1)} %pad_maximum_fusion.2), channel_id=1, source_target_pairs={{0,64},{64,128},{128,192},{192,0},{1,65},{65,129},{129,193},{193,1... | collective-permute-start | bytes 196616 | tf_op jit(solution)/shard_map/ppermute | solution.py:9
  52.8 5.8 %collective-permute-start.4 = (f32[128,128]{0,1:T(8,128)S(1)}, f32[128,128]{0,1:T(8,128)S(1)}, u32[]{:S(2)}, u32[]{:S(2)}) collective-permute-start(f32[128,128]{0,1:T(8,128)S(1)} %pad_maximum_fusion.2), channel_id=1, source_target_pairs={{0,128},{64,192},{128,0},{192,64},{1,129},{65,193},{129,1},{193,65... | collective-permute-start | bytes 196616 | tf_op jit(solution)/shard_map/ppermute | solution.py:9
  55.8 4.1 %collective-permute-start.5 = (f32[128,128]{0,1:T(8,128)S(1)}, f32[128,128]{0,1:T(8,128)S(1)}, u32[]{:S(2)}, u32[]{:S(2)}) collective-permute-start(f32[128,128]{0,1:T(8,128)S(1)} %pad_maximum_fusion.2), channel_id=1, source_target_pairs={{0,192},{64,0},{128,64},{192,128},{1,193},{65,1},{129,65},{193,129... | collective-permute-start | bytes 196616 | tf_op jit(solution)/shard_map/ppermute | solution.py:9
  61.3 0.8 copy-start.1
  62.5 5.1 %collective-permute-start.6 = (f32[128,128]{0,1:T(8,128)S(1)}, f32[128,128]{0,1:T(8,128)S(1)}, u32[]{:S(2)}, u32[]{:S(2)}) collective-permute-start(f32[128,128]{0,1:T(8,128)S(1)} %pad_maximum_fusion.3), channel_id=1, source_target_pairs={{0,64},{64,128},{128,192},{192,0},{1,65},{65,129},{129,193},{193,1... | collective-permute-start | bytes 196616 | tf_op jit(solution)/shard_map/ppermute | solution.py:9
  62.6 5.0 %collective-permute-start.7 = (f32[128,128]{0,1:T(8,128)S(1)}, f32[128,128]{0,1:T(8,128)S(1)}, u32[]{:S(2)}, u32[]{:S(2)}) collective-permute-start(f32[128,128]{0,1:T(8,128)S(1)} %pad_maximum_fusion.3), channel_id=1, source_target_pairs={{0,128},{64,192},{128,0},{192,64},{1,129},{65,193},{129,1},{193,65... | collective-permute-start | bytes 196616 | tf_op jit(solution)/shard_map/ppermute | solution.py:9
  64.2 4.2 %collective-permute-start.8 = (f32[128,128]{0,1:T(8,128)S(1)}, f32[128,128]{0,1:T(8,128)S(1)}, u32[]{:S(2)}, u32[]{:S(2)}) collective-permute-start(f32[128,128]{0,1:T(8,128)S(1)} %pad_maximum_fusion.3), channel_id=1, source_target_pairs={{0,192},{64,0},{128,64},{192,128},{1,193},{65,1},{129,65},{193,129... | collective-permute-start | bytes 196616 | tf_op jit(solution)/shard_map/ppermute | solution.py:9
  69.9 0.8 copy-start.2
  71.1 4.7 %collective-permute-start.10 = (f32[128,128]{0,1:T(8,128)S(1)}, f32[128,128]{0,1:T(8,128)S(1)}, u32[]{:S(2)}, u32[]{:S(2)}) collective-permute-start(f32[128,128]{0,1:T(8,128)S(1)} %pad_maximum_fusion.4), channel_id=1, source_target_pairs={{0,128},{64,192},{128,0},{192,64},{1,129},{65,193},{129,1},{193,65... | collective-permute-start | bytes 196616 | tf_op jit(solution)/shard_map/ppermute | solution.py:9
  71.8 4.1 %collective-permute-start.11 = (f32[128,128]{0,1:T(8,128)S(1)}, f32[128,128]{0,1:T(8,128)S(1)}, u32[]{:S(2)}, u32[]{:S(2)}) collective-permute-start(f32[128,128]{0,1:T(8,128)S(1)} %pad_maximum_fusion.4), channel_id=1, source_target_pairs={{0,192},{64,0},{128,64},{192,128},{1,193},{65,1},{129,65},{193,129... | collective-permute-start | bytes 196616 | tf_op jit(solution)/shard_map/ppermute | solution.py:9
  74.0 4.3 %collective-permute-start.9 = (f32[128,128]{0,1:T(8,128)S(1)}, f32[128,128]{0,1:T(8,128)S(1)}, u32[]{:S(2)}, u32[]{:S(2)}) collective-permute-start(f32[128,128]{0,1:T(8,128)S(1)} %pad_maximum_fusion.4), channel_id=1, source_target_pairs={{0,64},{64,128},{128,192},{192,0},{1,65},{65,129},{129,193},{193,1... | collective-permute-start | bytes 196616 | tf_op jit(solution)/shard_map/ppermute | solution.py:9
  79.9 0.8 copy-start.3
  81.0 9.3 %collective-permute-start.12 = (f32[128,128]{0,1:T(8,128)S(1)}, f32[128,128]{0,1:T(8,128)S(1)}, u32[]{:S(2)}, u32[]{:S(2)}) collective-permute-start(f32[128,128]{0,1:T(8,128)S(1)} %pad_maximum_fusion.5), channel_id=1, source_target_pairs={{0,64},{64,128},{128,192},{192,0},{1,65},{65,129},{129,193},{193,1... | collective-permute-start | bytes 196616 | tf_op jit(solution)/shard_map/ppermute | solution.py:9
  81.1 9.2 %collective-permute-start.13 = (f32[128,128]{0,1:T(8,128)S(1)}, f32[128,128]{0,1:T(8,128)S(1)}, u32[]{:S(2)}, u32[]{:S(2)}) collective-permute-start(f32[128,128]{0,1:T(8,128)S(1)} %pad_maximum_fusion.5), channel_id=1, source_target_pairs={{0,128},{64,192},{128,0},{192,64},{1,129},{65,193},{129,1},{193,65... | collective-permute-start | bytes 196616 | tf_op jit(solution)/shard_map/ppermute | solution.py:9
  82.3 8.1 %collective-permute-start.14 = (f32[128,128]{0,1:T(8,128)S(1)}, f32[128,128]{0,1:T(8,128)S(1)}, u32[]{:S(2)}, u32[]{:S(2)}) collective-permute-start(f32[128,128]{0,1:T(8,128)S(1)} %pad_maximum_fusion.5), channel_id=1, source_target_pairs={{0,192},{64,0},{128,64},{192,128},{1,193},{65,1},{129,65},{193,129... | collective-permute-start | bytes 196616 | tf_op jit(solution)/shard_map/ppermute | solution.py:9

commit v2 on v1

v2 whole, which is shorter than its diff:
```python
import jax
import jax.numpy as jnp
from jax import lax
from jax.experimental import pallas as pl
from jax.experimental.pallas import tpu as pltpu
from jax.sharding import PartitionSpec as P

GROUPS = 4
VMEM = pl.BlockSpec(memory_space=pltpu.VMEM)
SMEM = pl.BlockSpec(memory_space=pltpu.SMEM)
F32 = jnp.float32
BF16 = jnp.bfloat16


def shifted(value, axis, steps):
    count = lax.axis_size(axis)
    return lax.ppermute(value, axis, [(source, (source + steps) % count) for source in range(count)])


def dot(a, b, contract_b=0, precision=None):
    return lax.dot_general(
        a, b, (((1,), (contract_b,)), ((), ())), precision=precision, preferred_element_type=F32
    )


def call(kernel, outs, *, scratch=(), flops=0, specs=None, **options):
    return pl.pallas_call(
        kernel,
        out_shape=outs,
        in_specs=specs,
        out_specs=jax.tree.map(lambda _: VMEM, outs),
        scratch_shapes=list(scratch),
        compiler_params=pltpu.CompilerParams(vmem_limit_bytes=48 * 1024 * 1024),
        cost_estimate=pl.CostEstimate(flops=flops, bytes_accessed=4 << 20, transcendentals=0),
        **options,
    )


def pack_kernel(places, hidden, out):
    cols = out.shape[1]
    rows = lax.broadcasted_iota(jnp.int32, (out.shape[0], places.shape[1]), 0)
    chosen = jnp.where(rows == places[...], 1.0, 0.0).astype(BF16)
    stacked = jnp.concatenate(
        [hidden[:, g * cols : (g + 1) * cols] for g in range(GROUPS)], axis=0
    )
    out[...] = dot(chosen, stacked).astype(BF16)


def factors_kernel(depth, order, own, first, second, third, tiles, expand, every):
    rank = expand.shape[0] // 4
    pair = 2 * rank
    for steps, ref in enumerate((own, first, second, third)):
        section = order[steps]
        every[pl.ds(pl.multiple_of(section * pair, pair), pair), :] = ref[...]
    for section in range(4):
        expand[section * rank : (section + 1) * rank] = every[
            section * pair + rank : (section + 1) * pair
        ]
    product = dot(expand[: 3 * rank], every[...], 1)

    def tile(row, section):
        return product[row * rank : (row + 1) * rank, section * pair : (section + 1) * pair]

    lanes = lax.broadcasted_iota(jnp.int32, (rank, pair), 1)

    def last(row):
        return jnp.where(lanes < rank, tile(row, 3), tile(row, row))

    for place, value in enumerate(
        (tile(0, 1), tile(0, 2), tile(1, 2), last(0), last(1), last(2))
    ):
        tiles[place * rank : (place + 1) * rank] = value


def spread(shape, group_axis):
    rows = lax.broadcasted_iota(jnp.int32, shape, group_axis)
    blocks = lax.broadcasted_iota(jnp.int32, shape, 1 - group_axis)
    plain = shape[group_axis] // GROUPS
    group, row = rows // plain, rows % plain
    return jnp.where(blocks == (row // 2) * (2 * GROUPS) + group * 2 + row % 2, 1.0, 0.0).astype(
        BF16
    )


def products_kernel(order, blocks, own, first, second, third, sums, plain):
    count, width = plain.shape
    cols = width // GROUPS
    stacked = dot(spread((blocks.shape[0], blocks.shape[0]), 0), blocks[...]).astype(BF16)
    for g in range(GROUPS):
        plain[:, g * cols : (g + 1) * cols] = stacked[g * count : (g + 1) * count]
    rows = plain[...]
    pair = own.shape[0]
    for steps, ref in enumerate((own, first, second, third)):
        section = order[steps]
        sums[:, pl.ds(pl.multiple_of(section * pair, pair), pair)] = dot(rows, ref[...], 1)
    values = rows.astype(F32)
    squares = jnp.sum(values * values, axis=1, keepdims=True)
    half = pair // 2
    sums[:, 4 * pair - half :] = jnp.broadcast_to(squares, (count, half))


def sections_kernel(
    features, s0, s1, s2, s3, t0, t1, t2, t3, plain, expand, out, stack
):
    rank = expand.shape[0] // 4
    pair = 2 * rank
    count, width = plain.shape
    cols = width // GROUPS
    sums = s0[...] + s1[...] + s2[...] + s3[...]
    tiles = t0[...] + t1[...] + t2[...] + t3[...]
    exact = lax.Precision.HIGHEST

    def tile(place):
        return tiles[place * rank : (place + 1) * rank]

    x01, x02, x12, x03, x13, x23 = (tile(place) for place in range(6))
    y = [sums[:, s * pair : (s + 1) * pair] for s in range(4)]
    square = y[3][:, rank : rank + 1]
    forward = {0: ((1, x01), (2, x02)), 1: ((2, x12),), 2: ()}
    ends = (x03, x13, x23)
    lowers = []
    for s in range(4):
        scale = lax.rsqrt(jnp.maximum(square, 0.0) / features + 1e-05)
        lower = (y[s][:, :rank] * scale).astype(BF16)
        lowers.append(lower)
        if s == 3:
            break
        value = lower.astype(F32)
        for later, x in forward[s]:
            y[later] = y[later] + dot(value, x, 0, exact)
        end = dot(value, ends[s], 0, exact)
        y[3] = y[3] + end
        square = square + jnp.sum(
            value * (2.0 * y[s][:, rank:] + end[:, rank:]), axis=1, keepdims=True
        )
    for g in range(GROUPS):
        columns = slice(g * cols, (g + 1) * cols)
        current = plain[:, columns].astype(F32)
        for s in range(4):
            current = current + dot(lowers[s], expand[s * rank : (s + 1) * rank, columns])
            stack[s, g * count : (g + 1) * count] = current.astype(BF16)
    size = GROUPS * count
    moved = spread((size, size), 1)
    for s in range(4):
        out[s * size : (s + 1) * size] = dot(moved, stack[s]).astype(BF16)


def unpack_kernel(places, back, out):
    size, cols = places.shape[0], back.shape[2]
    count = size // GROUPS
    rows = lax.broadcasted_iota(jnp.int32, (size, back.shape[1]), 1)
    chosen = jnp.where(rows == places[...], 1.0, 0.0).astype(BF16)
    for plane in range(back.shape[0]):
        found = dot(chosen, back[plane]).astype(BF16)
        for g in range(GROUPS):
            start = (plane * GROUPS + g) * cols
            out[:, start : start + cols] = found[g * count : (g + 1) * count]


def local(hidden_in, request_adapter, home_slot, gains, shrink_tiles, expand_tiles):
    peers = lax.axis_size("rows")
    sections = lax.axis_size("segment")
    plane = lax.axis_index("segment")
    count, width = hidden_in.shape
    part = width // sections
    cols = part // GROUPS
    total = home_slot.shape[0]
    rank = expand_tiles.shape[2]
    pair = 2 * rank
    depth = 2
    adapter_ids = request_adapter[:, 0]
    catalog = jnp.arange(total, dtype=jnp.int32)
    storage = jnp.sum(
        jnp.where(adapter_ids[:, None] == catalog[None, :], home_slot[None, :], 0), axis=1
    )
    order = jnp.arange(count, dtype=jnp.int32)
    same_adapter = adapter_ids[:, None] == adapter_ids[None, :]
    earlier = jnp.sum((same_adapter & (order[None, :] < order[:, None])).astype(jnp.int32), axis=1)
    base = storage * (depth * GROUPS) + earlier
    places = (jnp.arange(GROUPS, dtype=jnp.int32)[:, None] * depth + base[None, :]).reshape(-1)
    places_row = places[None, :]
    places_column = places[:, None]
    size = peers * depth * GROUPS

    scaled = (shrink_tiles[0, 0].astype(F32) * gains[0][:, None]).astype(BF16)
    factors = jnp.concatenate([scaled.T, expand_tiles[0, 0]], axis=0)

    def quarter(steps):
        start = ((plane + steps) % sections) * part
        return lax.dynamic_slice(factors, (0, start), (pair, part))

    quarters = [quarter(steps) for steps in range(sections)]
    mine = lax.dynamic_slice(hidden_in, (0, plane * part), (count, part))
    packed = call(
        pack_kernel,
        jax.ShapeDtypeStruct((size, cols), BF16),
        specs=[VMEM, VMEM],
        name="pack",
    )(places_row, mine)
    quarters, packed = lax.optimization_barrier((quarters, packed))
    held = [quarters[0]] + [
        shifted(quarters[steps], "segment", steps) for steps in range(1, sections)
    ]
    arrived = lax.all_to_all(
        packed.reshape(peers, depth * GROUPS, cols), "rows", split_axis=0, concat_axis=0, tiled=True
    ).reshape(size, cols)

    section_order = (plane - jnp.arange(sections, dtype=jnp.int32)) % sections
    tiles, expand = call(
        lambda *refs: factors_kernel(depth, *refs),
        (
            jax.ShapeDtypeStruct((6 * rank, pair), F32),
            jax.ShapeDtypeStruct((sections * rank, part), BF16),
        ),
        scratch=[pltpu.VMEM((sections * pair, part), BF16)],
        specs=[SMEM] + [VMEM] * 4,
        name="factors",
    )(section_order, *held)
    all_tiles = [tiles] + [shifted(tiles, "segment", steps) for steps in range(1, sections)]

    sums, plain = call(
        products_kernel,
        (
            jax.ShapeDtypeStruct((peers * depth, sections * pair), F32),
            jax.ShapeDtypeStruct((peers * depth, part), BF16),
        ),
        specs=[SMEM] + [VMEM] * 5,
        name="products",
    )(section_order, arrived, *held)
    all_sums = [sums] + [shifted(sums, "segment", steps) for steps in range(1, sections)]

    results = call(
        lambda *refs: sections_kernel(width, *refs),
        jax.ShapeDtypeStruct((sections * size, cols), BF16),
        scratch=[pltpu.VMEM((sections, size, cols), BF16)],
        specs=[VMEM] * 10,
        name="sections",
    )(*all_sums, *all_tiles, plain, expand)

    back = lax.all_to_all(
        results.reshape(sections * peers, depth * GROUPS, cols),
        ("segment", "rows"),
        split_axis=0,
        concat_axis=0,
        tiled=True,
    ).reshape(sections, size, cols)
    rows = call(
        unpack_kernel,
        jax.ShapeDtypeStruct((count, width), BF16),
        specs=[VMEM, VMEM],
        name="unpack",
    )(places_column, back)
    return rows[None]


def solution(mesh):
    return jax.shard_map(
        local,
        mesh=mesh,
        in_specs=(
            P("rows", None),
            P("rows", None),
            P(),
            P("segment", None),
            P("segment", "rows", None, None),
            P("segment", "rows", None, None),
        ),
        out_specs=P("segment", "rows", None),
        check_vma=False,
    )
```

time: 178 us -> 151 us (0.85)
  blocking collectives: 72.2 us -> 0 us
  waiting for transfers between devices: 33.1 us -> 92.6 us
  local copies, waits for them, and re-layouts: 19.2 us -> 1.22 us
  Pallas kernels: 0 us -> 11.1 us
  matrix products: 10.2 us -> 0 us
  starting transfers between devices: 30.8 us -> 40.5 us
  other arithmetic: 11.2 us -> 4.83 us
    all_to_all x1 -> x0, blocking collectives: 72.2 us -> none  [local(): lax.all_to_all(jnp.concatenate(results, axis=0), ('segment', 'rows'), spl...]
    all_to_all x1 -> x2, waiting for transfers between devices: 0.01 us -> 54.7 us  [the longest x1 54.7 us: local(): lax.all_to_all(results.reshape(sections * peers, depth * GROUPS, cols), (...]
    all_to_all x1 -> x2, starting transfers between devices: 13.2 us -> 27.5 us  [the longest x1 14.3 us: local(): lax.all_to_all(results.reshape(sections * peers, depth * GROUPS, cols), (...]
    pallas_call x0 -> x5, Pallas kernels: none -> 11.1 us  [the longest x1 4.56 us: local(): call(lambda *refs: sections_kernel(width, *refs), jax.ShapeDtypeStruct((s...]
    reshape x6 -> x0, local copies, waits for them, and re-layouts: 11.1 us -> none  [the longest x4 7.94 us: local(): results.append(current.reshape(peers, depth, part))]
    dot_general x13 -> x0, matrix products: 10.2 us -> none  [the longest x4 6.6 us: local(): delta = jnp.dot(lower, own[rank:], preferred_element_type=jnp.float32)]
    ppermute x15 -> x9, waiting for transfers between devices: 33.1 us -> 38 us  [shifted(): lax.ppermute(value, axis, [(source, (source + steps) % count) for source...]
    ppermute x15 -> x9, starting transfers between devices: 17.6 us -> 13 us  [shifted(): lax.ppermute(value, axis, [(source, (source + steps) % count) for source...]
  transfers between devices with their start and end apart: 16 -> 11, of which waited for: 10 -> 5; matrix products, arithmetic and copies ran while one was open for 5% -> 0% of each run, Pallas kernels for 0% -> 2%
where the time goes in v2:
time: 151 us; the launch traced here: 150 us
  waiting for transfers between devices  92.6 us (61%)
  starting transfers between devices  40.5 us (27%)
  Pallas kernels  11.1 us (7%)
  other arithmetic  4.83 us (3%)
    all_to_all x1, waiting for transfers between devices, local(): lax.all_to_all(results.reshape(sections * peers, depth * GROUPS, cols), (...  54.7 us
    ppermute x9, waiting for transfers between devices, shifted(): lax.ppermute(value, axis, [(source, (source + steps) % count) for source...  38 us
    all_to_all x1, starting transfers between devices, local(): lax.all_to_all(results.reshape(sections * peers, depth * GROUPS, cols), (...  14.3 us
    all_to_all x1, starting transfers between devices, local(): lax.all_to_all(packed.reshape(peers, depth * GROUPS, cols), 'rows', split...  13.2 us
    ppermute x9, starting transfers between devices, shifted(): lax.ppermute(value, axis, [(source, (source + steps) % count) for source...  13 us
    pallas_call x1, Pallas kernels, local(): call(lambda *refs: sections_kernel(width, *refs), jax.ShapeDtypeStruct((s...  4.56 us
  transfers between devices with their start and end apart: 11, of which 5 were waited for; matrix products, arithmetic and copies ran while one was open for 0% of the time, Pallas kernels for 2%

profile of v2, /device:TPU:1, one launch (start us, length us, event | category | flops | bytes accessed | tf_op | source)
XLA Modules:
  0.0 150.5 jit_solution(10042423771902180248)
XLA Ops:
  0.0 1.0 select_reduce_fusion
  1.0 0.1 broadcast_add_fusion
  1.0 0.1 add.100.places
  1.1 1.4 fusion.1
  2.6 1.1 pack.1
  3.7 2.4 %fusion.2 = (bf16[128,2048]{1,0:T(8,128)(2,1)}, bf16[128,2048]{1,0:T(8,128)(2,1)S(1)}, bf16[128,2048]{1,0:T(8,128)(2,1)}, bf16[128,2048]{1,0:T(8,128)(2,1)}) fusion(s32[]{:T(128)S(6)} %select_n.53, bf16[64,8192]{1,0:T(8,128)(2,1)S(1)} %fusion.1, bf16[64,8192]{1,0:T(8,128)(2,1)} %bitcast.14, s32[]{:T(128)S(6)} %select_n.47, s32[]{:T(128)S(6)} %select_n.49, ...), kind=kLoop, calls=%fused_computation.11 | loop fusion | flops 4194304 | bytes 4194320 | tf_op jit(solution)/shard_map/concatenate | solution.py:186
  6.1 13.2 %all-to-all-start = ((bf16[64,8,512]{2,1,0:T(8,128)(2,1)}), bf16[64,8,512]{2,1,0:T(8,128)(2,1)}, u32[]{:S(2)}, u32[]{:S(2)}) async-start(bf16[64,8,512]{2,1,0:T(8,128)(2,1)} %bitcast.5), calls=%async_computation | async-start | bytes 1048576 | tf_op jit(solution)/shard_map/all_to_all | solution.py:204
  19.3 1.4 collective-permute-start
  20.6 2.6 %collective-permute-start.1 = (bf16[128,2048]{1,0:T(8,128)(2,1)}, bf16[128,2048]{1,0:T(8,128)(2,1)S(1)}, u32[]{:S(2)}, u32[]{:S(2)}) collective-permute-start(bf16[128,2048]{1,0:T(8,128)(2,1)} %get-tuple-element.17), channel_id=1, source_target_pairs={{0,128},{64,192},{128,0},{192,64},{1,129},{65,193},{129,1},{193,65... | collective-permute-start | bytes 1572872 | tf_op jit(solution)/shard_map/ppermute | solution.py:17
  23.2 1.1 collective-permute-start.2
  24.3 9.6 %collective-permute-done.first.refs_2_ = bf16[128,2048]{1,0:T(8,128)(2,1)S(1)} collective-permute-done((bf16[128,2048]{1,0:T(8,128)(2,1)}, bf16[128,2048]{1,0:T(8,128)(2,1)S(1)}, u32[]{:S(2)}, u32[]{:S(2)}) %collective-permute-start) | collective-permute-done | bytes 524320 | tf_op jit(solution)/shard_map/ppermute | solution.py:17
  33.9 12.2 %collective-permute-done.1.second.refs_3_ = bf16[128,2048]{1,0:T(8,128)(2,1)S(1)} collective-permute-done((bf16[128,2048]{1,0:T(8,128)(2,1)}, bf16[128,2048]{1,0:T(8,128)(2,1)S(1)}, u32[]{:S(2)}, u32[]{:S(2)}) %collective-permute-start.1) | collective-permute-done | bytes 524320 | tf_op jit(solution)/shard_map/ppermute | solution.py:17
  46.2 1.5 %factors.1 = (f32[384,128]{1,0:T(8,128)S(1)}, bf16[256,2048]{1,0:T(8,128)(2,1)S(1)}) custom-call(s32[4]{0:T(128)S(1)} %and_select_fusion.order.refs_0_, bf16[128,2048]{1,0:T(8,128)(2,1)S(1)} %get-tuple-element.15.own.refs_1_, bf16[128,2048]{1,0:T(8,128)(2,1)S(1)} %collective-permute-done.first.refs_2_, ...), custom_call_target="tpu_custom_call" | custom-call | bytes 4194304 | tf_op jit(solution)/shard_map/factors/pallas_call | solution.py:209
  47.7 0.0 copy-start.1
  47.8 1.0 copy-done.1
  48.7 1.1 collective-permute-start.6
  49.8 0.0 all-to-all-done
  49.8 2.2 %products.1 = (f32[128,512]{1,0:T(8,128)S(1)}, bf16[128,2048]{1,0:T(8,128)(2,1)S(1)}) custom-call(s32[4]{0:T(128)S(1)} %and_select_fusion.order.refs_0_, bf16[512,512]{1,0:T(8,128)(2,1)} %bitcast.6.blocks, bf16[128,2048]{1,0:T(8,128)(2,1)S(1)} %get-tuple-element.15.own.refs_1_, bf16[128,2048]{1,0:T(8,128)(2,1)S(1)} %collective-permute-done.first.refs_2_, ...), custom_call_target="tpu_custom_call" | custom-call | bytes 4194304 | tf_op jit(solution)/shard_map/products/pallas_call | solution.py:221
  52.0 0.7 collective-permute-start.3
  52.7 2.4 %collective-permute-start.4 = (f32[128,512]{1,0:T(8,128)S(1)}, f32[128,512]{1,0:T(8,128)S(1)}, u32[]{:S(2)}, u32[]{:S(2)}) collective-permute-start(f32[128,512]{1,0:T(8,128)S(1)} %get-tuple-element.19.refs_0_), channel_id=1, source_target_pairs={{0,128},{64,192},{128,0},{192,64},{1,129},{65,193},{129,1},{193,65... | collective-permute-start | bytes 786440 | tf_op jit(solution)/shard_map/ppermute | solution.py:17
  55.1 2.0 %collective-permute-start.5 = (f32[128,512]{1,0:T(8,128)S(1)}, f32[128,512]{1,0:T(8,128)S(1)}, u32[]{:S(2)}, u32[]{:S(2)}) collective-permute-start(f32[128,512]{1,0:T(8,128)S(1)} %get-tuple-element.19.refs_0_), channel_id=1, source_target_pairs={{0,192},{64,0},{128,64},{192,128},{1,193},{65,1},{129,65},{193,129... | collective-permute-start | bytes 786440 | tf_op jit(solution)/shard_map/ppermute | solution.py:17
  57.0 0.1 collective-permute-start.7
  57.2 0.0 collective-permute-done.6.refs_5_
  57.2 1.8 %collective-permute-start.8 = (f32[384,128]{1,0:T(8,128)S(1)}, f32[384,128]{1,0:T(8,128)S(1)}, u32[]{:S(2)}, u32[]{:S(2)}) collective-permute-start(f32[384,128]{1,0:T(8,128)S(1)} %get-tuple-element.20.refs_4_), channel_id=1, source_target_pairs={{0,192},{64,0},{128,64},{192,128},{1,193},{65,1},{129,65},{193,129... | collective-permute-start | bytes 589832 | tf_op jit(solution)/shard_map/ppermute | solution.py:17
  58.9 13.7 %collective-permute-done.7.refs_6_ = f32[384,128]{1,0:T(8,128)S(1)} collective-permute-done((f32[384,128]{1,0:T(8,128)S(1)}, f32[384,128]{1,0:T(8,128)S(1)}, u32[]{:S(2)}, u32[]{:S(2)}) %collective-permute-start.7) | collective-permute-done | bytes 196640 | tf_op jit(solution)/shard_map/ppermute | solution.py:17
  72.6 2.4 %collective-permute-done.8.refs_7_ = f32[384,128]{1,0:T(8,128)S(1)} collective-permute-done((f32[384,128]{1,0:T(8,128)S(1)}, f32[384,128]{1,0:T(8,128)S(1)}, u32[]{:S(2)}, u32[]{:S(2)}) %collective-permute-start.8) | collective-permute-done | bytes 196640 | tf_op jit(solution)/shard_map/ppermute | solution.py:17
  75.0 0.0 collective-permute-done.5.refs_3_
  75.0 4.6 %sections.1 = bf16[2048,512]{1,0:T(8,128)(2,1)} custom-call(f32[128,512]{1,0:T(8,128)S(1)} %get-tuple-element.19.refs_0_, f32[128,512]{1,0:T(8,128)S(1)} %collective-permute-done.3.refs_1_, f32[128,512]{1,0:T(8,128)S(1)} %collective-permute-done.4.refs_2_, f32[128,512]{1,0:T(8,128)S(1)} %collective-permute-done.5.refs_3_, ...), custom_call_target="tpu_custom_call" | custom-call | bytes 4194304 | tf_op jit(solution)/shard_map/sections/pallas_call | solution.py:232
  79.6 14.3 %all-to-all-start.1 = ((bf16[256,8,512]{2,1,0:T(8,128)(2,1)}), bf16[256,8,512]{2,1,0:T(8,128)(2,1)S(1)}, u32[]{:S(2)}, u32[]{:S(2)}) async-start(bf16[256,8,512]{2,1,0:T(8,128)(2,1)} %bitcast.7), calls=%async_computation.1 | async-start | bytes 4194304 | tf_op jit(solution)/shard_map/all_to_all | solution.py:240
  93.9 0.1 add.102.places
  94.1 54.7 %all-to-all-done.1 = bf16[256,8,512]{2,1,0:T(8,128)(2,1)S(1)} async-done(((bf16[256,8,512]{2,1,0:T(8,128)(2,1)}), bf16[256,8,512]{2,1,0:T(8,128)(2,1)S(1)}, u32[]{:S(2)}, u32[]{:S(2)}) %all-to-all-start.1) | async-done | bytes 2097184 | tf_op jit(solution)/shard_map/all_to_all | solution.py:240
  148.8 1.7 %unpack.1 = bf16[64,8192]{1,0:T(8,128)(2,1)} custom-call(s32[256,1]{1,0:T(8,128)S(1)} %add.102.places, bf16[4,512,512]{2,1,0:T(8,128)(2,1)S(1)} %bitcast.13), custom_call_target="tpu_custom_call" | custom-call | bytes 4194304 | tf_op jit(solution)/shard_map/unpack/pallas_call | solution.py:247
  (11 shorter events, 0.1 us)
Async XLA Ops:
  0.0 2.6 %copy-start = (bf16[64,8192]{1,0:T(8,128)(2,1)S(1)}, bf16[64,8192]{1,0:T(8,128)(2,1)}, u32[]{:S(2)}) copy-start(bf16[64,8192]{1,0:T(8,128)(2,1)} %param.6) | copy-start | bytes 3145732
  6.1 43.8 %all-to-all-start = ((bf16[64,8,512]{2,1,0:T(8,128)(2,1)}), bf16[64,8,512]{2,1,0:T(8,128)(2,1)}, u32[]{:S(2)}, u32[]{:S(2)}) async-start(bf16[64,8,512]{2,1,0:T(8,128)(2,1)} %bitcast.5), calls=%async_computation | async-start | bytes 1048576 | tf_op jit(solution)/shard_map/all_to_all | solution.py:204
  19.3 14.7 %collective-permute-start = (bf16[128,2048]{1,0:T(8,128)(2,1)}, bf16[128,2048]{1,0:T(8,128)(2,1)S(1)}, u32[]{:S(2)}, u32[]{:S(2)}) collective-permute-start(bf16[128,2048]{1,0:T(8,128)(2,1)} %get-tuple-element.16), channel_id=1, source_target_pairs={{0,64},{64,128},{128,192},{192,0},{1,65},{65,129},{129,193},{193,1... | collective-permute-start | bytes 1572872 | tf_op jit(solution)/shard_map/ppermute | solution.py:17
  20.6 25.5 %collective-permute-start.1 = (bf16[128,2048]{1,0:T(8,128)(2,1)}, bf16[128,2048]{1,0:T(8,128)(2,1)S(1)}, u32[]{:S(2)}, u32[]{:S(2)}) collective-permute-start(bf16[128,2048]{1,0:T(8,128)(2,1)} %get-tuple-element.17), channel_id=1, source_target_pairs={{0,128},{64,192},{128,0},{192,64},{1,129},{65,193},{129,1},{193,65... | collective-permute-start | bytes 1572872 | tf_op jit(solution)/shard_map/ppermute | solution.py:17
  23.2 22.9 %collective-permute-start.2 = (bf16[128,2048]{1,0:T(8,128)(2,1)}, bf16[128,2048]{1,0:T(8,128)(2,1)S(1)}, u32[]{:S(2)}, u32[]{:S(2)}) collective-permute-start(bf16[128,2048]{1,0:T(8,128)(2,1)} %get-tuple-element.18), channel_id=1, source_target_pairs={{0,192},{64,0},{128,64},{192,128},{1,193},{65,1},{129,65},{193,129... | collective-permute-start | bytes 1572872 | tf_op jit(solution)/shard_map/ppermute | solution.py:17
  47.7 1.0 copy-start.1
  48.7 8.4 %collective-permute-start.6 = (f32[384,128]{1,0:T(8,128)S(1)}, f32[384,128]{1,0:T(8,128)S(1)}, u32[]{:S(2)}, u32[]{:S(2)}) collective-permute-start(f32[384,128]{1,0:T(8,128)S(1)} %get-tuple-element.20.refs_4_), channel_id=1, source_target_pairs={{0,64},{64,128},{128,192},{192,0},{1,65},{65,129},{129,193},{193,1... | collective-permute-start | bytes 589832 | tf_op jit(solution)/shard_map/ppermute | solution.py:17
  49.8 25.2 %copy-start.2 = (bf16[256,2048]{1,0:T(8,128)(2,1)S(1)}, bf16[256,2048]{1,0:T(8,128)(2,1)}, u32[]{:S(2)}) copy-start(bf16[256,2048]{1,0:T(8,128)(2,1)} %copy-done.1) | copy-start | bytes 3145732
  52.0 23.0 %collective-permute-start.3 = (f32[128,512]{1,0:T(8,128)S(1)}, f32[128,512]{1,0:T(8,128)S(1)}, u32[]{:S(2)}, u32[]{:S(2)}) collective-permute-start(f32[128,512]{1,0:T(8,128)S(1)} %get-tuple-element.19.refs_0_), channel_id=1, source_target_pairs={{0,64},{64,128},{128,192},{192,0},{1,65},{65,129},{129,193},{193,1... | collective-permute-start | bytes 786440 | tf_op jit(solution)/shard_map/ppermute | solution.py:17
  52.7 22.3 %collective-permute-start.4 = (f32[128,512]{1,0:T(8,128)S(1)}, f32[128,512]{1,0:T(8,128)S(1)}, u32[]{:S(2)}, u32[]{:S(2)}) collective-permute-start(f32[128,512]{1,0:T(8,128)S(1)} %get-tuple-element.19.refs_0_), channel_id=1, source_target_pairs={{0,128},{64,192},{128,0},{192,64},{1,129},{65,193},{129,1},{193,65... | collective-permute-start | bytes 786440 | tf_op jit(solution)/shard_map/ppermute | solution.py:17
  55.1 20.0 %collective-permute-start.5 = (f32[128,512]{1,0:T(8,128)S(1)}, f32[128,512]{1,0:T(8,128)S(1)}, u32[]{:S(2)}, u32[]{:S(2)}) collective-permute-start(f32[128,512]{1,0:T(8,128)S(1)} %get-tuple-element.19.refs_0_), channel_id=1, source_target_pairs={{0,192},{64,0},{128,64},{192,128},{1,193},{65,1},{129,65},{193,129... | collective-permute-start | bytes 786440 | tf_op jit(solution)/shard_map/ppermute | solution.py:17
  57.0 15.6 %collective-permute-start.7 = (f32[384,128]{1,0:T(8,128)S(1)}, f32[384,128]{1,0:T(8,128)S(1)}, u32[]{:S(2)}, u32[]{:S(2)}) collective-permute-start(f32[384,128]{1,0:T(8,128)S(1)} %get-tuple-element.20.refs_4_), channel_id=1, source_target_pairs={{0,128},{64,192},{128,0},{192,64},{1,129},{65,193},{129,1},{193,65... | collective-permute-start | bytes 589832 | tf_op jit(solution)/shard_map/ppermute | solution.py:17
  57.2 17.9 %collective-permute-start.8 = (f32[384,128]{1,0:T(8,128)S(1)}, f32[384,128]{1,0:T(8,128)S(1)}, u32[]{:S(2)}, u32[]{:S(2)}) collective-permute-start(f32[384,128]{1,0:T(8,128)S(1)} %get-tuple-element.20.refs_4_), channel_id=1, source_target_pairs={{0,192},{64,0},{128,64},{192,128},{1,193},{65,1},{129,65},{193,129... | collective-permute-start | bytes 589832 | tf_op jit(solution)/shard_map/ppermute | solution.py:17
  79.6 69.1 %all-to-all-start.1 = ((bf16[256,8,512]{2,1,0:T(8,128)(2,1)}), bf16[256,8,512]{2,1,0:T(8,128)(2,1)S(1)}, u32[]{:S(2)}, u32[]{:S(2)}) async-start(bf16[256,8,512]{2,1,0:T(8,128)(2,1)} %bitcast.7), calls=%async_computation.1 | async-start | bytes 4194304 | tf_op jit(solution)/shard_map/all_to_all | solution.py:240

commit v3 on v2

v3 whole, which is shorter than its diff:
```python
import jax
import jax.numpy as jnp
from jax import lax
from jax.experimental import pallas as pl
from jax.experimental.pallas import tpu as pltpu
from jax.sharding import Mesh
from jax.sharding import PartitionSpec as P

GROUPS = 4
VMEM = pl.BlockSpec(memory_space=pltpu.VMEM)
SMEM = pl.BlockSpec(memory_space=pltpu.SMEM)
F32 = jnp.float32
BF16 = jnp.bfloat16


def shifted(value, axis, steps):
    count = lax.axis_size(axis)
    return lax.ppermute(value, axis, [(source, (source + steps) % count) for source in range(count)])


def dot(a, b, contract_b=0, precision=None):
    return lax.dot_general(
        a, b, (((1,), (contract_b,)), ((), ())), precision=precision, preferred_element_type=F32
    )


def call(kernel, outs, *, scratch=(), flops=0, specs=None, **options):
    return pl.pallas_call(
        kernel,
        out_shape=outs,
        in_specs=specs,
        out_specs=jax.tree.map(lambda _: VMEM, outs),
        scratch_shapes=list(scratch),
        compiler_params=pltpu.CompilerParams(vmem_limit_bytes=48 * 1024 * 1024),
        cost_estimate=pl.CostEstimate(flops=flops, bytes_accessed=4 << 20, transcendentals=0),
        **options,
    )


def one_hot(places, shape, axis):
    lines = lax.broadcasted_iota(jnp.int32, shape, axis)
    return jnp.where(lines == places, 1.0, 0.0).astype(BF16)


def block_places(shape, axis, count, core=None, only=None):
    line = lax.broadcasted_iota(jnp.int32, shape, axis)
    group = line // count
    row = line % count
    within = group * 2 + row % 2
    peer = row // 2
    if core is None:
        return peer * (2 * GROUPS) + within
    if only:
        return jnp.where(peer % 2 == core, peer * (2 * GROUPS) + within, -1)
    return jnp.where(peer % 2 == core, -1, (peer // 2) * (2 * GROUPS) + within)


def pack_kernel(places, hidden, out):
    cols = out.shape[1]
    chosen = one_hot(places[...], (out.shape[0], places.shape[1]), 0)
    stacked = jnp.concatenate(
        [hidden[:, g * cols : (g + 1) * cols] for g in range(GROUPS)], axis=0
    )
    out[...] = dot(chosen, stacked).astype(BF16)


def quarters_kernel(plane, shrink, gain, expand, *outs):
    rank = shrink.shape[0]
    part = outs[0].shape[1]
    for steps, out in enumerate(outs):
        start = lax.rem(plane[0] + steps, len(outs)) * part
        columns = pl.ds(pl.multiple_of(start, part), part)
        out[:rank] = (shrink[:, columns].astype(F32) * gain[:, columns]).astype(BF16)
        out[rank:] = expand[:, columns]


def factors_kernel(order, own, first, second, third, tiles, every):
    pair = own.shape[0]
    rank = pair // 2
    for steps, ref in enumerate((own, first, second, third)):
        section = order[steps]
        every[pl.ds(pl.multiple_of(section * pair, pair), pair), :] = ref[...]

    lanes = lax.broadcasted_iota(jnp.int32, (rank, pair), 1)
    needed = every[...]
    place = {(0, 1): 0, (0, 2): 1, (1, 2): 2}
    for row in range(3):
        product = dot(every[row * pair + rank : (row + 1) * pair], needed, 1)

        def tile(section):
            return product[:, section * pair : (section + 1) * pair]

        for section in range(row + 1, 3):
            at = place[row, section] * rank
            tiles[at : at + rank] = tile(section)
        at = (3 + row) * rank
        tiles[at : at + rank] = jnp.where(lanes < rank, tile(3), tile(row))


def products_kernel(order, blocks, others, own, first, second, third, sums, plain):
    count, width = plain.shape
    cols = width // GROUPS
    size = count * GROUPS
    core = order[4]
    stacked = dot(
        one_hot(block_places((size, 1), 0, count, core, True), (size, blocks.shape[0]), 1),
        blocks[...],
    ) + dot(
        one_hot(block_places((size, 1), 0, count, core, False), (size, others.shape[0]), 1),
        others[...],
    )
    stacked = stacked.astype(BF16)
    for g in range(GROUPS):
        plain[:, g * cols : (g + 1) * cols] = stacked[g * count : (g + 1) * count]
    rows = plain[...]
    pair = own.shape[0]
    for steps, ref in enumerate((own, first, second, third)):
        section = order[steps]
        sums[:, pl.ds(pl.multiple_of(section * pair, pair), pair)] = dot(rows, ref[...], 1)
    values = rows.astype(F32)
    squares = jnp.sum(values * values, axis=1, keepdims=True)
    half = pair // 2
    sums[:, 4 * pair - half :] = jnp.broadcast_to(squares, (count, half))


def sections_kernel(
    features, order, s0, s1, s2, s3, t0, t1, t2, t3, plain, f0, f1, f2, f3, out, stack, expand
):
    pair = f0.shape[0]
    rank = pair // 2
    count, width = plain.shape
    cols = width // GROUPS
    for steps, ref in enumerate((f0, f1, f2, f3)):
        section = order[steps]
        expand[pl.ds(pl.multiple_of(section * rank, rank), rank), :] = ref[rank:]
    sums = s0[...] + s1[...] + s2[...] + s3[...]
    tiles = t0[...] + t1[...] + t2[...] + t3[...]
    exact = lax.Precision.HIGHEST

    def tile(place):
        return tiles[place * rank : (place + 1) * rank]

    x01, x02, x12, x03, x13, x23 = (tile(place) for place in range(6))
    y = [sums[:, s * pair : (s + 1) * pair] for s in range(4)]
    square = y[3][:, rank : rank + 1]
    forward = {0: ((1, x01), (2, x02)), 1: ((2, x12),), 2: ()}
    ends = (x03, x13, x23)
    lowers = []
    for s in range(4):
        scale = lax.rsqrt(jnp.maximum(square, 0.0) / features + 1e-05)
        lower = (y[s][:, :rank] * scale).astype(BF16)
        lowers.append(lower)
        if s == 3:
            break
        value = lower.astype(F32)
        for later, x in forward[s]:
            y[later] = y[later] + dot(value, x, 0, exact)
        end = dot(value, ends[s], 0, exact)
        y[3] = y[3] + end
        square = square + jnp.sum(
            value * (2.0 * y[s][:, rank:] + end[:, rank:]), axis=1, keepdims=True
        )
    for g in range(GROUPS):
        columns = slice(g * cols, (g + 1) * cols)
        current = plain[:, columns].astype(F32)
        for s in range(4):
            current = current + dot(lowers[s], expand[s * rank : (s + 1) * rank, columns])
            stack[s, g * count : (g + 1) * count] = current.astype(BF16)
    size = GROUPS * count
    moved = one_hot(block_places((1, size), 1, count), (size, size), 0)
    for s in range(4):
        out[s * size : (s + 1) * size] = dot(moved, stack[s]).astype(BF16)


def place_rows(out, found, count, cols, plane):
    for g in range(GROUPS):
        start = (plane * GROUPS + g) * cols
        out[:, start : start + cols] = found[g * count : (g + 1) * count]


def unpack_kernel(places, back, out):
    size, cols = places.shape[0], back.shape[2]
    chosen = one_hot(places[...], (size, back.shape[1]), 1)
    for plane in range(back.shape[0]):
        found = dot(chosen, back[plane]).astype(BF16)
        place_rows(out, found, size // GROUPS, cols, plane)


def finish_kernel(places, back, begun, out):
    size, cols = places.shape[0], back.shape[2]
    count = size // GROUPS
    chosen = one_hot(places[...], (size, back.shape[1]), 1)
    for plane in range(back.shape[0]):
        found = dot(chosen, back[plane])
        for g in range(GROUPS):
            start = (plane * GROUPS + g) * cols
            kept = begun[:, start : start + cols].astype(F32)
            out[:, start : start + cols] = (kept + found[g * count : (g + 1) * count]).astype(BF16)


def local(hidden_in, request_adapter, home_slot, gains, shrink_tiles, expand_tiles):
    chips = lax.axis_size("chip")
    peers = 2 * chips
    sections = lax.axis_size("segment")
    plane = lax.axis_index("segment")
    core = lax.axis_index("core")
    count, width = hidden_in.shape
    part = width // sections
    cols = part // GROUPS
    total = home_slot.shape[0]
    rank = expand_tiles.shape[2]
    pair = 2 * rank
    depth = 2
    block = depth * GROUPS
    size = peers * block

    quarters = call(
        quarters_kernel,
        tuple(jax.ShapeDtypeStruct((pair, part), BF16) for _ in range(sections)),
        specs=[SMEM, VMEM, VMEM, VMEM],
        name="quarters",
    )(plane.reshape(1), shrink_tiles[0, 0].T, gains, expand_tiles[0, 0])

    adapter_ids = request_adapter[:, 0]
    catalog = jnp.arange(total, dtype=jnp.int32)
    storage = jnp.sum(
        jnp.where(adapter_ids[:, None] == catalog[None, :], home_slot[None, :], 0), axis=1
    )
    order = jnp.arange(count, dtype=jnp.int32)
    same_adapter = adapter_ids[:, None] == adapter_ids[None, :]
    earlier = jnp.sum((same_adapter & (order[None, :] < order[:, None])).astype(jnp.int32), axis=1)
    groups = jnp.arange(GROUPS, dtype=jnp.int32)[:, None] * depth

    def grouped(base):
        return jnp.where(base[None, :] < 0, -1, groups + base[None, :]).reshape(-1)

    near = storage % 2 == core
    homes = grouped(storage * block + earlier)[None, :]
    near_places = grouped(
        jnp.where(near, (storage // 2) * (2 * block) + core * block + earlier, -1)
    )[:, None]
    far_places = grouped(jnp.where(near, -1, (storage // 2) * block + earlier))[:, None]

    mine = lax.dynamic_slice(hidden_in, (0, plane * part), (count, part))
    packed = call(
        pack_kernel,
        jax.ShapeDtypeStruct((size, cols), BF16),
        specs=[VMEM, VMEM],
        name="pack",
    )(homes, mine)
    held = [quarters[0]] + [
        shifted(quarters[steps], "segment", steps) for steps in range(1, sections)
    ]

    def other_core(blocks):
        lead = blocks.shape[0]
        theirs = lax.dynamic_slice(blocks, (0, (1 - core) * block, 0), (lead, block, cols))
        return lax.ppermute(theirs, "core", [(0, 1), (1, 0)])

    arrived = lax.all_to_all(
        packed.reshape(chips, 2 * block, cols), "chip", split_axis=0, concat_axis=0, tiled=True
    )
    others = other_core(arrived).reshape(chips * block, cols)

    section_order = (plane - jnp.arange(sections, dtype=jnp.int32)) % sections
    section_order = jnp.concatenate([section_order, core.reshape(1)])
    tiles = call(
        factors_kernel,
        jax.ShapeDtypeStruct((6 * rank, pair), F32),
        scratch=[pltpu.VMEM((sections * pair, part), BF16)],
        specs=[SMEM] + [VMEM] * 4,
        name="factors",
    )(section_order, *held)
    all_tiles = [tiles] + [shifted(tiles, "segment", steps) for steps in range(1, sections)]

    sums, plain = call(
        products_kernel,
        (
            jax.ShapeDtypeStruct((peers * depth, sections * pair), F32),
            jax.ShapeDtypeStruct((peers * depth, part), BF16),
        ),
        specs=[SMEM] + [VMEM] * 6,
        name="products",
    )(section_order, arrived.reshape(size, cols), others, *held)
    all_sums = [sums] + [shifted(sums, "segment", steps) for steps in range(1, sections)]

    results = call(
        lambda *refs: sections_kernel(width, *refs),
        jax.ShapeDtypeStruct((sections * size, cols), BF16),
        scratch=[
            pltpu.VMEM((sections, size, cols), BF16),
            pltpu.VMEM((sections * rank, part), BF16),
        ],
        specs=[SMEM] + [VMEM] * 13,
        name="sections",
    )(section_order, *all_sums, *all_tiles, plain, *held)

    back = lax.all_to_all(
        results.reshape(sections * chips, 2 * block, cols),
        ("segment", "chip"),
        split_axis=0,
        concat_axis=0,
        tiled=True,
    )
    others = other_core(back).reshape(sections, chips * block, cols)
    begun = call(
        unpack_kernel,
        jax.ShapeDtypeStruct((count, width), BF16),
        specs=[VMEM, VMEM],
        name="unpack",
    )(near_places, back.reshape(sections, size, cols))
    rows = call(
        finish_kernel,
        jax.ShapeDtypeStruct((count, width), BF16),
        specs=[VMEM, VMEM, VMEM],
        name="finish",
    )(far_places, others, begun)
    return rows[None]


def solution(mesh):
    planes, peers = mesh.devices.shape
    split = Mesh(mesh.devices.reshape(planes, peers // 2, 2), ("segment", "chip", "core"))
    rows = ("chip", "core")
    return jax.shard_map(
        local,
        mesh=split,
        in_specs=(
            P(rows, None),
            P(rows, None),
            P(),
            P("segment", None),
            P("segment", rows, None, None),
            P("segment", rows, None, None),
        ),
        out_specs=P("segment", rows, None),
        check_vma=False,
    )
```

time: 151 us -> 154 us (1.020)
  blocking collectives: 0 us -> 66.5 us
  waiting for transfers between devices: 92.6 us -> 34.2 us
  starting transfers between devices: 40.5 us -> 32 us
  Pallas kernels: 11.1 us -> 15.6 us
  other arithmetic: 4.83 us -> 1.21 us
  local copies, waits for them, and re-layouts: 1.22 us -> 3.67 us
    all_to_all x0 -> x1, blocking collectives: none -> 66.5 us  [local(): lax.all_to_all(results.reshape(sections * chips, 2 * block, cols), ('segm...]
    all_to_all x2 -> x1, waiting for transfers between devices: 54.7 us -> 6.8 us  [local(): lax.all_to_all(packed.reshape(chips, 2 * block, cols), 'chip', split_axis...]
    all_to_all x2 -> x1, starting transfers between devices: 27.5 us -> 12 us  [local(): lax.all_to_all(packed.reshape(chips, 2 * block, cols), 'chip', split_axis...]
    ppermute x9, waiting for transfers between devices: 38 us -> 25.8 us  [shifted(): lax.ppermute(value, axis, [(source, (source + steps) % count) for source...]
    ppermute x0 -> x2, starting transfers between devices: none -> 6.55 us  [other_core(): return lax.ppermute(theirs, 'core', [(0, 1), (1, 0)])]
    pallas_call x1 -> x3, Pallas kernels: 1.55 us -> 6.3 us  [the longest x1 2.67 us: local(): call(finish_kernel, jax.ShapeDtypeStruct((count, width), BF16), specs=[VM...]
    concatenate x1, other arithmetic: 2.38 us -> 0.08 us  [local(): section_order = jnp.concatenate([section_order, core.reshape(1)])]
    dynamic_slice x0 -> x2, local copies, waits for them, and re-layouts: none -> 2.04 us  [other_core(): lax.dynamic_slice(blocks, (0, (1 - core) * block, 0), (lead, block, cols))]
  transfers between devices with their start and end apart: 11 -> 12, of which waited for: 5 -> 5; matrix products, arithmetic and copies ran while one was open for 0% -> 1% of each run, Pallas kernels for 2% -> 4%
where the time goes in v3:
time: 154 us; the launch traced here: 153 us
  blocking collectives  66.5 us (43%)
  waiting for transfers between devices  34.2 us (22%)
  starting transfers between devices  32 us (21%)
  Pallas kernels  15.6 us (10%)
  local copies, waits for them, and re-layouts  3.67 us (2%)
    all_to_all x1, blocking collectives, local(): lax.all_to_all(results.reshape(sections * chips, 2 * block, cols), ('segm...  66.5 us
    ppermute x9, waiting for transfers between devices, shifted(): lax.ppermute(value, axis, [(source, (source + steps) % count) for source...  25.8 us
    ppermute x9, starting transfers between devices, shifted(): lax.ppermute(value, axis, [(source, (source + steps) % count) for source...  13.4 us
    all_to_all x1, starting transfers between devices, local(): lax.all_to_all(packed.reshape(chips, 2 * block, cols), 'chip', split_axis...  12 us
    all_to_all x1, waiting for transfers between devices, local(): lax.all_to_all(packed.reshape(chips, 2 * block, cols), 'chip', split_axis...  6.8 us
    ppermute x2, starting transfers between devices, other_core(): return lax.ppermute(theirs, 'core', [(0, 1), (1, 0)])  6.55 us
    pallas_call x1, Pallas kernels, local(): call(lambda *refs: sections_kernel(width, *refs), jax.ShapeDtypeStruct((s...  5.12 us
  transfers between devices with their start and end apart: 12, of which 5 were waited for; matrix products, arithmetic and copies ran while one was open for 1% of the time, Pallas kernels for 4%

profile of v3, /device:TPU:1, one launch (start us, length us, event | category | flops | bytes accessed | tf_op | source)
XLA Modules:
  0.0 153.3 jit_solution(14161949497550175366)
XLA Ops:
  0.0 1.0 select_reduce_fusion
  1.2 0.1 select_n.126.places
  1.3 1.1 pack.1
  2.4 12.0 %all-to-all-start = ((bf16[32,16,512]{2,1,0:T(8,128)(2,1)}), bf16[32,16,512]{2,1,0:T(8,128)(2,1)}, u32[]{:S(2)}, u32[]{:S(2)}) async-start(bf16[32,16,512]{2,1,0:T(8,128)(2,1)} %bitcast.2), calls=%async_computation | async-start | bytes 1048576 | tf_op jit(solution)/shard_map/all_to_all | solution.py:260
  14.4 1.2 copy-done.2
  15.6 1.3 quarters.1
  16.9 1.3 collective-permute-start.1
  18.2 2.6 %collective-permute-start.2 = (bf16[128,2048]{1,0:T(8,128)(2,1)}, bf16[128,2048]{1,0:T(8,128)(2,1)S(1)}, u32[]{:S(2)}, u32[]{:S(2)}) collective-permute-start(bf16[128,2048]{1,0:T(8,128)(2,1)} %get-tuple-element.13), channel_id=1, source_target_pairs={{0,128},{64,192},{128,0},{192,64},{1,129},{65,193},{129,1},{193,65... | collective-permute-start | bytes 1572872 | tf_op jit(solution)/shard_map/ppermute | solution.py:18
  20.8 1.1 collective-permute-start.3
  21.9 6.8 %all-to-all-done = bf16[32,16,512]{2,1,0:T(8,128)(2,1)} async-done(((bf16[32,16,512]{2,1,0:T(8,128)(2,1)}), bf16[32,16,512]{2,1,0:T(8,128)(2,1)}, u32[]{:S(2)}, u32[]{:S(2)}) %all-to-all-start) | async-done | bytes 524320 | tf_op jit(solution)/shard_map/all_to_all | solution.py:260
  28.7 1.0 constant_dynamic-slice_fusion.1
  29.7 3.6 %collective-permute-start = (bf16[32,8,512]{2,1,0:T(8,128)(2,1)S(1)}, bf16[32,8,512]{2,1,0:T(8,128)(2,1)S(1)}, u32[]{:S(2)}, u32[]{:S(2)}) collective-permute-start(bf16[32,8,512]{2,1,0:T(8,128)(2,1)S(1)} %constant_dynamic-slice_fusion.1), channel_id=1, source_target_pairs={{0,1},{1,0},{2,3},{3,2},{4,5},{5,4},{6,7},{7,6},{8,9},{9,8},{10,11... | collective-permute-start | bytes 786440 | tf_op jit(solution)/shard_map/ppermute | solution.py:258
  33.3 0.1 pad_add_fusion.order.refs_0_
  33.3 9.9 %collective-permute-done.2.second.refs_12_ = bf16[128,2048]{1,0:T(8,128)(2,1)S(1)} collective-permute-done((bf16[128,2048]{1,0:T(8,128)(2,1)}, bf16[128,2048]{1,0:T(8,128)(2,1)S(1)}, u32[]{:S(2)}, u32[]{:S(2)}) %collective-permute-start.2) | collective-permute-done | bytes 524320 | tf_op jit(solution)/shard_map/ppermute | solution.py:18
  43.3 2.4 %factors.1.refs_5_ = f32[384,128]{1,0:T(8,128)S(1)} custom-call(s32[5]{0:T(128)S(1)} %pad_add_fusion.order.refs_0_, bf16[128,2048]{1,0:T(8,128)(2,1)S(1)} %get-tuple-element.11.own.refs_10_, bf16[128,2048]{1,0:T(8,128)(2,1)S(1)} %collective-permute-done.1.first.refs_11_, bf16[128,2048]{1,0:T(8,128)(2,1)S(1)} %collective-permute-done.2.second.refs_12_, ...), custom_call_target="tpu_custom_call" | custom-call | bytes 4194304 | tf_op jit(solution)/shard_map/factors/pallas_call | solution.py:267
  45.6 1.5 collective-permute-start.7
  47.1 2.4 %products.1 = (f32[128,512]{1,0:T(8,128)S(1)}, bf16[128,2048]{1,0:T(8,128)(2,1)S(1)}) custom-call(s32[5]{0:T(128)S(1)} %pad_add_fusion.order.refs_0_, bf16[512,512]{1,0:T(8,128)(2,1)} %bitcast.3.blocks, bf16[256,512]{1,0:T(8,128)(2,1)S(1)} %bitcast.17, bf16[128,2048]{1,0:T(8,128)(2,1)S(1)} %get-tuple-element.11.own.refs_10_, ...), custom_call_target="tpu_custom_call" | custom-call | bytes 4194304 | tf_op jit(solution)/shard_map/products/pallas_call | solution.py:276
  49.5 0.4 collective-permute-start.4
  49.9 2.7 %collective-permute-start.5 = (f32[128,512]{1,0:T(8,128)S(1)}, f32[128,512]{1,0:T(8,128)S(1)}, u32[]{:S(2)}, u32[]{:S(2)}) collective-permute-start(f32[128,512]{1,0:T(8,128)S(1)} %get-tuple-element.15.refs_1_), channel_id=1, source_target_pairs={{0,128},{64,192},{128,0},{192,64},{1,129},{65,193},{129,1},{193,65... | collective-permute-start | bytes 786440 | tf_op jit(solution)/shard_map/ppermute | solution.py:18
  52.6 2.0 %collective-permute-start.6 = (f32[128,512]{1,0:T(8,128)S(1)}, f32[128,512]{1,0:T(8,128)S(1)}, u32[]{:S(2)}, u32[]{:S(2)}) collective-permute-start(f32[128,512]{1,0:T(8,128)S(1)} %get-tuple-element.15.refs_1_), channel_id=1, source_target_pairs={{0,192},{64,0},{128,64},{192,128},{1,193},{65,1},{129,65},{193,129... | collective-permute-start | bytes 786440 | tf_op jit(solution)/shard_map/ppermute | solution.py:18
  54.6 1.9 %collective-permute-start.9 = (f32[384,128]{1,0:T(8,128)S(1)}, f32[384,128]{1,0:T(8,128)S(1)}, u32[]{:S(2)}, u32[]{:S(2)}) collective-permute-start(f32[384,128]{1,0:T(8,128)S(1)} %factors.1.refs_5_), channel_id=1, source_target_pairs={{0,192},{64,0},{128,64},{192,128},{1,193},{65,1},{129,65},{193,129... | collective-permute-start | bytes 589832 | tf_op jit(solution)/shard_map/ppermute | solution.py:18
  56.5 13.5 %collective-permute-done.8.refs_7_ = f32[384,128]{1,0:T(8,128)S(1)} collective-permute-done((f32[384,128]{1,0:T(8,128)S(1)}, f32[384,128]{1,0:T(8,128)S(1)}, u32[]{:S(2)}, u32[]{:S(2)}) %collective-permute-start.8) | collective-permute-done | bytes 196640 | tf_op jit(solution)/shard_map/ppermute | solution.py:18
  70.0 2.3 %collective-permute-done.9.refs_8_ = f32[384,128]{1,0:T(8,128)S(1)} collective-permute-done((f32[384,128]{1,0:T(8,128)S(1)}, f32[384,128]{1,0:T(8,128)S(1)}, u32[]{:S(2)}, u32[]{:S(2)}) %collective-permute-start.9) | collective-permute-done | bytes 196640 | tf_op jit(solution)/shard_map/ppermute | solution.py:18
  72.4 5.1 %sections.1 = bf16[2048,512]{1,0:T(8,128)(2,1)} custom-call(s32[5]{0:T(128)S(1)} %pad_add_fusion.order.refs_0_, f32[128,512]{1,0:T(8,128)S(1)} %get-tuple-element.15.refs_1_, f32[128,512]{1,0:T(8,128)S(1)} %collective-permute-done.4.refs_2_, f32[128,512]{1,0:T(8,128)S(1)} %collective-permute-done.5.refs_3_, f32[128,512]{1,0:T(8,128)S(1)} %collective-permute-done.6.refs_4_, ...), custom_call_target="tpu_custom_call" | custom-call | bytes 4194304 | tf_op jit(solution)/shard_map/sections/pallas_call | solution.py:287
  77.5 66.5 %all_to_all.10 = bf16[128,16,512]{2,1,0:T(8,128)(2,1)S(1)} all-to-all(bf16[128,16,512]{2,1,0:T(8,128)(2,1)} %bitcast.18), channel_id=1, replica_groups=mesh['segment'=4,'chip'=32,'core'=2] {'segment','chip'}, dimensions={0} | all-to-all | bytes 4194304 | tf_op jit(solution)/shard_map/all_to_all | solution.py:298
  144.0 1.1 constant_dynamic-slice_fusion
  145.1 3.0 %collective-permute-start.10 = (bf16[128,8,512]{2,1,0:T(8,128)(2,1)}, bf16[128,8,512]{2,1,0:T(8,128)(2,1)}, u32[]{:S(2)}, u32[]{:S(2)}) collective-permute-start(bf16[128,8,512]{2,1,0:T(8,128)(2,1)} %constant_dynamic-slice_fusion), channel_id=1, source_target_pairs={{0,1},{1,0},{2,3},{3,2},{4,5},{5,4},{6,7},{7,6},{8,9},{9,8},{10,11... | collective-permute-start | bytes 3145736 | tf_op jit(solution)/shard_map/ppermute | solution.py:258
  148.0 0.1 select_n.133.places
  148.2 0.1 select_n.132.places
  148.3 0.7 unpack.1.begun
  149.1 1.6 %collective-permute-done.10 = bf16[128,8,512]{2,1,0:T(8,128)(2,1)} collective-permute-done((bf16[128,8,512]{2,1,0:T(8,128)(2,1)}, bf16[128,8,512]{2,1,0:T(8,128)(2,1)}, u32[]{:S(2)}, u32[]{:S(2)}) %collective-permute-start.10) | collective-permute-done | bytes 1048608 | tf_op jit(solution)/shard_map/ppermute | solution.py:258
  150.6 2.7 %finish.1 = bf16[64,8192]{1,0:T(8,128)(2,1)} custom-call(s32[256,1]{1,0:T(8,128)S(1)} %select_n.132.places, bf16[4,256,512]{2,1,0:T(8,128)(2,1)} %bitcast.10.back, bf16[64,8192]{1,0:T(8,128)(2,1)S(1)} %unpack.1.begun), custom_call_target="tpu_custom_call" | custom-call | bytes 4194304 | tf_op jit(solution)/shard_map/finish/pallas_call | solution.py:312
  (21 shorter events, 0.2 us)
Async XLA Ops:
  0.0 1.3 copy-start
  0.0 14.4 %copy-start.1 = (bf16[1,1,8192,64]{2,3,1,0:T(8,128)(2,1)S(1)}, bf16[1,1,8192,64]{2,3,1,0:T(8,128)(2,1)}, u32[]{:S(2)}) copy-start(bf16[1,1,8192,64]{2,3,1,0:T(8,128)(2,1)} %param.10) | copy-start | bytes 3145732
  0.0 14.4 %copy-start.3 = (f32[1,8192]{1,0:T(1,128)S(1)}, f32[1,8192]{1,0:T(1,128)}, u32[]{:S(2)}) copy-start(f32[1,8192]{1,0:T(1,128)} %gain.1) | copy-start | bytes 98308
  2.4 26.3 %all-to-all-start = ((bf16[32,16,512]{2,1,0:T(8,128)(2,1)}), bf16[32,16,512]{2,1,0:T(8,128)(2,1)}, u32[]{:S(2)}, u32[]{:S(2)}) async-start(bf16[32,16,512]{2,1,0:T(8,128)(2,1)} %bitcast.2), calls=%async_computation | async-start | bytes 1048576 | tf_op jit(solution)/shard_map/all_to_all | solution.py:260
  14.4 1.2 copy-start.2
  16.9 16.4 %collective-permute-start.1 = (bf16[128,2048]{1,0:T(8,128)(2,1)}, bf16[128,2048]{1,0:T(8,128)(2,1)S(1)}, u32[]{:S(2)}, u32[]{:S(2)}) collective-permute-start(bf16[128,2048]{1,0:T(8,128)(2,1)} %get-tuple-element.12), channel_id=1, source_target_pairs={{0,64},{64,128},{128,192},{192,0},{1,65},{65,129},{129,193},{193,1... | collective-permute-start | bytes 1572872 | tf_op jit(solution)/shard_map/ppermute | solution.py:18
  18.2 25.1 %collective-permute-start.2 = (bf16[128,2048]{1,0:T(8,128)(2,1)}, bf16[128,2048]{1,0:T(8,128)(2,1)S(1)}, u32[]{:S(2)}, u32[]{:S(2)}) collective-permute-start(bf16[128,2048]{1,0:T(8,128)(2,1)} %get-tuple-element.13), channel_id=1, source_target_pairs={{0,128},{64,192},{128,0},{192,64},{1,129},{65,193},{129,1},{193,65... | collective-permute-start | bytes 1572872 | tf_op jit(solution)/shard_map/ppermute | solution.py:18
  20.8 22.5 %collective-permute-start.3 = (bf16[128,2048]{1,0:T(8,128)(2,1)}, bf16[128,2048]{1,0:T(8,128)(2,1)S(1)}, u32[]{:S(2)}, u32[]{:S(2)}) collective-permute-start(bf16[128,2048]{1,0:T(8,128)(2,1)} %get-tuple-element.14), channel_id=1, source_target_pairs={{0,192},{64,0},{128,64},{192,128},{1,193},{65,1},{129,65},{193,129... | collective-permute-start | bytes 1572872 | tf_op jit(solution)/shard_map/ppermute | solution.py:18
  29.7 17.5 %collective-permute-start = (bf16[32,8,512]{2,1,0:T(8,128)(2,1)S(1)}, bf16[32,8,512]{2,1,0:T(8,128)(2,1)S(1)}, u32[]{:S(2)}, u32[]{:S(2)}) collective-permute-start(bf16[32,8,512]{2,1,0:T(8,128)(2,1)S(1)} %constant_dynamic-slice_fusion.1), channel_id=1, source_target_pairs={{0,1},{1,0},{2,3},{3,2},{4,5},{5,4},{6,7},{7,6},{8,9},{9,8},{10,11... | collective-permute-start | bytes 786440 | tf_op jit(solution)/shard_map/ppermute | solution.py:258
  45.6 9.0 %collective-permute-start.7 = (f32[384,128]{1,0:T(8,128)S(1)}, f32[384,128]{1,0:T(8,128)S(1)}, u32[]{:S(2)}, u32[]{:S(2)}) collective-permute-start(f32[384,128]{1,0:T(8,128)S(1)} %factors.1.refs_5_), channel_id=1, source_target_pairs={{0,64},{64,128},{128,192},{192,0},{1,65},{65,129},{129,193},{193,1... | collective-permute-start | bytes 589832 | tf_op jit(solution)/shard_map/ppermute | solution.py:18
  49.5 22.9 %collective-permute-start.4 = (f32[128,512]{1,0:T(8,128)S(1)}, f32[128,512]{1,0:T(8,128)S(1)}, u32[]{:S(2)}, u32[]{:S(2)}) collective-permute-start(f32[128,512]{1,0:T(8,128)S(1)} %get-tuple-element.15.refs_1_), channel_id=1, source_target_pairs={{0,64},{64,128},{128,192},{192,0},{1,65},{65,129},{129,193},{193,1... | collective-permute-start | bytes 786440 | tf_op jit(solution)/shard_map/ppermute | solution.py:18
  49.9 22.5 %collective-permute-start.5 = (f32[128,512]{1,0:T(8,128)S(1)}, f32[128,512]{1,0:T(8,128)S(1)}, u32[]{:S(2)}, u32[]{:S(2)}) collective-permute-start(f32[128,512]{1,0:T(8,128)S(1)} %get-tuple-element.15.refs_1_), channel_id=1, source_target_pairs={{0,128},{64,192},{128,0},{192,64},{1,129},{65,193},{129,1},{193,65... | collective-permute-start | bytes 786440 | tf_op jit(solution)/shard_map/ppermute | solution.py:18
  52.6 19.8 %collective-permute-start.6 = (f32[128,512]{1,0:T(8,128)S(1)}, f32[128,512]{1,0:T(8,128)S(1)}, u32[]{:S(2)}, u32[]{:S(2)}) collective-permute-start(f32[128,512]{1,0:T(8,128)S(1)} %get-tuple-element.15.refs_1_), channel_id=1, source_target_pairs={{0,192},{64,0},{128,64},{192,128},{1,193},{65,1},{129,65},{193,129... | collective-permute-start | bytes 786440 | tf_op jit(solution)/shard_map/ppermute | solution.py:18
  54.6 15.4 %collective-permute-start.8 = (f32[384,128]{1,0:T(8,128)S(1)}, f32[384,128]{1,0:T(8,128)S(1)}, u32[]{:S(2)}, u32[]{:S(2)}) collective-permute-start(f32[384,128]{1,0:T(8,128)S(1)} %factors.1.refs_5_), channel_id=1, source_target_pairs={{0,128},{64,192},{128,0},{192,64},{1,129},{65,193},{129,1},{193,65... | collective-permute-start | bytes 589832 | tf_op jit(solution)/shard_map/ppermute | solution.py:18
  54.6 17.8 %collective-permute-start.9 = (f32[384,128]{1,0:T(8,128)S(1)}, f32[384,128]{1,0:T(8,128)S(1)}, u32[]{:S(2)}, u32[]{:S(2)}) collective-permute-start(f32[384,128]{1,0:T(8,128)S(1)} %factors.1.refs_5_), channel_id=1, source_target_pairs={{0,192},{64,0},{128,64},{192,128},{1,193},{65,1},{129,65},{193,129... | collective-permute-start | bytes 589832 | tf_op jit(solution)/shard_map/ppermute | solution.py:18
  145.1 5.6 %collective-permute-start.10 = (bf16[128,8,512]{2,1,0:T(8,128)(2,1)}, bf16[128,8,512]{2,1,0:T(8,128)(2,1)}, u32[]{:S(2)}, u32[]{:S(2)}) collective-permute-start(bf16[128,8,512]{2,1,0:T(8,128)(2,1)} %constant_dynamic-slice_fusion), channel_id=1, source_target_pairs={{0,1},{1,0},{2,3},{3,2},{4,5},{5,4},{6,7},{7,6},{8,9},{9,8},{10,11... | collective-permute-start | bytes 3145736 | tf_op jit(solution)/shard_map/ppermute | solution.py:258

commit v4 on v3

--- a/solution.py
+++ b/solution.py
@@ -7,6 +7,7 @@
 from jax.sharding import PartitionSpec as P
 
 GROUPS = 4
+FACTOR_FLOPS = 40_000_000_000
 VMEM = pl.BlockSpec(memory_space=pltpu.VMEM)
 SMEM = pl.BlockSpec(memory_space=pltpu.SMEM)
 F32 = jnp.float32
@@ -74,27 +75,27 @@
         out[rank:] = expand[:, columns]
 
 
-def factors_kernel(order, own, first, second, third, tiles, every):
+def factors_kernel(order, own, first, second, third, tiles, every, expand):
     pair = own.shape[0]
     rank = pair // 2
     for steps, ref in enumerate((own, first, second, third)):
         section = order[steps]
         every[pl.ds(pl.multiple_of(section * pair, pair), pair), :] = ref[...]
+        expand[pl.ds(pl.multiple_of(section * rank, rank), rank), :] = ref[rank:]
+    product = dot(expand[: 3 * rank], every[...], 1)
+
+    def tile(row, section):
+        return product[row * rank : (row + 1) * rank, section * pair : (section + 1) * pair]
 
     lanes = lax.broadcasted_iota(jnp.int32, (rank, pair), 1)
-    needed = every[...]
-    place = {(0, 1): 0, (0, 2): 1, (1, 2): 2}
-    for row in range(3):
-        product = dot(every[row * pair + rank : (row + 1) * pair], needed, 1)
-
-        def tile(section):
-            return product[:, section * pair : (section + 1) * pair]
-
-        for section in range(row + 1, 3):
-            at = place[row, section] * rank
-            tiles[at : at + rank] = tile(section)
-        at = (3 + row) * rank
-        tiles[at : at + rank] = jnp.where(lanes < rank, tile(3), tile(row))
+
+    def last(row):
+        return jnp.where(lanes < rank, tile(row, 3), tile(row, row))
+
+    for place, value in enumerate(
+        (tile(0, 1), tile(0, 2), tile(1, 2), last(0), last(1), last(2))
+    ):
+        tiles[place * rank : (place + 1) * rank] = value
 
 
 def products_kernel(order, blocks, others, own, first, second, third, sums, plain):
@@ -172,30 +173,15 @@
         out[s * size : (s + 1) * size] = dot(moved, stack[s]).astype(BF16)
 
 
-def place_rows(out, found, count, cols, plane):
-    for g in range(GROUPS):
-        start = (plane * GROUPS + g) * cols
-        out[:, start : start + cols] = found[g * count : (g + 1) * count]
-
-
 def unpack_kernel(places, back, out):
-    size, cols = places.shape[0], back.shape[2]
-    chosen = one_hot(places[...], (size, back.shape[1]), 1)
-    for plane in range(back.shape[0]):
-        found = dot(chosen, back[plane]).astype(BF16)
-        place_rows(out, found, size // GROUPS, cols, plane)
-
-
-def finish_kernel(places, back, begun, out):
     size, cols = places.shape[0], back.shape[2]
     count = size // GROUPS
     chosen = one_hot(places[...], (size, back.shape[1]), 1)
     for plane in range(back.shape[0]):
-        found = dot(chosen, back[plane])
+        found = dot(chosen, back[plane]).astype(BF16)
         for g in range(GROUPS):
             start = (plane * GROUPS + g) * cols
-            kept = begun[:, start : start + cols].astype(F32)
-            out[:, start : start + cols] = (kept + found[g * count : (g + 1) * count]).astype(BF16)
+            out[:, start : start + cols] = found[g * count : (g + 1) * count]
 
 
 def local(hidden_in, request_adapter, home_slot, gains, shrink_tiles, expand_tiles):
@@ -230,16 +216,7 @@
     same_adapter = adapter_ids[:, None] == adapter_ids[None, :]
     earlier = jnp.sum((same_adapter & (order[None, :] < order[:, None])).astype(jnp.int32), axis=1)
     groups = jnp.arange(GROUPS, dtype=jnp.int32)[:, None] * depth
-
-    def grouped(base):
-        return jnp.where(base[None, :] < 0, -1, groups + base[None, :]).reshape(-1)
-
-    near = storage % 2 == core
-    homes = grouped(storage * block + earlier)[None, :]
-    near_places = grouped(
-        jnp.where(near, (storage // 2) * (2 * block) + core * block + earlier, -1)
-    )[:, None]
-    far_places = grouped(jnp.where(near, -1, (storage // 2) * block + earlier))[:, None]
+    homes = (groups + (storage * block + earlier)[None, :]).reshape(-1)
 
     mine = lax.dynamic_slice(hidden_in, (0, plane * part), (count, part))
     packed = call(
@@ -247,32 +224,33 @@
         jax.ShapeDtypeStruct((size, cols), BF16),
         specs=[VMEM, VMEM],
         name="pack",
-    )(homes, mine)
+    )(homes[None, :], mine)
     held = [quarters[0]] + [
         shifted(quarters[steps], "segment", steps) for steps in range(1, sections)
     ]
 
-    def other_core(blocks):
-        lead = blocks.shape[0]
-        theirs = lax.dynamic_slice(blocks, (0, (1 - core) * block, 0), (lead, block, cols))
-        return lax.ppermute(theirs, "core", [(0, 1), (1, 0)])
-
     arrived = lax.all_to_all(
         packed.reshape(chips, 2 * block, cols), "chip", split_axis=0, concat_axis=0, tiled=True
     )
-    others = other_core(arrived).reshape(chips * block, cols)
 
     section_order = (plane - jnp.arange(sections, dtype=jnp.int32)) % sections
     section_order = jnp.concatenate([section_order, core.reshape(1)])
     tiles = call(
         factors_kernel,
         jax.ShapeDtypeStruct((6 * rank, pair), F32),
-        scratch=[pltpu.VMEM((sections * pair, part), BF16)],
+        scratch=[
+            pltpu.VMEM((sections * pair, part), BF16),
+            pltpu.VMEM((sections * rank, part), BF16),
+        ],
         specs=[SMEM] + [VMEM] * 4,
+        flops=FACTOR_FLOPS,
         name="factors",
     )(section_order, *held)
+    arrived, tiles = lax.optimization_barrier((arrived, tiles))
     all_tiles = [tiles] + [shifted(tiles, "segment", steps) for steps in range(1, sections)]
 
+    theirs = lax.dynamic_slice(arrived, (0, (1 - core) * block, 0), (chips, block, cols))
+    others = lax.ppermute(theirs, "core", [(0, 1), (1, 0)]).reshape(chips * block, cols)
     sums, plain = call(
         products_kernel,
         (
@@ -296,25 +274,18 @@
     )(section_order, *all_sums, *all_tiles, plain, *held)
 
     back = lax.all_to_all(
-        results.reshape(sections * chips, 2 * block, cols),
-        ("segment", "chip"),
+        results.reshape(sections * peers, block, cols),
+        ("segment", "chip", "core"),
         split_axis=0,
         concat_axis=0,
         tiled=True,
     )
-    others = other_core(back).reshape(sections, chips * block, cols)
-    begun = call(
+    rows = call(
         unpack_kernel,
         jax.ShapeDtypeStruct((count, width), BF16),
         specs=[VMEM, VMEM],
         name="unpack",
-    )(near_places, back.reshape(sections, size, cols))
-    rows = call(
-        finish_kernel,
-        jax.ShapeDtypeStruct((count, width), BF16),
-        specs=[VMEM, VMEM, VMEM],
-        name="finish",
-    )(far_places, others, begun)
+    )(homes[:, None], back.reshape(sections, size, cols))
     return rows[None]
 
 

time: 154 us -> 140 us (0.909)
  blocking collectives: 66.5 us -> 0 us
  waiting for transfers between devices: 34.2 us -> 82.8 us
  starting transfers between devices: 32 us -> 39 us
    all_to_all x1 -> x0, blocking collectives: 66.5 us -> none  [local(): lax.all_to_all(results.reshape(sections * chips, 2 * block, cols), ('segm...]
    all_to_all x0 -> x1, waiting for transfers between devices: none -> 54.7 us  [local(): lax.all_to_all(results.reshape(sections * peers, block, cols), ('segment'...]
    all_to_all x0 -> x1, starting transfers between devices: none -> 9.6 us  [local(): lax.all_to_all(results.reshape(sections * peers, block, cols), ('segment'...]
    all_to_all x1, waiting for transfers between devices: 6.8 us -> 1.69 us  [local(): lax.all_to_all(packed.reshape(chips, 2 * block, cols), 'chip', split_axis...]
    pallas_call x1 -> x0, Pallas kernels: 2.67 us -> none  [local(): call(finish_kernel, jax.ShapeDtypeStruct((count, width), BF16), specs=[VM...]
    unnamed x8 -> x12, local copies, waits for them, and re-layouts: 1.25 us -> 3.3 us
    dynamic_slice x2 -> x1, local copies, waits for them, and re-layouts: 2.04 us -> 0.02 us  [local(): lax.dynamic_slice(arrived, (0, (1 - core) * block, 0), (chips, block, cols))]
    ppermute x2 -> x1, starting transfers between devices: 6.55 us -> 5.5 us  [local(): lax.ppermute(theirs, 'core', [(0, 1), (1, 0)]).reshape(chips * block, cols)]
  transfers between devices with their start and end apart: 12 -> 12, of which waited for: 5 -> 6; matrix products, arithmetic and copies ran while one was open for 1% -> 0% of each run, Pallas kernels for 4% -> 4%
where the time goes in v4:
time: 140 us
  waiting for transfers between devices  82.8 us (59%)
  starting transfers between devices  39 us (28%)
  Pallas kernels  14.1 us (10%)
  local copies, waits for them, and re-layouts  3.56 us (3%)
    all_to_all x1, waiting for transfers between devices, local(): lax.all_to_all(results.reshape(sections * peers, block, cols), ('segment'...  54.7 us
    ppermute x9, waiting for transfers between devices, shifted(): lax.ppermute(value, axis, [(source, (source + steps) % count) for source...  25.7 us
    ppermute x9, starting transfers between devices, shifted(): lax.ppermute(value, axis, [(source, (source + steps) % count) for source...  12.9 us
    all_to_all x1, starting transfers between devices, local(): lax.all_to_all(packed.reshape(chips, 2 * block, cols), 'chip', split_axis...  11 us
    all_to_all x1, starting transfers between devices, local(): lax.all_to_all(results.reshape(sections * peers, block, cols), ('segment'...  9.6 us
    pallas_call x1, Pallas kernels, local(): call(lambda *refs: sections_kernel(width, *refs), jax.ShapeDtypeStruct((s...  5.62 us
    ppermute x1, starting transfers between devices, local(): lax.ppermute(theirs, 'core', [(0, 1), (1, 0)]).reshape(chips * block, cols)  5.5 us
    unnamed x12, local copies, waits for them, and re-layouts  3.3 us
  transfers between devices with their start and end apart: 12, of which 6 were waited for; matrix products, arithmetic and copies ran while one was open for 0% of the time, Pallas kernels for 4%

profile of v4, /device:TPU:1, one launch (start us, length us, event | category | flops | bytes accessed | tf_op | source)
XLA Modules:
  0.0 139.9 jit_solution(5713148103791837808)
XLA Ops:
  0.0 1.3 copy-done.1
  1.3 1.2 copy-done.2
  2.6 0.8 copy-done.3
  3.3 1.3 quarters.1
  4.6 2.1 %collective-permute-start = (bf16[128,2048]{1,0:T(8,128)(2,1)}, bf16[128,2048]{1,0:T(8,128)(2,1)S(1)}, u32[]{:S(2)}, u32[]{:S(2)}) collective-permute-start(bf16[128,2048]{1,0:T(8,128)(2,1)} %get-tuple-element.14), channel_id=1, source_target_pairs={{0,64},{64,128},{128,192},{192,0},{1,65},{65,129},{129,193},{193,1... | collective-permute-start | bytes 1572872 | tf_op jit(solution)/shard_map/ppermute | solution.py:19
  6.7 2.6 %collective-permute-start.1 = (bf16[128,2048]{1,0:T(8,128)(2,1)}, bf16[128,2048]{1,0:T(8,128)(2,1)S(1)}, u32[]{:S(2)}, u32[]{:S(2)}) collective-permute-start(bf16[128,2048]{1,0:T(8,128)(2,1)} %get-tuple-element.15), channel_id=1, source_target_pairs={{0,128},{64,192},{128,0},{192,64},{1,129},{65,193},{129,1},{193,65... | collective-permute-start | bytes 1572872 | tf_op jit(solution)/shard_map/ppermute | solution.py:19
  9.3 1.1 collective-permute-start.2
  10.4 0.2 select_reduce_fusion
  10.6 0.1 broadcast_add_fusion
  10.7 0.1 add.58.places
  10.8 1.1 pack.1
  11.9 11.0 %all-to-all-start = ((bf16[32,16,512]{2,1,0:T(8,128)(2,1)}), bf16[32,16,512]{2,1,0:T(8,128)(2,1)S(1)}, u32[]{:S(2)}, u32[]{:S(2)}) async-start(bf16[32,16,512]{2,1,0:T(8,128)(2,1)} %bitcast.2), calls=%async_computation | async-start | bytes 1048576 | tf_op jit(solution)/shard_map/all_to_all | solution.py:232
  22.9 0.1 pad_add_fusion.order.refs_0_
  23.0 9.1 %collective-permute-done.1.second.refs_12_ = bf16[128,2048]{1,0:T(8,128)(2,1)S(1)} collective-permute-done((bf16[128,2048]{1,0:T(8,128)(2,1)}, bf16[128,2048]{1,0:T(8,128)(2,1)S(1)}, u32[]{:S(2)}, u32[]{:S(2)}) %collective-permute-start.1) | collective-permute-done | bytes 524320 | tf_op jit(solution)/shard_map/ppermute | solution.py:19
  32.1 2.0 %factors.1.refs_5_ = f32[384,128]{1,0:T(8,128)S(1)} custom-call(s32[5]{0:T(128)S(1)} %pad_add_fusion.order.refs_0_, bf16[128,2048]{1,0:T(8,128)(2,1)S(1)} %get-tuple-element.13.own.refs_10_, bf16[128,2048]{1,0:T(8,128)(2,1)S(1)} %collective-permute-done.first.refs_11_, bf16[128,2048]{1,0:T(8,128)(2,1)S(1)} %collective-permute-done.1.second.refs_12_, ...), custom_call_target="tpu_custom_call" | custom-call | flops 40000000000 | bytes 4194304 | tf_op jit(solution)/shard_map/factors/pallas_call | solution.py:238
  34.2 1.7 %all-to-all-done = bf16[32,16,512]{2,1,0:T(8,128)(2,1)S(1)} async-done(((bf16[32,16,512]{2,1,0:T(8,128)(2,1)}), bf16[32,16,512]{2,1,0:T(8,128)(2,1)S(1)}, u32[]{:S(2)}, u32[]{:S(2)}) %all-to-all-start) | async-done | bytes 524320 | tf_op jit(solution)/shard_map/all_to_all | solution.py:232
  35.9 5.5 %collective-permute-start.3 = (bf16[32,8,512]{2,1,0:T(8,128)(2,1)S(1)}, bf16[32,8,512]{2,1,0:T(8,128)(2,1)S(1)}, u32[]{:S(2)}, u32[]{:S(2)}) collective-permute-start(bf16[32,8,512]{2,1,0:T(8,128)(2,1)S(1)} %constant_dynamic-slice_fusion), channel_id=1, source_target_pairs={{0,1},{1,0},{2,3},{3,2},{4,5},{5,4},{6,7},{7,6},{8,9},{9,8},{10,11... | collective-permute-start | bytes 786440 | tf_op jit(solution)/shard_map/ppermute | solution.py:253
  41.4 0.4 collective-permute-start.7
  41.8 0.8 collective-permute-done.3
  42.5 2.3 %products.1 = (f32[128,512]{1,0:T(8,128)S(1)}, bf16[128,2048]{1,0:T(8,128)(2,1)S(1)}) custom-call(s32[5]{0:T(128)S(1)} %pad_add_fusion.order.refs_0_, bf16[512,512]{1,0:T(8,128)(2,1)S(1)} %bitcast.14, bf16[256,512]{1,0:T(8,128)(2,1)S(1)} %bitcast.17, bf16[128,2048]{1,0:T(8,128)(2,1)S(1)} %get-tuple-element.13.own.refs_10_, ...), custom_call_target="tpu_custom_call" | custom-call | bytes 4194304 | tf_op jit(solution)/shard_map/products/pallas_call | solution.py:254
  44.9 0.5 collective-permute-start.4
  45.3 2.3 %collective-permute-start.5 = (f32[128,512]{1,0:T(8,128)S(1)}, f32[128,512]{1,0:T(8,128)S(1)}, u32[]{:S(2)}, u32[]{:S(2)}) collective-permute-start(f32[128,512]{1,0:T(8,128)S(1)} %get-tuple-element.18.refs_1_), channel_id=1, source_target_pairs={{0,128},{64,192},{128,0},{192,64},{1,129},{65,193},{129,1},{193,65... | collective-permute-start | bytes 786440 | tf_op jit(solution)/shard_map/ppermute | solution.py:19
  47.7 0.2 collective-permute-start.6
  47.8 2.2 %collective-permute-start.8 = (f32[384,128]{1,0:T(8,128)S(1)}, f32[384,128]{1,0:T(8,128)S(1)}, u32[]{:S(2)}, u32[]{:S(2)}) collective-permute-start(f32[384,128]{1,0:T(8,128)S(1)} %factors.1.refs_5_), channel_id=1, source_target_pairs={{0,128},{64,192},{128,0},{192,64},{1,129},{65,193},{129,1},{193,65... | collective-permute-start | bytes 589832 | tf_op jit(solution)/shard_map/ppermute | solution.py:19
  50.0 1.5 %collective-permute-start.9 = (f32[384,128]{1,0:T(8,128)S(1)}, f32[384,128]{1,0:T(8,128)S(1)}, u32[]{:S(2)}, u32[]{:S(2)}) collective-permute-start(f32[384,128]{1,0:T(8,128)S(1)} %factors.1.refs_5_), channel_id=1, source_target_pairs={{0,192},{64,0},{128,64},{192,128},{1,193},{65,1},{129,65},{193,129... | collective-permute-start | bytes 589832 | tf_op jit(solution)/shard_map/ppermute | solution.py:19
  51.5 12.1 %collective-permute-done.8.refs_7_ = f32[384,128]{1,0:T(8,128)S(1)} collective-permute-done((f32[384,128]{1,0:T(8,128)S(1)}, f32[384,128]{1,0:T(8,128)S(1)}, u32[]{:S(2)}, u32[]{:S(2)}) %collective-permute-start.8) | collective-permute-done | bytes 196640 | tf_op jit(solution)/shard_map/ppermute | solution.py:19
  63.6 4.5 %collective-permute-done.9.refs_8_ = f32[384,128]{1,0:T(8,128)S(1)} collective-permute-done((f32[384,128]{1,0:T(8,128)S(1)}, f32[384,128]{1,0:T(8,128)S(1)}, u32[]{:S(2)}, u32[]{:S(2)}) %collective-permute-start.9) | collective-permute-done | bytes 196640 | tf_op jit(solution)/shard_map/ppermute | solution.py:19
  68.1 5.6 %sections.1 = bf16[2048,512]{1,0:T(8,128)(2,1)} custom-call(s32[5]{0:T(128)S(1)} %pad_add_fusion.order.refs_0_, f32[128,512]{1,0:T(8,128)S(1)} %get-tuple-element.18.refs_1_, f32[128,512]{1,0:T(8,128)S(1)} %collective-permute-done.4.refs_2_, f32[128,512]{1,0:T(8,128)S(1)} %collective-permute-done.5.refs_3_, f32[128,512]{1,0:T(8,128)S(1)} %collective-permute-done.6.refs_4_, ...), custom_call_target="tpu_custom_call" | custom-call | bytes 4194304 | tf_op jit(solution)/shard_map/sections/pallas_call | solution.py:265
  73.8 9.6 %all-to-all-start.1 = ((bf16[256,8,512]{2,1,0:T(8,128)(2,1)}), bf16[256,8,512]{2,1,0:T(8,128)(2,1)S(1)}, u32[]{:S(2)}, u32[]{:S(2)}) async-start(bf16[256,8,512]{2,1,0:T(8,128)(2,1)} %bitcast.18), calls=%async_computation.1 | async-start | bytes 4194304 | tf_op jit(solution)/shard_map/all_to_all | solution.py:276
  83.4 0.1 add.61.places
  83.5 54.7 %all-to-all-done.1 = bf16[256,8,512]{2,1,0:T(8,128)(2,1)S(1)} async-done(((bf16[256,8,512]{2,1,0:T(8,128)(2,1)}), bf16[256,8,512]{2,1,0:T(8,128)(2,1)S(1)}, u32[]{:S(2)}, u32[]{:S(2)}) %all-to-all-start.1) | async-done | bytes 2097184 | tf_op jit(solution)/shard_map/all_to_all | solution.py:276
  138.2 1.7 %unpack.1 = bf16[64,8192]{1,0:T(8,128)(2,1)} custom-call(s32[256,1]{1,0:T(8,128)S(1)} %add.61.places, bf16[4,512,512]{2,1,0:T(8,128)(2,1)S(1)} %bitcast.13), custom_call_target="tpu_custom_call" | custom-call | bytes 4194304 | tf_op jit(solution)/shard_map/unpack/pallas_call | solution.py:283
  (20 shorter events, 0.1 us)
Async XLA Ops:
  0.0 10.7 %copy-start = (bf16[64,8192]{1,0:T(8,128)(2,1)S(1)}, bf16[64,8192]{1,0:T(8,128)(2,1)}, u32[]{:S(2)}) copy-start(bf16[64,8192]{1,0:T(8,128)(2,1)} %param.6) | copy-start | bytes 3145732
  0.0 10.4 %copy-start.4 = (s32[64,1]{0,1:T(1,128)S(1)}, s32[64,1]{0,1:T(1,128)}, u32[]{:S(2)}) copy-start(s32[64,1]{0,1:T(1,128)} %param.7) | copy-start | bytes 772
  0.0 10.4 %copy-start.5 = (s32[64]{0:T(128)S(1)}, s32[64]{0:T(128)}, u32[]{:S(2)}) copy-start(s32[64]{0:T(128)} %param.8) | copy-start | bytes 772
  0.0 1.3 copy-start.1
  1.3 1.2 copy-start.2
  2.6 0.8 copy-start.3
  4.6 18.4 %collective-permute-start = (bf16[128,2048]{1,0:T(8,128)(2,1)}, bf16[128,2048]{1,0:T(8,128)(2,1)S(1)}, u32[]{:S(2)}, u32[]{:S(2)}) collective-permute-start(bf16[128,2048]{1,0:T(8,128)(2,1)} %get-tuple-element.14), channel_id=1, source_target_pairs={{0,64},{64,128},{128,192},{192,0},{1,65},{65,129},{129,193},{193,1... | collective-permute-start | bytes 1572872 | tf_op jit(solution)/shard_map/ppermute | solution.py:19
  6.7 25.4 %collective-permute-start.1 = (bf16[128,2048]{1,0:T(8,128)(2,1)}, bf16[128,2048]{1,0:T(8,128)(2,1)S(1)}, u32[]{:S(2)}, u32[]{:S(2)}) collective-permute-start(bf16[128,2048]{1,0:T(8,128)(2,1)} %get-tuple-element.15), channel_id=1, source_target_pairs={{0,128},{64,192},{128,0},{192,64},{1,129},{65,193},{129,1},{193,65... | collective-permute-start | bytes 1572872 | tf_op jit(solution)/shard_map/ppermute | solution.py:19
  9.3 22.8 %collective-permute-start.2 = (bf16[128,2048]{1,0:T(8,128)(2,1)}, bf16[128,2048]{1,0:T(8,128)(2,1)}, u32[]{:S(2)}, u32[]{:S(2)}) collective-permute-start(bf16[128,2048]{1,0:T(8,128)(2,1)} %get-tuple-element.16), channel_id=1, source_target_pairs={{0,192},{64,0},{128,64},{192,128},{1,193},{65,1},{129,65},{193,129... | collective-permute-start | bytes 1572872 | tf_op jit(solution)/shard_map/ppermute | solution.py:19
  11.9 24.0 %all-to-all-start = ((bf16[32,16,512]{2,1,0:T(8,128)(2,1)}), bf16[32,16,512]{2,1,0:T(8,128)(2,1)S(1)}, u32[]{:S(2)}, u32[]{:S(2)}) async-start(bf16[32,16,512]{2,1,0:T(8,128)(2,1)} %bitcast.2), calls=%async_computation | async-start | bytes 1048576 | tf_op jit(solution)/shard_map/all_to_all | solution.py:232
  35.9 6.7 %collective-permute-start.3 = (bf16[32,8,512]{2,1,0:T(8,128)(2,1)S(1)}, bf16[32,8,512]{2,1,0:T(8,128)(2,1)S(1)}, u32[]{:S(2)}, u32[]{:S(2)}) collective-permute-start(bf16[32,8,512]{2,1,0:T(8,128)(2,1)S(1)} %constant_dynamic-slice_fusion), channel_id=1, source_target_pairs={{0,1},{1,0},{2,3},{3,2},{4,5},{5,4},{6,7},{7,6},{8,9},{9,8},{10,11... | collective-permute-start | bytes 786440 | tf_op jit(solution)/shard_map/ppermute | solution.py:253
  41.4 8.6 %collective-permute-start.7 = (f32[384,128]{1,0:T(8,128)S(1)}, f32[384,128]{1,0:T(8,128)S(1)}, u32[]{:S(2)}, u32[]{:S(2)}) collective-permute-start(f32[384,128]{1,0:T(8,128)S(1)} %factors.1.refs_5_), channel_id=1, source_target_pairs={{0,64},{64,128},{128,192},{192,0},{1,65},{65,129},{129,193},{193,1... | collective-permute-start | bytes 589832 | tf_op jit(solution)/shard_map/ppermute | solution.py:19
  44.9 23.2 %collective-permute-start.4 = (f32[128,512]{1,0:T(8,128)S(1)}, f32[128,512]{1,0:T(8,128)S(1)}, u32[]{:S(2)}, u32[]{:S(2)}) collective-permute-start(f32[128,512]{1,0:T(8,128)S(1)} %get-tuple-element.18.refs_1_), channel_id=1, source_target_pairs={{0,64},{64,128},{128,192},{192,0},{1,65},{65,129},{129,193},{193,1... | collective-permute-start | bytes 786440 | tf_op jit(solution)/shard_map/ppermute | solution.py:19
  45.3 22.8 %collective-permute-start.5 = (f32[128,512]{1,0:T(8,128)S(1)}, f32[128,512]{1,0:T(8,128)S(1)}, u32[]{:S(2)}, u32[]{:S(2)}) collective-permute-start(f32[128,512]{1,0:T(8,128)S(1)} %get-tuple-element.18.refs_1_), channel_id=1, source_target_pairs={{0,128},{64,192},{128,0},{192,64},{1,129},{65,193},{129,1},{193,65... | collective-permute-start | bytes 786440 | tf_op jit(solution)/shard_map/ppermute | solution.py:19
  47.7 20.5 %collective-permute-start.6 = (f32[128,512]{1,0:T(8,128)S(1)}, f32[128,512]{1,0:T(8,128)S(1)}, u32[]{:S(2)}, u32[]{:S(2)}) collective-permute-start(f32[128,512]{1,0:T(8,128)S(1)} %get-tuple-element.18.refs_1_), channel_id=1, source_target_pairs={{0,192},{64,0},{128,64},{192,128},{1,193},{65,1},{129,65},{193,129... | collective-permute-start | bytes 786440 | tf_op jit(solution)/shard_map/ppermute | solution.py:19
  47.8 15.8 %collective-permute-start.8 = (f32[384,128]{1,0:T(8,128)S(1)}, f32[384,128]{1,0:T(8,128)S(1)}, u32[]{:S(2)}, u32[]{:S(2)}) collective-permute-start(f32[384,128]{1,0:T(8,128)S(1)} %factors.1.refs_5_), channel_id=1, source_target_pairs={{0,128},{64,192},{128,0},{192,64},{1,129},{65,193},{129,1},{193,65... | collective-permute-start | bytes 589832 | tf_op jit(solution)/shard_map/ppermute | solution.py:19
  50.0 18.1 %collective-permute-start.9 = (f32[384,128]{1,0:T(8,128)S(1)}, f32[384,128]{1,0:T(8,128)S(1)}, u32[]{:S(2)}, u32[]{:S(2)}) collective-permute-start(f32[384,128]{1,0:T(8,128)S(1)} %factors.1.refs_5_), channel_id=1, source_target_pairs={{0,192},{64,0},{128,64},{192,128},{1,193},{65,1},{129,65},{193,129... | collective-permute-start | bytes 589832 | tf_op jit(solution)/shard_map/ppermute | solution.py:19
  73.8 64.4 %all-to-all-start.1 = ((bf16[256,8,512]{2,1,0:T(8,128)(2,1)}), bf16[256,8,512]{2,1,0:T(8,128)(2,1)S(1)}, u32[]{:S(2)}, u32[]{:S(2)}) async-start(bf16[256,8,512]{2,1,0:T(8,128)(2,1)} %bitcast.18), calls=%async_computation.1 | async-start | bytes 4194304 | tf_op jit(solution)/shard_map/all_to_all | solution.py:276

commit v5 on v4

--- a/solution.py
+++ b/solution.py
@@ -9,6 +9,7 @@
 GROUPS = 4
 FACTOR_FLOPS = 40_000_000_000
 VMEM = pl.BlockSpec(memory_space=pltpu.VMEM)
+ANY = pl.BlockSpec(memory_space=pl.ANY)
 SMEM = pl.BlockSpec(memory_space=pltpu.SMEM)
 F32 = jnp.float32
 BF16 = jnp.bfloat16
@@ -25,14 +26,14 @@
     )
 
 
-def call(kernel, outs, *, scratch=(), flops=0, specs=None, **options):
+def call(kernel, outs, *, scratch=(), flops=0, specs=None, out_spec=VMEM, room=48, **options):
     return pl.pallas_call(
         kernel,
         out_shape=outs,
         in_specs=specs,
-        out_specs=jax.tree.map(lambda _: VMEM, outs),
+        out_specs=jax.tree.map(lambda _: out_spec, outs),
         scratch_shapes=list(scratch),
-        compiler_params=pltpu.CompilerParams(vmem_limit_bytes=48 * 1024 * 1024),
+        compiler_params=pltpu.CompilerParams(vmem_limit_bytes=room * 1024 * 1024),
         cost_estimate=pl.CostEstimate(flops=flops, bytes_accessed=4 << 20, transcendentals=0),
         **options,
     )
@@ -56,23 +57,51 @@
     return jnp.where(peer % 2 == core, -1, (peer // 2) * (2 * GROUPS) + within)
 
 
-def pack_kernel(places, hidden, out):
+def quarter_columns(plane, steps, part, planes=4):
+    return pl.ds(pl.multiple_of(lax.rem(plane + steps, planes) * part, part), part)
+
+
+def pack_kernel(plane, places, hidden, out, mine, arrival):
     cols = out.shape[1]
+    part = mine.shape[1]
+    copy = pltpu.make_async_copy(
+        hidden.at[:, quarter_columns(plane[0], 0, part)], mine, arrival
+    )
+    copy.start()
     chosen = one_hot(places[...], (out.shape[0], places.shape[1]), 0)
-    stacked = jnp.concatenate(
-        [hidden[:, g * cols : (g + 1) * cols] for g in range(GROUPS)], axis=0
-    )
+    copy.wait()
+    stacked = jnp.concatenate([mine[:, g * cols : (g + 1) * cols] for g in range(GROUPS)], axis=0)
     out[...] = dot(chosen, stacked).astype(BF16)
 
 
-def quarters_kernel(plane, shrink, gain, expand, *outs):
+def quarters_kernel(
+    plane, shrink, gain, expand, q0, q1, q2, q3, taken, weights, made, gain_in, in_sem, put_sem, out_sem
+):
     rank = shrink.shape[0]
-    part = outs[0].shape[1]
-    for steps, out in enumerate(outs):
-        start = lax.rem(plane[0] + steps, len(outs)) * part
-        columns = pl.ds(pl.multiple_of(start, part), part)
-        out[:rank] = (shrink[:, columns].astype(F32) * gain[:, columns]).astype(BF16)
-        out[rank:] = expand[:, columns]
+    outs = (q0, q1, q2, q3)
+    part = q0.shape[1]
+    columns = [quarter_columns(plane[0], steps, part) for steps in range(4)]
+    order = (2, 1, 3, 0)
+    load = pltpu.make_async_copy(gain, weights, gain_in)
+    load.start()
+    ins, puts, sends = {}, {}, {}
+    for k in order:
+        ins[k] = pltpu.make_async_copy(shrink.at[:, columns[k]], taken.at[k], in_sem.at[k])
+        ins[k].start()
+    for k in order:
+        puts[k] = pltpu.make_async_copy(
+            expand.at[:, columns[k]], outs[k].at[pl.ds(rank, rank)], put_sem.at[k]
+        )
+        puts[k].start()
+    load.wait()
+    for k in order:
+        ins[k].wait()
+        made[k] = (taken[k].astype(F32) * weights[:, columns[k]]).astype(BF16)
+        sends[k] = pltpu.make_async_copy(made.at[k], outs[k].at[pl.ds(0, rank)], out_sem.at[k])
+        sends[k].start()
+    for k in order:
+        puts[k].wait()
+        sends[k].wait()
 
 
 def factors_kernel(order, own, first, second, third, tiles, every, expand):
@@ -98,7 +127,14 @@
         tiles[place * rank : (place + 1) * rank] = value
 
 
-def products_kernel(order, blocks, others, own, first, second, third, sums, plain):
+def rounded(value):
+    high = value.astype(BF16)
+    return high, value - high.astype(F32)
+
+
+def products_kernel(
+    order, blocks, others, tiles, own, first, second, third, sums, plain, product
+):
     count, width = plain.shape
     cols = width // GROUPS
     size = count * GROUPS
@@ -115,17 +151,37 @@
         plain[:, g * cols : (g + 1) * cols] = stacked[g * count : (g + 1) * count]
     rows = plain[...]
     pair = own.shape[0]
+    half = pair // 2
     for steps, ref in enumerate((own, first, second, third)):
         section = order[steps]
-        sums[:, pl.ds(pl.multiple_of(section * pair, pair), pair)] = dot(rows, ref[...], 1)
+        product[:, pl.ds(pl.multiple_of(section * pair, pair), pair)] = dot(rows, ref[...], 1)
     values = rows.astype(F32)
     squares = jnp.sum(values * values, axis=1, keepdims=True)
-    half = pair // 2
-    sums[:, 4 * pair - half :] = jnp.broadcast_to(squares, (count, half))
+    lanes = lax.broadcasted_iota(jnp.int32, (count, pair), 1)
+    low = []
+    for s in range(3):
+        high, rest = rounded(product[:, s * pair : (s + 1) * pair])
+        sums[:, s * pair : (s + 1) * pair] = high
+        low.append(rest)
+    high, rest = rounded(squares)
+    ends = jnp.where(lanes < half, product[:, 3 * pair :], high.astype(F32))
+    sums[:, 3 * pair : 4 * pair] = jnp.where(lanes < half + half // 2, ends, rest).astype(BF16)
+    tile_low = []
+    for at in range(3):
+        high, rest = rounded(tiles[at * pair : (at + 1) * pair])
+        sums[:, (6 + at) * pair : (7 + at) * pair] = high
+        tile_low.append(rest)
+
+    def both(left, right):
+        return jnp.where(lanes < half, pltpu.roll(left, half, 1), right).astype(BF16)
+
+    sums[:, 4 * pair : 5 * pair] = both(low[1], low[0])
+    sums[:, 5 * pair : 6 * pair] = both(tile_low[2], low[2])
+    sums[:, 9 * pair :] = both(tile_low[1], tile_low[0])
 
 
 def sections_kernel(
-    features, order, s0, s1, s2, s3, t0, t1, t2, t3, plain, f0, f1, f2, f3, out, stack, expand
+    features, order, s0, s1, s2, s3, plain, f0, f1, f2, f3, out, stack, expand
 ):
     pair = f0.shape[0]
     rank = pair // 2
@@ -134,18 +190,32 @@
     for steps, ref in enumerate((f0, f1, f2, f3)):
         section = order[steps]
         expand[pl.ds(pl.multiple_of(section * rank, rank), rank), :] = ref[rank:]
-    sums = s0[...] + s1[...] + s2[...] + s3[...]
-    tiles = t0[...] + t1[...] + t2[...] + t3[...]
-    exact = lax.Precision.HIGHEST
-
-    def tile(place):
-        return tiles[place * rank : (place + 1) * rank]
-
-    x01, x02, x12, x03, x13, x23 = (tile(place) for place in range(6))
-    y = [sums[:, s * pair : (s + 1) * pair] for s in range(4)]
-    square = y[3][:, rank : rank + 1]
-    forward = {0: ((1, x01), (2, x02)), 1: ((2, x12),), 2: ()}
-    ends = (x03, x13, x23)
+    lanes = lax.broadcasted_iota(jnp.int32, (count, pair), 1)
+
+    def summed(at):
+        columns = slice(at * pair, (at + 1) * pair)
+        parts = [ref[:, columns].astype(F32) for ref in (s0, s1, s2, s3)]
+        return (parts[0] + parts[1]) + (parts[2] + parts[3])
+
+    def right(value):
+        return jnp.where(lanes < rank, 0.0, value)
+
+    def left(value):
+        return right(pltpu.roll(value, rank, 1))
+
+    low, mixed, tile_low = summed(4), summed(5), summed(9)
+    y = [summed(0) + right(low), summed(1) + left(low), summed(2) + right(mixed), summed(3)]
+    square = y[3][:, rank : rank + 1] + y[3][:, pair - 1 :]
+    stacks = [summed(6) + right(tile_low), summed(7) + left(tile_low), summed(8) + left(mixed)]
+
+    def thirds(place):
+        at = (place % 2) * rank
+        value = stacks[place // 2][at : at + rank]
+        high, rest = rounded(value)
+        middle, rest = rounded(rest)
+        return jnp.concatenate([high, middle, rest.astype(BF16)], axis=0)
+
+    uses = (((1, 0), (2, 1), (3, 3)), ((2, 2), (3, 4)), ((3, 5),))
     lowers = []
     for s in range(4):
         scale = lax.rsqrt(jnp.maximum(square, 0.0) / features + 1e-05)
@@ -153,14 +223,15 @@
         lowers.append(lower)
         if s == 3:
             break
+        added = dot(
+            jnp.concatenate([lower] * 3, axis=1),
+            jnp.concatenate([thirds(place) for _, place in uses[s]], axis=1),
+        )
         value = lower.astype(F32)
-        for later, x in forward[s]:
-            y[later] = y[later] + dot(value, x, 0, exact)
-        end = dot(value, ends[s], 0, exact)
-        y[3] = y[3] + end
-        square = square + jnp.sum(
-            value * (2.0 * y[s][:, rank:] + end[:, rank:]), axis=1, keepdims=True
-        )
+        for at, (later, _) in enumerate(uses[s]):
+            y[later] = y[later] + added[:, at * pair : (at + 1) * pair]
+        ends = added[:, added.shape[1] - rank :]
+        square = square + jnp.sum(value * (2.0 * y[s][:, rank:] + ends), axis=1, keepdims=True)
     for g in range(GROUPS):
         columns = slice(g * cols, (g + 1) * cols)
         current = plain[:, columns].astype(F32)
@@ -203,7 +274,18 @@
     quarters = call(
         quarters_kernel,
         tuple(jax.ShapeDtypeStruct((pair, part), BF16) for _ in range(sections)),
-        specs=[SMEM, VMEM, VMEM, VMEM],
+        scratch=[
+            pltpu.VMEM((sections, rank, part), BF16),
+            pltpu.VMEM((1, width), F32),
+            pltpu.VMEM((sections, rank, part), BF16),
+            pltpu.SemaphoreType.DMA,
+            pltpu.SemaphoreType.DMA((sections,)),
+            pltpu.SemaphoreType.DMA((sections,)),
+            pltpu.SemaphoreType.DMA((sections,)),
+        ],
+        specs=[SMEM, ANY, ANY, ANY],
+        out_spec=ANY,
+        room=60,
         name="quarters",
     )(plane.reshape(1), shrink_tiles[0, 0].T, gains, expand_tiles[0, 0])
 
@@ -218,13 +300,14 @@
     groups = jnp.arange(GROUPS, dtype=jnp.int32)[:, None] * depth
     homes = (groups + (storage * block + earlier)[None, :]).reshape(-1)
 
-    mine = lax.dynamic_slice(hidden_in, (0, plane * part), (count, part))
     packed = call(
         pack_kernel,
         jax.ShapeDtypeStruct((size, cols), BF16),
-        specs=[VMEM, VMEM],
+        scratch=[pltpu.VMEM((count, part), BF16), pltpu.SemaphoreType.DMA],
+        specs=[SMEM, VMEM, ANY],
+        room=60,
         name="pack",
-    )(homes[None, :], mine)
+    )(plane.reshape(1), homes[None, :], hidden_in)
     held = [quarters[0]] + [
         shifted(quarters[steps], "segment", steps) for steps in range(1, sections)
     ]
@@ -247,19 +330,19 @@
         name="factors",
     )(section_order, *held)
     arrived, tiles = lax.optimization_barrier((arrived, tiles))
-    all_tiles = [tiles] + [shifted(tiles, "segment", steps) for steps in range(1, sections)]
 
     theirs = lax.dynamic_slice(arrived, (0, (1 - core) * block, 0), (chips, block, cols))
     others = lax.ppermute(theirs, "core", [(0, 1), (1, 0)]).reshape(chips * block, cols)
     sums, plain = call(
         products_kernel,
         (
-            jax.ShapeDtypeStruct((peers * depth, sections * pair), F32),
+            jax.ShapeDtypeStruct((peers * depth, 10 * pair), BF16),
             jax.ShapeDtypeStruct((peers * depth, part), BF16),
         ),
-        specs=[SMEM] + [VMEM] * 6,
+        scratch=[pltpu.VMEM((peers * depth, sections * pair), F32)],
+        specs=[SMEM] + [VMEM] * 7,
         name="products",
-    )(section_order, arrived.reshape(size, cols), others, *held)
+    )(section_order, arrived.reshape(size, cols), others, tiles, *held)
     all_sums = [sums] + [shifted(sums, "segment", steps) for steps in range(1, sections)]
 
     results = call(
@@ -269,9 +352,9 @@
             pltpu.VMEM((sections, size, cols), BF16),
             pltpu.VMEM((sections * rank, part), BF16),
         ],
-        specs=[SMEM] + [VMEM] * 13,
+        specs=[SMEM] + [VMEM] * 9,
         name="sections",
-    )(section_order, *all_sums, *all_tiles, plain, *held)
+    )(section_order, *all_sums, plain, *held)
 
     back = lax.all_to_all(
         results.reshape(sections * peers, block, cols),

time: 140 us -> 163 us (1.16)
  Pallas kernels: 14.1 us -> 45.8 us
  starting transfers between devices: 39 us -> 34.2 us
  local copies, waits for them, and re-layouts: 3.56 us -> 0.83 us
    pallas_call x1, Pallas kernels: 1.26 us -> 33 us  [local(): call(quarters_kernel, tuple((jax.ShapeDtypeStruct((pair, part), BF16) for...]
    ppermute x9 -> x6, waiting for transfers between devices: 25.7 us -> 21.5 us  [shifted(): lax.ppermute(value, axis, [(source, (source + steps) % count) for source...]
    ppermute x9 -> x6, starting transfers between devices: 12.9 us -> 8.85 us  [shifted(): lax.ppermute(value, axis, [(source, (source + steps) % count) for source...]
    unnamed x12 -> x6, local copies, waits for them, and re-layouts: 3.3 us -> 0.01 us
    all_to_all x1, waiting for transfers between devices: 1.69 us -> 4.38 us  [local(): lax.all_to_all(packed.reshape(chips, 2 * block, cols), 'chip', split_axis...]
  transfers between devices with their start and end apart: 12 -> 9, of which waited for: 6 -> 6; matrix products, arithmetic and copies ran while one was open for 0% -> 1% of each run, Pallas kernels for 4% -> 3%
where the time goes in v5:
time: 163 us
  waiting for transfers between devices  81.7 us (50%)
  Pallas kernels  45.8 us (28%)
  starting transfers between devices  34.2 us (21%)
    all_to_all x1, waiting for transfers between devices, local(): lax.all_to_all(results.reshape(sections * peers, block, cols), ('segment'...  54.7 us
    pallas_call x1, Pallas kernels, local(): call(quarters_kernel, tuple((jax.ShapeDtypeStruct((pair, part), BF16) for...  33 us
    ppermute x6, waiting for transfers between devices, shifted(): lax.ppermute(value, axis, [(source, (source + steps) % count) for source...  21.5 us
    all_to_all x1, starting transfers between devices, local(): lax.all_to_all(packed.reshape(chips, 2 * block, cols), 'chip', split_axis...  11 us
    ppermute x6, starting transfers between devices, shifted(): lax.ppermute(value, axis, [(source, (source + steps) % count) for source...  8.85 us
    all_to_all x1, starting transfers between devices, local(): lax.all_to_all(results.reshape(sections * peers, block, cols), ('segment'...  8.82 us
    ppermute x1, starting transfers between devices, local(): lax.ppermute(theirs, 'core', [(0, 1), (1, 0)]).reshape(chips * block, cols)  5.5 us
    pallas_call x1, Pallas kernels, local(): call(lambda *refs: sections_kernel(width, *refs), jax.ShapeDtypeStruct((s...  4.96 us
  transfers between devices with their start and end apart: 9, of which 6 were waited for; matrix products, arithmetic and copies ran while one was open for 1% of the time, Pallas kernels for 3%

profile of v5, /device:TPU:1, one launch (start us, length us, event | category | flops | bytes accessed | tf_op | source)
XLA Modules:
  0.0 163.0 jit_solution(14984024412911054294)
XLA Ops:
  0.0 33.0 %quarters.1 = (bf16[128,2048]{1,0:T(8,128)(2,1)}, bf16[128,2048]{1,0:T(8,128)(2,1)}, bf16[128,2048]{1,0:T(8,128)(2,1)}, bf16[128,2048]{1,0:T(8,128)(2,1)}) custom-call(s32[1]{0:T(128)} %bitcast.2.plane, bf16[64,8192]{1,0:T(8,128)(2,1)} %bitcast.17, f32[1,8192]{1,0:T(1,128)} %gain.1, bf16[64,8192]{1,0:T(8,128)(2,1)} %bitcast.18), custom_call_target="tpu_custom_call" | custom-call | bytes 4194304 | tf_op jit(solution)/shard_map/quarters/pallas_call | solution.py:274
  33.0 0.0 copy-start
  33.0 2.2 %collective-permute-start = (bf16[128,2048]{1,0:T(8,128)(2,1)}, bf16[128,2048]{1,0:T(8,128)(2,1)S(1)}, u32[]{:S(2)}, u32[]{:S(2)}) collective-permute-start(bf16[128,2048]{1,0:T(8,128)(2,1)} %get-tuple-element.14), channel_id=1, source_target_pairs={{0,64},{64,128},{128,192},{192,0},{1,65},{65,129},{129,193},{193,1... | collective-permute-start | bytes 1572872 | tf_op jit(solution)/shard_map/ppermute | solution.py:20
  35.2 2.6 %collective-permute-start.1 = (bf16[128,2048]{1,0:T(8,128)(2,1)}, bf16[128,2048]{1,0:T(8,128)(2,1)S(1)}, u32[]{:S(2)}, u32[]{:S(2)}) collective-permute-start(bf16[128,2048]{1,0:T(8,128)(2,1)} %get-tuple-element.15), channel_id=1, source_target_pairs={{0,128},{64,192},{128,0},{192,64},{1,129},{65,193},{129,1},{193,65... | collective-permute-start | bytes 1572872 | tf_op jit(solution)/shard_map/ppermute | solution.py:20
  37.8 1.1 collective-permute-start.2
  38.9 0.0 copy-done.1
  38.9 0.0 copy-done.2
  38.9 0.2 select_reduce_fusion
  39.1 0.1 broadcast_add_fusion
  39.2 0.7 add.55.places
  39.8 2.7 %pack.1 = bf16[512,512]{1,0:T(8,128)(2,1)} custom-call(s32[1]{0:T(128)} %bitcast.2.plane, s32[1,256]{1,0:T(1,128)} %add.55.places, bf16[64,8192]{1,0:T(8,128)(2,1)} %hidden.1), custom_call_target="tpu_custom_call" | custom-call | bytes 4194304 | tf_op jit(solution)/shard_map/pack/pallas_call | solution.py:303
  42.6 11.0 %all-to-all-start = ((bf16[32,16,512]{2,1,0:T(8,128)(2,1)}), bf16[32,16,512]{2,1,0:T(8,128)(2,1)S(1)}, u32[]{:S(2)}, u32[]{:S(2)}) async-start(bf16[32,16,512]{2,1,0:T(8,128)(2,1)} %bitcast.16), calls=%async_computation | async-start | bytes 1048576 | tf_op jit(solution)/shard_map/all_to_all | solution.py:315
  53.6 0.1 pad_add_fusion.order.refs_0_
  53.7 0.0 collective-permute-done.first.refs_7_
  53.7 6.9 %collective-permute-done.1.second.refs_8_ = bf16[128,2048]{1,0:T(8,128)(2,1)S(1)} collective-permute-done((bf16[128,2048]{1,0:T(8,128)(2,1)}, bf16[128,2048]{1,0:T(8,128)(2,1)S(1)}, u32[]{:S(2)}, u32[]{:S(2)}) %collective-permute-start.1) | collective-permute-done | bytes 524320 | tf_op jit(solution)/shard_map/ppermute | solution.py:20
  60.6 0.0 collective-permute-done.2.third.refs_9_
  60.6 1.5 factors.1.tiles
  62.2 4.4 %all-to-all-done = bf16[32,16,512]{2,1,0:T(8,128)(2,1)S(1)} async-done(((bf16[32,16,512]{2,1,0:T(8,128)(2,1)}), bf16[32,16,512]{2,1,0:T(8,128)(2,1)S(1)}, u32[]{:S(2)}, u32[]{:S(2)}) %all-to-all-start) | async-done | bytes 524320 | tf_op jit(solution)/shard_map/all_to_all | solution.py:315
  66.6 5.5 %collective-permute-start.3 = (bf16[32,8,512]{2,1,0:T(8,128)(2,1)S(1)}, bf16[32,8,512]{2,1,0:T(8,128)(2,1)S(1)}, u32[]{:S(2)}, u32[]{:S(2)}) collective-permute-start(bf16[32,8,512]{2,1,0:T(8,128)(2,1)S(1)} %constant_dynamic-slice_fusion), channel_id=1, source_target_pairs={{0,1},{1,0},{2,3},{3,2},{4,5},{5,4},{6,7},{7,6},{8,9},{9,8},{10,11... | collective-permute-start | bytes 786440 | tf_op jit(solution)/shard_map/ppermute | solution.py:335
  72.1 1.2 collective-permute-done.3
  73.2 1.9 %products.1 = (bf16[128,1280]{1,0:T(8,128)(2,1)S(1)}, bf16[128,2048]{1,0:T(8,128)(2,1)S(1)}) custom-call(s32[5]{0:T(128)S(1)} %pad_add_fusion.order.refs_0_, bf16[512,512]{1,0:T(8,128)(2,1)S(1)} %bitcast.14, bf16[256,512]{1,0:T(8,128)(2,1)S(1)} %bitcast.15, f32[384,128]{1,0:T(8,128)S(1)} %factors.1.tiles, bf16[128,2048]{1,0:T(8,128)(2,1)S(1)} %copy-done, ...), custom_call_target="tpu_custom_call" | custom-call | bytes 4194304 | tf_op jit(solution)/shard_map/products/pallas_call | solution.py:336
  75.2 0.5 collective-permute-start.4
  75.6 0.7 collective-permute-start.5
  76.3 1.8 %collective-permute-start.6 = (bf16[128,1280]{1,0:T(8,128)(2,1)S(1)}, bf16[128,1280]{1,0:T(8,128)(2,1)S(1)}, u32[]{:S(2)}, u32[]{:S(2)}) collective-permute-start(bf16[128,1280]{1,0:T(8,128)(2,1)S(1)} %get-tuple-element.19.refs_1_), channel_id=1, source_target_pairs={{0,192},{64,0},{128,64},{192,128},{1,193},{65,1},{129,65},{193,129... | collective-permute-start | bytes 983048 | tf_op jit(solution)/shard_map/ppermute | solution.py:20
  78.1 14.3 %collective-permute-done.4.refs_2_ = bf16[128,1280]{1,0:T(8,128)(2,1)S(1)} collective-permute-done((bf16[128,1280]{1,0:T(8,128)(2,1)S(1)}, bf16[128,1280]{1,0:T(8,128)(2,1)S(1)}, u32[]{:S(2)}, u32[]{:S(2)}) %collective-permute-start.4) | collective-permute-done | bytes 327712 | tf_op jit(solution)/shard_map/ppermute | solution.py:20
  92.4 0.0 collective-permute-done.5.refs_3_
  92.4 0.3 collective-permute-done.6.refs_4_
  92.7 5.0 %sections.1 = bf16[2048,512]{1,0:T(8,128)(2,1)} custom-call(s32[5]{0:T(128)S(1)} %pad_add_fusion.order.refs_0_, bf16[128,1280]{1,0:T(8,128)(2,1)S(1)} %get-tuple-element.19.refs_1_, bf16[128,1280]{1,0:T(8,128)(2,1)S(1)} %collective-permute-done.4.refs_2_, bf16[128,1280]{1,0:T(8,128)(2,1)S(1)} %collective-permute-done.5.refs_3_, ...), custom_call_target="tpu_custom_call" | custom-call | bytes 4194304 | tf_op jit(solution)/shard_map/sections/pallas_call | solution.py:348
  97.7 8.8 %all-to-all-start.1 = ((bf16[256,8,512]{2,1,0:T(8,128)(2,1)}), bf16[256,8,512]{2,1,0:T(8,128)(2,1)S(1)}, u32[]{:S(2)}, u32[]{:S(2)}) async-start(bf16[256,8,512]{2,1,0:T(8,128)(2,1)} %bitcast.9), calls=%async_computation.1 | async-start | bytes 4194304 | tf_op jit(solution)/shard_map/all_to_all | solution.py:359
  106.5 0.1 add.57.places
  106.6 54.7 %all-to-all-done.1 = bf16[256,8,512]{2,1,0:T(8,128)(2,1)S(1)} async-done(((bf16[256,8,512]{2,1,0:T(8,128)(2,1)}), bf16[256,8,512]{2,1,0:T(8,128)(2,1)S(1)}, u32[]{:S(2)}, u32[]{:S(2)}) %all-to-all-start.1) | async-done | bytes 2097184 | tf_op jit(solution)/shard_map/all_to_all | solution.py:359
  161.3 1.7 %unpack.1 = bf16[64,8192]{1,0:T(8,128)(2,1)} custom-call(s32[256,1]{1,0:T(8,128)S(1)} %add.57.places, bf16[4,512,512]{2,1,0:T(8,128)(2,1)S(1)} %bitcast.13), custom_call_target="tpu_custom_call" | custom-call | bytes 4194304 | tf_op jit(solution)/shard_map/unpack/pallas_call | solution.py:366
  (7 shorter events, 0.0 us)
Async XLA Ops:
  0.0 38.9 %copy-start.1 = (s32[64,1]{0,1:T(1,128)S(1)}, s32[64,1]{0,1:T(1,128)}, u32[]{:S(2)}) copy-start(s32[64,1]{0,1:T(1,128)} %param.7) | copy-start | bytes 772
  0.0 38.9 %copy-start.2 = (s32[64]{0:T(128)S(1)}, s32[64]{0:T(128)}, u32[]{:S(2)}) copy-start(s32[64]{0:T(128)} %param.8) | copy-start | bytes 772
  33.0 27.6 %copy-start = (bf16[128,2048]{1,0:T(8,128)(2,1)S(1)}, bf16[128,2048]{1,0:T(8,128)(2,1)}, u32[]{:S(2)}) copy-start(bf16[128,2048]{1,0:T(8,128)(2,1)} %get-tuple-element.13.own.refs_6_) | copy-start | bytes 1572868
  33.0 20.7 %collective-permute-start = (bf16[128,2048]{1,0:T(8,128)(2,1)}, bf16[128,2048]{1,0:T(8,128)(2,1)S(1)}, u32[]{:S(2)}, u32[]{:S(2)}) collective-permute-start(bf16[128,2048]{1,0:T(8,128)(2,1)} %get-tuple-element.14), channel_id=1, source_target_pairs={{0,64},{64,128},{128,192},{192,0},{1,65},{65,129},{129,193},{193,1... | collective-permute-start | bytes 1572872 | tf_op jit(solution)/shard_map/ppermute | solution.py:20
  35.2 25.4 %collective-permute-start.1 = (bf16[128,2048]{1,0:T(8,128)(2,1)}, bf16[128,2048]{1,0:T(8,128)(2,1)S(1)}, u32[]{:S(2)}, u32[]{:S(2)}) collective-permute-start(bf16[128,2048]{1,0:T(8,128)(2,1)} %get-tuple-element.15), channel_id=1, source_target_pairs={{0,128},{64,192},{128,0},{192,64},{1,129},{65,193},{129,1},{193,65... | collective-permute-start | bytes 1572872 | tf_op jit(solution)/shard_map/ppermute | solution.py:20
  37.8 22.8 %collective-permute-start.2 = (bf16[128,2048]{1,0:T(8,128)(2,1)}, bf16[128,2048]{1,0:T(8,128)(2,1)S(1)}, u32[]{:S(2)}, u32[]{:S(2)}) collective-permute-start(bf16[128,2048]{1,0:T(8,128)(2,1)} %get-tuple-element.16), channel_id=1, source_target_pairs={{0,192},{64,0},{128,64},{192,128},{1,193},{65,1},{129,65},{193,129... | collective-permute-start | bytes 1572872 | tf_op jit(solution)/shard_map/ppermute | solution.py:20
  42.6 24.0 %all-to-all-start = ((bf16[32,16,512]{2,1,0:T(8,128)(2,1)}), bf16[32,16,512]{2,1,0:T(8,128)(2,1)S(1)}, u32[]{:S(2)}, u32[]{:S(2)}) async-start(bf16[32,16,512]{2,1,0:T(8,128)(2,1)} %bitcast.16), calls=%async_computation | async-start | bytes 1048576 | tf_op jit(solution)/shard_map/all_to_all | solution.py:315
  66.6 6.7 %collective-permute-start.3 = (bf16[32,8,512]{2,1,0:T(8,128)(2,1)S(1)}, bf16[32,8,512]{2,1,0:T(8,128)(2,1)S(1)}, u32[]{:S(2)}, u32[]{:S(2)}) collective-permute-start(bf16[32,8,512]{2,1,0:T(8,128)(2,1)S(1)} %constant_dynamic-slice_fusion), channel_id=1, source_target_pairs={{0,1},{1,0},{2,3},{3,2},{4,5},{5,4},{6,7},{7,6},{8,9},{9,8},{10,11... | collective-permute-start | bytes 786440 | tf_op jit(solution)/shard_map/ppermute | solution.py:335
  75.2 17.2 %collective-permute-start.4 = (bf16[128,1280]{1,0:T(8,128)(2,1)S(1)}, bf16[128,1280]{1,0:T(8,128)(2,1)S(1)}, u32[]{:S(2)}, u32[]{:S(2)}) collective-permute-start(bf16[128,1280]{1,0:T(8,128)(2,1)S(1)} %get-tuple-element.19.refs_1_), channel_id=1, source_target_pairs={{0,64},{64,128},{128,192},{192,0},{1,65},{65,129},{129,193},{193,1... | collective-permute-start | bytes 983048 | tf_op jit(solution)/shard_map/ppermute | solution.py:20
  75.6 16.7 %collective-permute-start.5 = (bf16[128,1280]{1,0:T(8,128)(2,1)S(1)}, bf16[128,1280]{1,0:T(8,128)(2,1)S(1)}, u32[]{:S(2)}, u32[]{:S(2)}) collective-permute-start(bf16[128,1280]{1,0:T(8,128)(2,1)S(1)} %get-tuple-element.19.refs_1_), channel_id=1, source_target_pairs={{0,128},{64,192},{128,0},{192,64},{1,129},{65,193},{129,1},{193,65... | collective-permute-start | bytes 983048 | tf_op jit(solution)/shard_map/ppermute | solution.py:20
  76.3 16.4 %collective-permute-start.6 = (bf16[128,1280]{1,0:T(8,128)(2,1)S(1)}, bf16[128,1280]{1,0:T(8,128)(2,1)S(1)}, u32[]{:S(2)}, u32[]{:S(2)}) collective-permute-start(bf16[128,1280]{1,0:T(8,128)(2,1)S(1)} %get-tuple-element.19.refs_1_), channel_id=1, source_target_pairs={{0,192},{64,0},{128,64},{192,128},{1,193},{65,1},{129,65},{193,129... | collective-permute-start | bytes 983048 | tf_op jit(solution)/shard_map/ppermute | solution.py:20
  97.7 63.7 %all-to-all-start.1 = ((bf16[256,8,512]{2,1,0:T(8,128)(2,1)}), bf16[256,8,512]{2,1,0:T(8,128)(2,1)S(1)}, u32[]{:S(2)}, u32[]{:S(2)}) async-start(bf16[256,8,512]{2,1,0:T(8,128)(2,1)} %bitcast.9), calls=%async_computation.1 | async-start | bytes 4194304 | tf_op jit(solution)/shard_map/all_to_all | solution.py:359

commit v6 on v5

--- a/solution.py
+++ b/solution.py
@@ -26,12 +26,12 @@
     )
 
 
-def call(kernel, outs, *, scratch=(), flops=0, specs=None, out_spec=VMEM, room=48, **options):
+def call(kernel, outs, *, scratch=(), flops=0, specs=None, room=48, **options):
     return pl.pallas_call(
         kernel,
         out_shape=outs,
         in_specs=specs,
-        out_specs=jax.tree.map(lambda _: out_spec, outs),
+        out_specs=jax.tree.map(lambda _: VMEM, outs),
         scratch_shapes=list(scratch),
         compiler_params=pltpu.CompilerParams(vmem_limit_bytes=room * 1024 * 1024),
         cost_estimate=pl.CostEstimate(flops=flops, bytes_accessed=4 << 20, transcendentals=0),
@@ -61,47 +61,44 @@
     return pl.ds(pl.multiple_of(lax.rem(plane + steps, planes) * part, part), part)
 
 
-def pack_kernel(plane, places, hidden, out, mine, arrival):
+def pack_kernel(places, hidden, out):
     cols = out.shape[1]
-    part = mine.shape[1]
-    copy = pltpu.make_async_copy(
-        hidden.at[:, quarter_columns(plane[0], 0, part)], mine, arrival
-    )
-    copy.start()
     chosen = one_hot(places[...], (out.shape[0], places.shape[1]), 0)
-    copy.wait()
-    stacked = jnp.concatenate([mine[:, g * cols : (g + 1) * cols] for g in range(GROUPS)], axis=0)
+    stacked = jnp.concatenate(
+        [hidden[:, g * cols : (g + 1) * cols] for g in range(GROUPS)], axis=0
+    )
     out[...] = dot(chosen, stacked).astype(BF16)
 
 
 def quarters_kernel(
-    plane, shrink, gain, expand, q0, q1, q2, q3, taken, weights, made, gain_in, in_sem, put_sem, out_sem
+    plane, shrink, gain, expand, q0, q1, q2, q3, taken, weights, gain_in, in_sem, put_sem
 ):
     rank = shrink.shape[0]
     outs = (q0, q1, q2, q3)
     part = q0.shape[1]
-    columns = [quarter_columns(plane[0], steps, part) for steps in range(4)]
-    order = (2, 1, 3, 0)
+    columns = [
+        pl.ds(pl.multiple_of(lax.rem(plane[0] + k, 4) * part, part), part) for k in range(4)
+    ]
     load = pltpu.make_async_copy(gain, weights, gain_in)
     load.start()
-    ins, puts, sends = {}, {}, {}
-    for k in order:
-        ins[k] = pltpu.make_async_copy(shrink.at[:, columns[k]], taken.at[k], in_sem.at[k])
-        ins[k].start()
-    for k in order:
-        puts[k] = pltpu.make_async_copy(
+    ins = [
+        pltpu.make_async_copy(shrink.at[:, columns[k]], taken.at[k], in_sem.at[k])
+        for k in range(4)
+    ]
+    puts = [
+        pltpu.make_async_copy(
             expand.at[:, columns[k]], outs[k].at[pl.ds(rank, rank)], put_sem.at[k]
         )
-        puts[k].start()
+        for k in range(4)
+    ]
+    for copy in ins + puts:
+        copy.start()
     load.wait()
-    for k in order:
+    for k in range(4):
         ins[k].wait()
-        made[k] = (taken[k].astype(F32) * weights[:, columns[k]]).astype(BF16)
-        sends[k] = pltpu.make_async_copy(made.at[k], outs[k].at[pl.ds(0, rank)], out_sem.at[k])
-        sends[k].start()
-    for k in order:
-        puts[k].wait()
-        sends[k].wait()
+        outs[k][:rank] = (taken[k].astype(F32) * weights[:, columns[k]]).astype(BF16)
+    for copy in puts:
+        copy.wait()
 
 
 def factors_kernel(order, own, first, second, third, tiles, every, expand):
@@ -277,14 +274,11 @@
         scratch=[
             pltpu.VMEM((sections, rank, part), BF16),
             pltpu.VMEM((1, width), F32),
-            pltpu.VMEM((sections, rank, part), BF16),
             pltpu.SemaphoreType.DMA,
-            pltpu.SemaphoreType.DMA((sections,)),
             pltpu.SemaphoreType.DMA((sections,)),
             pltpu.SemaphoreType.DMA((sections,)),
         ],
         specs=[SMEM, ANY, ANY, ANY],
-        out_spec=ANY,
         room=60,
         name="quarters",
     )(plane.reshape(1), shrink_tiles[0, 0].T, gains, expand_tiles[0, 0])
@@ -300,14 +294,13 @@
     groups = jnp.arange(GROUPS, dtype=jnp.int32)[:, None] * depth
     homes = (groups + (storage * block + earlier)[None, :]).reshape(-1)
 
+    mine = lax.dynamic_slice(hidden_in, (0, plane * part), (count, part))
     packed = call(
         pack_kernel,
         jax.ShapeDtypeStruct((size, cols), BF16),
-        scratch=[pltpu.VMEM((count, part), BF16), pltpu.SemaphoreType.DMA],
-        specs=[SMEM, VMEM, ANY],
-        room=60,
+        specs=[VMEM, VMEM],
         name="pack",
-    )(plane.reshape(1), homes[None, :], hidden_in)
+    )(homes[None, :], mine)
     held = [quarters[0]] + [
         shifted(quarters[steps], "segment", steps) for steps in range(1, sections)
     ]

time: 163 us -> 133 us (0.82)
  Pallas kernels: 45.8 us -> 15 us
    pallas_call x1, Pallas kernels: 33 us -> 3 us  [local(): call(quarters_kernel, tuple((jax.ShapeDtypeStruct((pair, part), BF16) for...]
    all_to_all x1, waiting for transfers between devices: 4.38 us -> 1.69 us  [local(): lax.all_to_all(packed.reshape(chips, 2 * block, cols), 'chip', split_axis...]
    pallas_call x1, Pallas kernels: 2.72 us -> 0.3 us  [local(): call(pack_kernel, jax.ShapeDtypeStruct((size, cols), BF16), specs=[VMEM,...]
    ppermute x6, waiting for transfers between devices: 21.5 us -> 23.7 us  [shifted(): lax.ppermute(value, axis, [(source, (source + steps) % count) for source...]
  transfers between devices with their start and end apart: 9 -> 9, of which waited for: 6 -> 6; matrix products, arithmetic and copies ran while one was open for 1% -> 0% of each run, Pallas kernels for 3% -> 2%
where the time goes in v6:
time: 133 us
  waiting for transfers between devices  81.2 us (61%)
  starting transfers between devices  35 us (26%)
  Pallas kernels  15 us (11%)
    all_to_all x1, waiting for transfers between devices, local(): lax.all_to_all(results.reshape(sections * peers, block, cols), ('segment'...  54.7 us
    ppermute x6, waiting for transfers between devices, shifted(): lax.ppermute(value, axis, [(source, (source + steps) % count) for source...  23.7 us
    all_to_all x1, starting transfers between devices, local(): lax.all_to_all(packed.reshape(chips, 2 * block, cols), 'chip', split_axis...  11 us
    all_to_all x1, starting transfers between devices, local(): lax.all_to_all(results.reshape(sections * peers, block, cols), ('segment'...  9.59 us
    ppermute x6, starting transfers between devices, shifted(): lax.ppermute(value, axis, [(source, (source + steps) % count) for source...  8.87 us
    pallas_call x1, Pallas kernels, local(): call(lambda *refs: sections_kernel(width, *refs), jax.ShapeDtypeStruct((s...  5.47 us
    ppermute x1, starting transfers between devices, local(): lax.ppermute(theirs, 'core', [(0, 1), (1, 0)]).reshape(chips * block, cols)  5.47 us
    pallas_call x1, Pallas kernels, local(): call(quarters_kernel, tuple((jax.ShapeDtypeStruct((pair, part), BF16) for...  3 us
  transfers between devices with their start and end apart: 9, of which 6 were waited for; matrix products, arithmetic and copies ran while one was open for 0% of the time, Pallas kernels for 2%

profile of v6, /device:TPU:1, one launch (start us, length us, event | category | flops | bytes accessed | tf_op | source)
XLA Modules:
  0.0 132.7 jit_solution(7626645217710850227)
XLA Ops:
  0.0 0.0 copy-start
  0.0 3.0 %quarters.1 = (bf16[128,2048]{1,0:T(8,128)(2,1)}, bf16[128,2048]{1,0:T(8,128)(2,1)}, bf16[128,2048]{1,0:T(8,128)(2,1)}, bf16[128,2048]{1,0:T(8,128)(2,1)}) custom-call(s32[1]{0:T(128)} %bitcast.3.plane, bf16[64,8192]{1,0:T(8,128)(2,1)} %bitcast.17, f32[1,8192]{1,0:T(1,128)} %gain.1, bf16[64,8192]{1,0:T(8,128)(2,1)} %bitcast.18), custom_call_target="tpu_custom_call" | custom-call | bytes 4194304 | tf_op jit(solution)/shard_map/quarters/pallas_call | solution.py:271
  3.0 2.2 %collective-permute-start = (bf16[128,2048]{1,0:T(8,128)(2,1)}, bf16[128,2048]{1,0:T(8,128)(2,1)S(1)}, u32[]{:S(2)}, u32[]{:S(2)}) collective-permute-start(bf16[128,2048]{1,0:T(8,128)(2,1)} %get-tuple-element.14), channel_id=1, source_target_pairs={{0,64},{64,128},{128,192},{192,0},{1,65},{65,129},{129,193},{193,1... | collective-permute-start | bytes 1572872 | tf_op jit(solution)/shard_map/ppermute | solution.py:20
  5.2 2.6 %collective-permute-start.1 = (bf16[128,2048]{1,0:T(8,128)(2,1)}, bf16[128,2048]{1,0:T(8,128)(2,1)S(1)}, u32[]{:S(2)}, u32[]{:S(2)}) collective-permute-start(bf16[128,2048]{1,0:T(8,128)(2,1)} %get-tuple-element.15), channel_id=1, source_target_pairs={{0,128},{64,192},{128,0},{192,64},{1,129},{65,193},{129,1},{193,65... | collective-permute-start | bytes 1572872 | tf_op jit(solution)/shard_map/ppermute | solution.py:20
  7.9 1.1 collective-permute-start.2
  8.9 0.2 select_reduce_fusion
  9.1 0.1 broadcast_add_fusion
  9.2 0.1 add.58.places
  9.3 0.3 pack.1
  9.6 0.0 copy-start.2
  9.6 0.8 copy-done.2
  10.4 11.0 %all-to-all-start = ((bf16[32,16,512]{2,1,0:T(8,128)(2,1)}), bf16[32,16,512]{2,1,0:T(8,128)(2,1)S(1)}, u32[]{:S(2)}, u32[]{:S(2)}) async-start(bf16[32,16,512]{2,1,0:T(8,128)(2,1)} %bitcast.15), calls=%async_computation | async-start | bytes 1048576 | tf_op jit(solution)/shard_map/all_to_all | solution.py:308
  21.5 0.1 pad_add_fusion.order.refs_0_
  21.6 0.0 collective-permute-done.first.refs_7_
  21.6 9.1 %collective-permute-done.1.second.refs_8_ = bf16[128,2048]{1,0:T(8,128)(2,1)S(1)} collective-permute-done((bf16[128,2048]{1,0:T(8,128)(2,1)}, bf16[128,2048]{1,0:T(8,128)(2,1)S(1)}, u32[]{:S(2)}, u32[]{:S(2)}) %collective-permute-start.1) | collective-permute-done | bytes 524320 | tf_op jit(solution)/shard_map/ppermute | solution.py:20
  30.6 0.0 collective-permute-done.2.third.refs_9_
  30.6 2.0 %factors.1.tiles = f32[384,128]{1,0:T(8,128)S(1)} custom-call(s32[5]{0:T(128)S(1)} %pad_add_fusion.order.refs_0_, bf16[128,2048]{1,0:T(8,128)(2,1)S(1)} %copy-done.1, bf16[128,2048]{1,0:T(8,128)(2,1)S(1)} %collective-permute-done.first.refs_7_, bf16[128,2048]{1,0:T(8,128)(2,1)S(1)} %collective-permute-done.1.second.refs_8_, ...), custom_call_target="tpu_custom_call" | custom-call | flops 40000000000 | bytes 4194304 | tf_op jit(solution)/shard_map/factors/pallas_call | solution.py:314
  32.7 1.7 %all-to-all-done = bf16[32,16,512]{2,1,0:T(8,128)(2,1)S(1)} async-done(((bf16[32,16,512]{2,1,0:T(8,128)(2,1)}), bf16[32,16,512]{2,1,0:T(8,128)(2,1)S(1)}, u32[]{:S(2)}, u32[]{:S(2)}) %all-to-all-start) | async-done | bytes 524320 | tf_op jit(solution)/shard_map/all_to_all | solution.py:308
  34.4 5.5 %collective-permute-start.3 = (bf16[32,8,512]{2,1,0:T(8,128)(2,1)S(1)}, bf16[32,8,512]{2,1,0:T(8,128)(2,1)S(1)}, u32[]{:S(2)}, u32[]{:S(2)}) collective-permute-start(bf16[32,8,512]{2,1,0:T(8,128)(2,1)S(1)} %constant_dynamic-slice_fusion), channel_id=1, source_target_pairs={{0,1},{1,0},{2,3},{3,2},{4,5},{5,4},{6,7},{7,6},{8,9},{9,8},{10,11... | collective-permute-start | bytes 786440 | tf_op jit(solution)/shard_map/ppermute | solution.py:328
  39.9 1.2 collective-permute-done.3
  41.0 2.4 %products.1 = (bf16[128,1280]{1,0:T(8,128)(2,1)S(1)}, bf16[128,2048]{1,0:T(8,128)(2,1)S(1)}) custom-call(s32[5]{0:T(128)S(1)} %pad_add_fusion.order.refs_0_, bf16[512,512]{1,0:T(8,128)(2,1)S(1)} %bitcast.14, bf16[256,512]{1,0:T(8,128)(2,1)S(1)} %bitcast.16, f32[384,128]{1,0:T(8,128)S(1)} %factors.1.tiles, bf16[128,2048]{1,0:T(8,128)(2,1)S(1)} %copy-done.1, ...), custom_call_target="tpu_custom_call" | custom-call | bytes 4194304 | tf_op jit(solution)/shard_map/products/pallas_call | solution.py:329
  43.5 0.5 collective-permute-start.4
  44.0 0.7 collective-permute-start.5
  44.7 1.8 %collective-permute-start.6 = (bf16[128,1280]{1,0:T(8,128)(2,1)S(1)}, bf16[128,1280]{1,0:T(8,128)(2,1)S(1)}, u32[]{:S(2)}, u32[]{:S(2)}) collective-permute-start(bf16[128,1280]{1,0:T(8,128)(2,1)S(1)} %get-tuple-element.19.refs_1_), channel_id=1, source_target_pairs={{0,192},{64,0},{128,64},{192,128},{1,193},{65,1},{129,65},{193,129... | collective-permute-start | bytes 983048 | tf_op jit(solution)/shard_map/ppermute | solution.py:20
  46.5 14.3 %collective-permute-done.4.refs_2_ = bf16[128,1280]{1,0:T(8,128)(2,1)S(1)} collective-permute-done((bf16[128,1280]{1,0:T(8,128)(2,1)S(1)}, bf16[128,1280]{1,0:T(8,128)(2,1)S(1)}, u32[]{:S(2)}, u32[]{:S(2)}) %collective-permute-start.4) | collective-permute-done | bytes 327712 | tf_op jit(solution)/shard_map/ppermute | solution.py:20
  60.7 0.0 collective-permute-done.5.refs_3_
  60.7 0.4 collective-permute-done.6.refs_4_
  61.1 5.5 %sections.1 = bf16[2048,512]{1,0:T(8,128)(2,1)} custom-call(s32[5]{0:T(128)S(1)} %pad_add_fusion.order.refs_0_, bf16[128,1280]{1,0:T(8,128)(2,1)S(1)} %get-tuple-element.19.refs_1_, bf16[128,1280]{1,0:T(8,128)(2,1)S(1)} %collective-permute-done.4.refs_2_, bf16[128,1280]{1,0:T(8,128)(2,1)S(1)} %collective-permute-done.5.refs_3_, ...), custom_call_target="tpu_custom_call" | custom-call | bytes 4194304 | tf_op jit(solution)/shard_map/sections/pallas_call | solution.py:341
  66.6 9.6 %all-to-all-start.1 = ((bf16[256,8,512]{2,1,0:T(8,128)(2,1)}), bf16[256,8,512]{2,1,0:T(8,128)(2,1)S(1)}, u32[]{:S(2)}, u32[]{:S(2)}) async-start(bf16[256,8,512]{2,1,0:T(8,128)(2,1)} %bitcast.9), calls=%async_computation.1 | async-start | bytes 4194304 | tf_op jit(solution)/shard_map/all_to_all | solution.py:352
  76.2 0.1 add.61.places
  76.3 54.7 %all-to-all-done.1 = bf16[256,8,512]{2,1,0:T(8,128)(2,1)S(1)} async-done(((bf16[256,8,512]{2,1,0:T(8,128)(2,1)}), bf16[256,8,512]{2,1,0:T(8,128)(2,1)S(1)}, u32[]{:S(2)}, u32[]{:S(2)}) %all-to-all-start.1) | async-done | bytes 2097184 | tf_op jit(solution)/shard_map/all_to_all | solution.py:352
  131.0 1.7 %unpack.1 = bf16[64,8192]{1,0:T(8,128)(2,1)} custom-call(s32[256,1]{1,0:T(8,128)S(1)} %add.61.places, bf16[4,512,512]{2,1,0:T(8,128)(2,1)S(1)} %bitcast.13), custom_call_target="tpu_custom_call" | custom-call | bytes 4194304 | tf_op jit(solution)/shard_map/unpack/pallas_call | solution.py:359
  (12 shorter events, 0.1 us)
Async XLA Ops:
  0.0 9.3 %copy-start = (bf16[64,8192]{1,0:T(8,128)(2,1)S(1)}, bf16[64,8192]{1,0:T(8,128)(2,1)}, u32[]{:S(2)}) copy-start(bf16[64,8192]{1,0:T(8,128)(2,1)} %param.6) | copy-start | bytes 3145732
  0.0 8.9 %copy-start.3 = (s32[64,1]{0,1:T(1,128)S(1)}, s32[64,1]{0,1:T(1,128)}, u32[]{:S(2)}) copy-start(s32[64,1]{0,1:T(1,128)} %param.7) | copy-start | bytes 772
  0.0 8.9 %copy-start.4 = (s32[64]{0:T(128)S(1)}, s32[64]{0:T(128)}, u32[]{:S(2)}) copy-start(s32[64]{0:T(128)} %param.8) | copy-start | bytes 772
  3.0 27.6 %copy-start.1 = (bf16[128,2048]{1,0:T(8,128)(2,1)S(1)}, bf16[128,2048]{1,0:T(8,128)(2,1)}, u32[]{:S(2)}) copy-start(bf16[128,2048]{1,0:T(8,128)(2,1)} %get-tuple-element.13.own.refs_6_) | copy-start | bytes 1572868
  3.0 18.5 %collective-permute-start = (bf16[128,2048]{1,0:T(8,128)(2,1)}, bf16[128,2048]{1,0:T(8,128)(2,1)S(1)}, u32[]{:S(2)}, u32[]{:S(2)}) collective-permute-start(bf16[128,2048]{1,0:T(8,128)(2,1)} %get-tuple-element.14), channel_id=1, source_target_pairs={{0,64},{64,128},{128,192},{192,0},{1,65},{65,129},{129,193},{193,1... | collective-permute-start | bytes 1572872 | tf_op jit(solution)/shard_map/ppermute | solution.py:20
  5.2 25.4 %collective-permute-start.1 = (bf16[128,2048]{1,0:T(8,128)(2,1)}, bf16[128,2048]{1,0:T(8,128)(2,1)S(1)}, u32[]{:S(2)}, u32[]{:S(2)}) collective-permute-start(bf16[128,2048]{1,0:T(8,128)(2,1)} %get-tuple-element.15), channel_id=1, source_target_pairs={{0,128},{64,192},{128,0},{192,64},{1,129},{65,193},{129,1},{193,65... | collective-permute-start | bytes 1572872 | tf_op jit(solution)/shard_map/ppermute | solution.py:20
  7.9 22.8 %collective-permute-start.2 = (bf16[128,2048]{1,0:T(8,128)(2,1)}, bf16[128,2048]{1,0:T(8,128)(2,1)}, u32[]{:S(2)}, u32[]{:S(2)}) collective-permute-start(bf16[128,2048]{1,0:T(8,128)(2,1)} %get-tuple-element.16), channel_id=1, source_target_pairs={{0,192},{64,0},{128,64},{192,128},{1,193},{65,1},{129,65},{193,129... | collective-permute-start | bytes 1572872 | tf_op jit(solution)/shard_map/ppermute | solution.py:20
  9.6 0.8 copy-start.2
  10.4 24.0 %all-to-all-start = ((bf16[32,16,512]{2,1,0:T(8,128)(2,1)}), bf16[32,16,512]{2,1,0:T(8,128)(2,1)S(1)}, u32[]{:S(2)}, u32[]{:S(2)}) async-start(bf16[32,16,512]{2,1,0:T(8,128)(2,1)} %bitcast.15), calls=%async_computation | async-start | bytes 1048576 | tf_op jit(solution)/shard_map/all_to_all | solution.py:308
  34.4 6.6 %collective-permute-start.3 = (bf16[32,8,512]{2,1,0:T(8,128)(2,1)S(1)}, bf16[32,8,512]{2,1,0:T(8,128)(2,1)S(1)}, u32[]{:S(2)}, u32[]{:S(2)}) collective-permute-start(bf16[32,8,512]{2,1,0:T(8,128)(2,1)S(1)} %constant_dynamic-slice_fusion), channel_id=1, source_target_pairs={{0,1},{1,0},{2,3},{3,2},{4,5},{5,4},{6,7},{7,6},{8,9},{9,8},{10,11... | collective-permute-start | bytes 786440 | tf_op jit(solution)/shard_map/ppermute | solution.py:328
  43.5 17.2 %collective-permute-start.4 = (bf16[128,1280]{1,0:T(8,128)(2,1)S(1)}, bf16[128,1280]{1,0:T(8,128)(2,1)S(1)}, u32[]{:S(2)}, u32[]{:S(2)}) collective-permute-start(bf16[128,1280]{1,0:T(8,128)(2,1)S(1)} %get-tuple-element.19.refs_1_), channel_id=1, source_target_pairs={{0,64},{64,128},{128,192},{192,0},{1,65},{65,129},{129,193},{193,1... | collective-permute-start | bytes 983048 | tf_op jit(solution)/shard_map/ppermute | solution.py:20
  44.0 16.8 %collective-permute-start.5 = (bf16[128,1280]{1,0:T(8,128)(2,1)S(1)}, bf16[128,1280]{1,0:T(8,128)(2,1)S(1)}, u32[]{:S(2)}, u32[]{:S(2)}) collective-permute-start(bf16[128,1280]{1,0:T(8,128)(2,1)S(1)} %get-tuple-element.19.refs_1_), channel_id=1, source_target_pairs={{0,128},{64,192},{128,0},{192,64},{1,129},{65,193},{129,1},{193,65... | collective-permute-start | bytes 983048 | tf_op jit(solution)/shard_map/ppermute | solution.py:20
  44.7 16.4 %collective-permute-start.6 = (bf16[128,1280]{1,0:T(8,128)(2,1)S(1)}, bf16[128,1280]{1,0:T(8,128)(2,1)S(1)}, u32[]{:S(2)}, u32[]{:S(2)}) collective-permute-start(bf16[128,1280]{1,0:T(8,128)(2,1)S(1)} %get-tuple-element.19.refs_1_), channel_id=1, source_target_pairs={{0,192},{64,0},{128,64},{192,128},{1,193},{65,1},{129,65},{193,129... | collective-permute-start | bytes 983048 | tf_op jit(solution)/shard_map/ppermute | solution.py:20
  66.6 64.4 %all-to-all-start.1 = ((bf16[256,8,512]{2,1,0:T(8,128)(2,1)}), bf16[256,8,512]{2,1,0:T(8,128)(2,1)S(1)}, u32[]{:S(2)}, u32[]{:S(2)}) async-start(bf16[256,8,512]{2,1,0:T(8,128)(2,1)} %bitcast.9), calls=%async_computation.1 | async-start | bytes 4194304 | tf_op jit(solution)/shard_map/all_to_all | solution.py:352

commit v7 on v6

--- a/solution.py
+++ b/solution.py
@@ -26,12 +26,12 @@
     )
 
 
-def call(kernel, outs, *, scratch=(), flops=0, specs=None, room=48, **options):
+def call(kernel, outs, *, scratch=(), flops=0, specs=None, out_spec=VMEM, room=48, **options):
     return pl.pallas_call(
         kernel,
         out_shape=outs,
         in_specs=specs,
-        out_specs=jax.tree.map(lambda _: VMEM, outs),
+        out_specs=jax.tree.map(lambda _: out_spec, outs),
         scratch_shapes=list(scratch),
         compiler_params=pltpu.CompilerParams(vmem_limit_bytes=room * 1024 * 1024),
         cost_estimate=pl.CostEstimate(flops=flops, bytes_accessed=4 << 20, transcendentals=0),
@@ -101,13 +101,27 @@
         copy.wait()
 
 
-def factors_kernel(order, own, first, second, third, tiles, every, expand):
+def ordered_copies(order, refs, first_row, rows, target, arrivals):
+    copies = []
+    for steps, ref in enumerate(refs):
+        start = pl.multiple_of(order[steps] * rows, rows)
+        copies.append(
+            pltpu.make_async_copy(
+                ref.at[pl.ds(first_row, rows)], target.at[pl.ds(start, rows)], arrivals.at[steps]
+            )
+        )
+        copies[-1].start()
+    return copies
+
+
+def factors_kernel(order, own, first, second, third, tiles, every, expand, every_in, expand_in):
     pair = own.shape[0]
     rank = pair // 2
-    for steps, ref in enumerate((own, first, second, third)):
-        section = order[steps]
-        every[pl.ds(pl.multiple_of(section * pair, pair), pair), :] = ref[...]
-        expand[pl.ds(pl.multiple_of(section * rank, rank), rank), :] = ref[rank:]
+    refs = (own, first, second, third)
+    copies = ordered_copies(order, refs, 0, pair, every, every_in)
+    copies += ordered_copies(order, refs, rank, rank, expand, expand_in)
+    for copy in copies:
+        copy.wait()
     product = dot(expand[: 3 * rank], every[...], 1)
 
     def tile(row, section):
@@ -129,38 +143,42 @@
     return high, value - high.astype(F32)
 
 
-def products_kernel(
-    order, blocks, others, tiles, own, first, second, third, sums, plain, product
-):
+def plain_kernel(core, blocks, others, plain, squares):
     count, width = plain.shape
     cols = width // GROUPS
     size = count * GROUPS
-    core = order[4]
     stacked = dot(
-        one_hot(block_places((size, 1), 0, count, core, True), (size, blocks.shape[0]), 1),
+        one_hot(block_places((size, 1), 0, count, core[0], True), (size, blocks.shape[0]), 1),
         blocks[...],
     ) + dot(
-        one_hot(block_places((size, 1), 0, count, core, False), (size, others.shape[0]), 1),
+        one_hot(block_places((size, 1), 0, count, core[0], False), (size, others.shape[0]), 1),
         others[...],
     )
-    stacked = stacked.astype(BF16)
+    total = jnp.zeros((count, 1), F32)
     for g in range(GROUPS):
-        plain[:, g * cols : (g + 1) * cols] = stacked[g * count : (g + 1) * count]
+        rows = stacked[g * count : (g + 1) * count]
+        plain[:, g * cols : (g + 1) * cols] = rows.astype(BF16)
+        total = total + jnp.sum(rows * rows, axis=1, keepdims=True)
+    squares[...] = jnp.broadcast_to(total, squares.shape)
+
+
+def products_kernel(
+    order, plain, squares, tiles, own, first, second, third, sums, product
+):
+    count = plain.shape[0]
     rows = plain[...]
     pair = own.shape[0]
     half = pair // 2
     for steps, ref in enumerate((own, first, second, third)):
         section = order[steps]
         product[:, pl.ds(pl.multiple_of(section * pair, pair), pair)] = dot(rows, ref[...], 1)
-    values = rows.astype(F32)
-    squares = jnp.sum(values * values, axis=1, keepdims=True)
     lanes = lax.broadcasted_iota(jnp.int32, (count, pair), 1)
     low = []
     for s in range(3):
         high, rest = rounded(product[:, s * pair : (s + 1) * pair])
         sums[:, s * pair : (s + 1) * pair] = high
         low.append(rest)
-    high, rest = rounded(squares)
+    high, rest = rounded(squares[...])
     ends = jnp.where(lanes < half, product[:, 3 * pair :], high.astype(F32))
     sums[:, 3 * pair : 4 * pair] = jnp.where(lanes < half + half // 2, ends, rest).astype(BF16)
     tile_low = []
@@ -178,15 +196,16 @@
 
 
 def sections_kernel(
-    features, order, s0, s1, s2, s3, plain, f0, f1, f2, f3, out, stack, expand
+    features, order, s0, s1, s2, s3, plain_ref, f0, f1, f2, f3, out,
+    stack, expand, plain, made, expand_in, plain_in, sent
 ):
     pair = f0.shape[0]
     rank = pair // 2
     count, width = plain.shape
     cols = width // GROUPS
-    for steps, ref in enumerate((f0, f1, f2, f3)):
-        section = order[steps]
-        expand[pl.ds(pl.multiple_of(section * rank, rank), rank), :] = ref[rank:]
+    copies = ordered_copies(order, (f0, f1, f2, f3), rank, rank, expand, expand_in)
+    copies.append(pltpu.make_async_copy(plain_ref, plain, plain_in))
+    copies[-1].start()
     lanes = lax.broadcasted_iota(jnp.int32, (count, pair), 1)
 
     def summed(at):
@@ -229,16 +248,24 @@
             y[later] = y[later] + added[:, at * pair : (at + 1) * pair]
         ends = added[:, added.shape[1] - rank :]
         square = square + jnp.sum(value * (2.0 * y[s][:, rank:] + ends), axis=1, keepdims=True)
-    for g in range(GROUPS):
-        columns = slice(g * cols, (g + 1) * cols)
-        current = plain[:, columns].astype(F32)
-        for s in range(4):
-            current = current + dot(lowers[s], expand[s * rank : (s + 1) * rank, columns])
-            stack[s, g * count : (g + 1) * count] = current.astype(BF16)
     size = GROUPS * count
     moved = one_hot(block_places((1, size), 1, count), (size, size), 0)
+    for copy in copies:
+        copy.wait()
+    current = [plain[:, g * cols : (g + 1) * cols].astype(F32) for g in range(GROUPS)]
+    sends = []
     for s in range(4):
-        out[s * size : (s + 1) * size] = dot(moved, stack[s]).astype(BF16)
+        for g in range(GROUPS):
+            columns = slice(g * cols, (g + 1) * cols)
+            current[g] = current[g] + dot(lowers[s], expand[s * rank : (s + 1) * rank, columns])
+            stack[s, g * count : (g + 1) * count] = current[g].astype(BF16)
+        made[s] = dot(moved, stack[s]).astype(BF16)
+        sends.append(
+            pltpu.make_async_copy(made.at[s], out.at[pl.ds(s * size, size)], sent.at[s])
+        )
+        sends[-1].start()
+    for copy in sends:
+        copy.wait()
 
 
 def unpack_kernel(places, back, out):
@@ -310,32 +337,38 @@
     )
 
     section_order = (plane - jnp.arange(sections, dtype=jnp.int32)) % sections
-    section_order = jnp.concatenate([section_order, core.reshape(1)])
     tiles = call(
         factors_kernel,
         jax.ShapeDtypeStruct((6 * rank, pair), F32),
         scratch=[
             pltpu.VMEM((sections * pair, part), BF16),
             pltpu.VMEM((sections * rank, part), BF16),
+            pltpu.SemaphoreType.DMA((sections,)),
+            pltpu.SemaphoreType.DMA((sections,)),
         ],
-        specs=[SMEM] + [VMEM] * 4,
+        specs=[SMEM] + [ANY] * 4,
         flops=FACTOR_FLOPS,
         name="factors",
     )(section_order, *held)
     arrived, tiles = lax.optimization_barrier((arrived, tiles))
-
     theirs = lax.dynamic_slice(arrived, (0, (1 - core) * block, 0), (chips, block, cols))
     others = lax.ppermute(theirs, "core", [(0, 1), (1, 0)]).reshape(chips * block, cols)
-    sums, plain = call(
+    plain, squares = call(
+        plain_kernel,
+        (
+            jax.ShapeDtypeStruct((peers * depth, part), BF16),
+            jax.ShapeDtypeStruct((peers * depth, pair), F32),
+        ),
+        specs=[SMEM] + [VMEM] * 2,
+        name="plain",
+    )(core.reshape(1), arrived.reshape(size, cols), others)
+    sums = call(
         products_kernel,
-        (
-            jax.ShapeDtypeStruct((peers * depth, 10 * pair), BF16),
-            jax.ShapeDtypeStruct((peers * depth, part), BF16),
-        ),
+        jax.ShapeDtypeStruct((peers * depth, 10 * pair), BF16),
         scratch=[pltpu.VMEM((peers * depth, sections * pair), F32)],
         specs=[SMEM] + [VMEM] * 7,
         name="products",
-    )(section_order, arrived.reshape(size, cols), others, tiles, *held)
+    )(section_order, plain, squares, tiles, *held)
     all_sums = [sums] + [shifted(sums, "segment", steps) for steps in range(1, sections)]
 
     results = call(
@@ -344,8 +377,14 @@
         scratch=[
             pltpu.VMEM((sections, size, cols), BF16),
             pltpu.VMEM((sections * rank, part), BF16),
+            pltpu.VMEM((peers * depth, part), BF16),
+            pltpu.VMEM((sections, size, cols), BF16),
+            pltpu.SemaphoreType.DMA((sections,)),
+            pltpu.SemaphoreType.DMA,
+            pltpu.SemaphoreType.DMA((sections,)),
         ],
-        specs=[SMEM] + [VMEM] * 9,
+        specs=[SMEM] + [VMEM] * 4 + [ANY] * 5,
+        out_spec=ANY,
         name="sections",
     )(section_order, *all_sums, plain, *held)
 

time: 133 us -> 134 us (level)
  no operation moved by 1% of the time
where the time goes in v7:
time: 134 us; the launch traced here: 133 us
  waiting for transfers between devices  80.6 us (60%)
  starting transfers between devices  35.6 us (27%)
  Pallas kernels  15.5 us (12%)
    all_to_all x1, waiting for transfers between devices, local(): lax.all_to_all(results.reshape(sections * peers, block, cols), ('segment'...  54.7 us
    ppermute x6, waiting for transfers between devices, shifted(): lax.ppermute(value, axis, [(source, (source + steps) % count) for source...  23.8 us
    all_to_all x1, starting transfers between devices, local(): lax.all_to_all(packed.reshape(chips, 2 * block, cols), 'chip', split_axis...  11 us
    all_to_all x1, starting transfers between devices, local(): lax.all_to_all(results.reshape(sections * peers, block, cols), ('segment'...  10.3 us
    ppermute x6, starting transfers between devices, shifted(): lax.ppermute(value, axis, [(source, (source + steps) % count) for source...  8.88 us
    ppermute x1, starting transfers between devices, local(): lax.ppermute(theirs, 'core', [(0, 1), (1, 0)]).reshape(chips * block, cols)  5.47 us
    pallas_call x1, Pallas kernels, local(): call(lambda *refs: sections_kernel(width, *refs), jax.ShapeDtypeStruct((s...  5.13 us
    pallas_call x1, Pallas kernels, local(): call(quarters_kernel, tuple((jax.ShapeDtypeStruct((pair, part), BF16) for...  3 us
  transfers between devices with their start and end apart: 9, of which 6 were waited for; matrix products, arithmetic and copies ran while one was open for 0% of the time, Pallas kernels for 2%

profile of v7, /device:TPU:1, one launch (start us, length us, event | category | flops | bytes accessed | tf_op | source)
XLA Modules:
  0.0 133.3 jit_solution(15652971672900418755)
XLA Ops:
  0.0 3.0 %quarters.1 = (bf16[128,2048]{1,0:T(8,128)(2,1)}, bf16[128,2048]{1,0:T(8,128)(2,1)}, bf16[128,2048]{1,0:T(8,128)(2,1)}, bf16[128,2048]{1,0:T(8,128)(2,1)}) custom-call(s32[1]{0:T(128)} %bitcast.3.plane, bf16[64,8192]{1,0:T(8,128)(2,1)} %bitcast.17, f32[1,8192]{1,0:T(1,128)} %gain.1, bf16[64,8192]{1,0:T(8,128)(2,1)} %bitcast.18), custom_call_target="tpu_custom_call" | custom-call | bytes 4194304 | tf_op jit(solution)/shard_map/quarters/pallas_call | solution.py:298
  3.0 2.2 %collective-permute-start = (bf16[128,2048]{1,0:T(8,128)(2,1)}, bf16[128,2048]{1,0:T(8,128)(2,1)S(1)}, u32[]{:S(2)}, u32[]{:S(2)}) collective-permute-start(bf16[128,2048]{1,0:T(8,128)(2,1)} %get-tuple-element.14), channel_id=1, source_target_pairs={{0,64},{64,128},{128,192},{192,0},{1,65},{65,129},{129,193},{193,1... | collective-permute-start | bytes 1572872 | tf_op jit(solution)/shard_map/ppermute | solution.py:20
  5.2 2.6 %collective-permute-start.1 = (bf16[128,2048]{1,0:T(8,128)(2,1)}, bf16[128,2048]{1,0:T(8,128)(2,1)S(1)}, u32[]{:S(2)}, u32[]{:S(2)}) collective-permute-start(bf16[128,2048]{1,0:T(8,128)(2,1)} %get-tuple-element.15), channel_id=1, source_target_pairs={{0,128},{64,192},{128,0},{192,64},{1,129},{65,193},{129,1},{193,65... | collective-permute-start | bytes 1572872 | tf_op jit(solution)/shard_map/ppermute | solution.py:20
  7.9 1.1 collective-permute-start.2
  8.9 0.0 copy-done.3
  8.9 0.2 select_reduce_fusion
  9.1 0.1 broadcast_add_fusion
  9.2 0.1 add.58.places
  9.3 0.3 pack.1
  9.6 0.0 copy-start.2
  9.6 0.8 copy-done.2
  10.4 11.0 %all-to-all-start = ((bf16[32,16,512]{2,1,0:T(8,128)(2,1)}), bf16[32,16,512]{2,1,0:T(8,128)(2,1)S(1)}, u32[]{:S(2)}, u32[]{:S(2)}) async-start(bf16[32,16,512]{2,1,0:T(8,128)(2,1)} %bitcast.15), calls=%async_computation | async-start | bytes 1048576 | tf_op jit(solution)/shard_map/all_to_all | solution.py:335
  21.5 0.0 collective-permute-done.first.refs_7_
  21.5 9.1 %collective-permute-done.1.second.refs_8_ = bf16[128,2048]{1,0:T(8,128)(2,1)S(1)} collective-permute-done((bf16[128,2048]{1,0:T(8,128)(2,1)}, bf16[128,2048]{1,0:T(8,128)(2,1)S(1)}, u32[]{:S(2)}, u32[]{:S(2)}) %collective-permute-start.1) | collective-permute-done | bytes 524320 | tf_op jit(solution)/shard_map/ppermute | solution.py:20
  30.6 0.0 collective-permute-done.2.third.refs_9_
  30.6 2.7 %factors.1.tiles = f32[384,128]{1,0:T(8,128)S(1)} custom-call(s32[4]{0:T(128)S(1)} %and_select_fusion.order.refs_0_, bf16[128,2048]{1,0:T(8,128)(2,1)S(1)} %copy-done.1, bf16[128,2048]{1,0:T(8,128)(2,1)S(1)} %collective-permute-done.first.refs_7_, bf16[128,2048]{1,0:T(8,128)(2,1)S(1)} %collective-permute-done.1.second.refs_8_, ...), custom_call_target="tpu_custom_call" | custom-call | flops 40000000000 | bytes 4194304 | tf_op jit(solution)/shard_map/factors/pallas_call | solution.py:340
  33.4 1.0 all-to-all-done
  34.4 5.5 %collective-permute-start.3 = (bf16[32,8,512]{2,1,0:T(8,128)(2,1)S(1)}, bf16[32,8,512]{2,1,0:T(8,128)(2,1)S(1)}, u32[]{:S(2)}, u32[]{:S(2)}) collective-permute-start(bf16[32,8,512]{2,1,0:T(8,128)(2,1)S(1)} %constant_dynamic-slice_fusion.1), channel_id=1, source_target_pairs={{0,1},{1,0},{2,3},{3,2},{4,5},{5,4},{6,7},{7,6},{8,9},{9,8},{10,11... | collective-permute-start | bytes 786440 | tf_op jit(solution)/shard_map/ppermute | solution.py:355
  39.9 1.2 collective-permute-done.3
  41.0 0.8 plain.1
  41.8 1.9 %products.1.refs_1_ = bf16[128,1280]{1,0:T(8,128)(2,1)S(1)} custom-call(s32[4]{0:T(128)S(1)} %and_select_fusion.order.refs_0_, bf16[128,2048]{1,0:T(8,128)(2,1)S(1)} %get-tuple-element.18.plain.refs_5_, f32[128,128]{1,0:T(8,128)S(1)} %get-tuple-element.19.squares, f32[384,128]{1,0:T(8,128)S(1)} %factors.1.tiles, bf16[128,2048]{1,0:T(8,128)(2,1)S(1)} %copy-done.1, ...), custom_call_target="tpu_custom_call" | custom-call | bytes 4194304 | tf_op jit(solution)/shard_map/products/pallas_call | solution.py:365
  43.7 0.5 collective-permute-start.4
  44.2 0.7 collective-permute-start.5
  44.9 1.8 %collective-permute-start.6 = (bf16[128,1280]{1,0:T(8,128)(2,1)S(1)}, bf16[128,1280]{1,0:T(8,128)(2,1)S(1)}, u32[]{:S(2)}, u32[]{:S(2)}) collective-permute-start(bf16[128,1280]{1,0:T(8,128)(2,1)S(1)} %products.1.refs_1_), channel_id=1, source_target_pairs={{0,192},{64,0},{128,64},{192,128},{1,193},{65,1},{129,65},{193,129... | collective-permute-start | bytes 983048 | tf_op jit(solution)/shard_map/ppermute | solution.py:20
  46.7 14.3 %collective-permute-done.4.refs_2_ = bf16[128,1280]{1,0:T(8,128)(2,1)S(1)} collective-permute-done((bf16[128,1280]{1,0:T(8,128)(2,1)S(1)}, bf16[128,1280]{1,0:T(8,128)(2,1)S(1)}, u32[]{:S(2)}, u32[]{:S(2)}) %collective-permute-start.4) | collective-permute-done | bytes 327712 | tf_op jit(solution)/shard_map/ppermute | solution.py:20
  61.0 0.0 collective-permute-done.5.refs_3_
  61.0 0.3 collective-permute-done.6.refs_4_
  61.3 5.1 %sections.1 = bf16[2048,512]{1,0:T(8,128)(2,1)} custom-call(s32[4]{0:T(128)S(1)} %and_select_fusion.order.refs_0_, bf16[128,1280]{1,0:T(8,128)(2,1)S(1)} %products.1.refs_1_, bf16[128,1280]{1,0:T(8,128)(2,1)S(1)} %collective-permute-done.4.refs_2_, bf16[128,1280]{1,0:T(8,128)(2,1)S(1)} %collective-permute-done.5.refs_3_, ...), custom_call_target="tpu_custom_call" | custom-call | bytes 4194304 | tf_op jit(solution)/shard_map/sections/pallas_call | solution.py:374
  66.4 10.3 %all-to-all-start.1 = ((bf16[256,8,512]{2,1,0:T(8,128)(2,1)}), bf16[256,8,512]{2,1,0:T(8,128)(2,1)S(1)}, u32[]{:S(2)}, u32[]{:S(2)}) async-start(bf16[256,8,512]{2,1,0:T(8,128)(2,1)} %bitcast.9), calls=%async_computation.1 | async-start | bytes 4194304 | tf_op jit(solution)/shard_map/all_to_all | solution.py:391
  76.7 0.1 add.61.places
  76.8 54.7 %all-to-all-done.1 = bf16[256,8,512]{2,1,0:T(8,128)(2,1)S(1)} async-done(((bf16[256,8,512]{2,1,0:T(8,128)(2,1)}), bf16[256,8,512]{2,1,0:T(8,128)(2,1)S(1)}, u32[]{:S(2)}, u32[]{:S(2)}) %all-to-all-start.1) | async-done | bytes 2097184 | tf_op jit(solution)/shard_map/all_to_all | solution.py:391
  131.5 1.7 %unpack.1 = bf16[64,8192]{1,0:T(8,128)(2,1)} custom-call(s32[256,1]{1,0:T(8,128)S(1)} %add.61.places, bf16[4,512,512]{2,1,0:T(8,128)(2,1)S(1)} %bitcast.13), custom_call_target="tpu_custom_call" | custom-call | bytes 4194304 | tf_op jit(solution)/shard_map/unpack/pallas_call | solution.py:398
  (12 shorter events, 0.1 us)
Async XLA Ops:
  0.0 9.3 %copy-start = (bf16[64,8192]{1,0:T(8,128)(2,1)S(1)}, bf16[64,8192]{1,0:T(8,128)(2,1)}, u32[]{:S(2)}) copy-start(bf16[64,8192]{1,0:T(8,128)(2,1)} %param.6) | copy-start | bytes 3145732
  0.0 8.9 %copy-start.3 = (s32[64,1]{0,1:T(1,128)S(1)}, s32[64,1]{0,1:T(1,128)}, u32[]{:S(2)}) copy-start(s32[64,1]{0,1:T(1,128)} %param.7) | copy-start | bytes 772
  0.0 8.9 %copy-start.4 = (s32[64]{0:T(128)S(1)}, s32[64]{0:T(128)}, u32[]{:S(2)}) copy-start(s32[64]{0:T(128)} %param.8) | copy-start | bytes 772
  3.0 27.6 %copy-start.1 = (bf16[128,2048]{1,0:T(8,128)(2,1)S(1)}, bf16[128,2048]{1,0:T(8,128)(2,1)}, u32[]{:S(2)}) copy-start(bf16[128,2048]{1,0:T(8,128)(2,1)} %get-tuple-element.13.own.refs_6_) | copy-start | bytes 1572868
  3.0 18.4 %collective-permute-start = (bf16[128,2048]{1,0:T(8,128)(2,1)}, bf16[128,2048]{1,0:T(8,128)(2,1)S(1)}, u32[]{:S(2)}, u32[]{:S(2)}) collective-permute-start(bf16[128,2048]{1,0:T(8,128)(2,1)} %get-tuple-element.14), channel_id=1, source_target_pairs={{0,64},{64,128},{128,192},{192,0},{1,65},{65,129},{129,193},{193,1... | collective-permute-start | bytes 1572872 | tf_op jit(solution)/shard_map/ppermute | solution.py:20
  5.2 25.4 %collective-permute-start.1 = (bf16[128,2048]{1,0:T(8,128)(2,1)}, bf16[128,2048]{1,0:T(8,128)(2,1)S(1)}, u32[]{:S(2)}, u32[]{:S(2)}) collective-permute-start(bf16[128,2048]{1,0:T(8,128)(2,1)} %get-tuple-element.15), channel_id=1, source_target_pairs={{0,128},{64,192},{128,0},{192,64},{1,129},{65,193},{129,1},{193,65... | collective-permute-start | bytes 1572872 | tf_op jit(solution)/shard_map/ppermute | solution.py:20
  7.9 22.8 %collective-permute-start.2 = (bf16[128,2048]{1,0:T(8,128)(2,1)}, bf16[128,2048]{1,0:T(8,128)(2,1)}, u32[]{:S(2)}, u32[]{:S(2)}) collective-permute-start(bf16[128,2048]{1,0:T(8,128)(2,1)} %get-tuple-element.16), channel_id=1, source_target_pairs={{0,192},{64,0},{128,64},{192,128},{1,193},{65,1},{129,65},{193,129... | collective-permute-start | bytes 1572872 | tf_op jit(solution)/shard_map/ppermute | solution.py:20
  9.6 0.8 copy-start.2
  10.4 24.0 %all-to-all-start = ((bf16[32,16,512]{2,1,0:T(8,128)(2,1)}), bf16[32,16,512]{2,1,0:T(8,128)(2,1)S(1)}, u32[]{:S(2)}, u32[]{:S(2)}) async-start(bf16[32,16,512]{2,1,0:T(8,128)(2,1)} %bitcast.15), calls=%async_computation | async-start | bytes 1048576 | tf_op jit(solution)/shard_map/all_to_all | solution.py:335
  34.4 6.6 %collective-permute-start.3 = (bf16[32,8,512]{2,1,0:T(8,128)(2,1)S(1)}, bf16[32,8,512]{2,1,0:T(8,128)(2,1)S(1)}, u32[]{:S(2)}, u32[]{:S(2)}) collective-permute-start(bf16[32,8,512]{2,1,0:T(8,128)(2,1)S(1)} %constant_dynamic-slice_fusion.1), channel_id=1, source_target_pairs={{0,1},{1,0},{2,3},{3,2},{4,5},{5,4},{6,7},{7,6},{8,9},{9,8},{10,11... | collective-permute-start | bytes 786440 | tf_op jit(solution)/shard_map/ppermute | solution.py:355
  43.7 17.2 %collective-permute-start.4 = (bf16[128,1280]{1,0:T(8,128)(2,1)S(1)}, bf16[128,1280]{1,0:T(8,128)(2,1)S(1)}, u32[]{:S(2)}, u32[]{:S(2)}) collective-permute-start(bf16[128,1280]{1,0:T(8,128)(2,1)S(1)} %products.1.refs_1_), channel_id=1, source_target_pairs={{0,64},{64,128},{128,192},{192,0},{1,65},{65,129},{129,193},{193,1... | collective-permute-start | bytes 983048 | tf_op jit(solution)/shard_map/ppermute | solution.py:20
  44.2 16.8 %collective-permute-start.5 = (bf16[128,1280]{1,0:T(8,128)(2,1)S(1)}, bf16[128,1280]{1,0:T(8,128)(2,1)S(1)}, u32[]{:S(2)}, u32[]{:S(2)}) collective-permute-start(bf16[128,1280]{1,0:T(8,128)(2,1)S(1)} %products.1.refs_1_), channel_id=1, source_target_pairs={{0,128},{64,192},{128,0},{192,64},{1,129},{65,193},{129,1},{193,65... | collective-permute-start | bytes 983048 | tf_op jit(solution)/shard_map/ppermute | solution.py:20
  44.9 16.4 %collective-permute-start.6 = (bf16[128,1280]{1,0:T(8,128)(2,1)S(1)}, bf16[128,1280]{1,0:T(8,128)(2,1)S(1)}, u32[]{:S(2)}, u32[]{:S(2)}) collective-permute-start(bf16[128,1280]{1,0:T(8,128)(2,1)S(1)} %products.1.refs_1_), channel_id=1, source_target_pairs={{0,192},{64,0},{128,64},{192,128},{1,193},{65,1},{129,65},{193,129... | collective-permute-start | bytes 983048 | tf_op jit(solution)/shard_map/ppermute | solution.py:20
  66.4 65.1 %all-to-all-start.1 = ((bf16[256,8,512]{2,1,0:T(8,128)(2,1)}), bf16[256,8,512]{2,1,0:T(8,128)(2,1)S(1)}, u32[]{:S(2)}, u32[]{:S(2)}) async-start(bf16[256,8,512]{2,1,0:T(8,128)(2,1)} %bitcast.9), calls=%async_computation.1 | async-start | bytes 4194304 | tf_op jit(solution)/shard_map/all_to_all | solution.py:391

commit v8 on v6

--- a/solution.py
+++ b/solution.py
@@ -26,12 +26,12 @@
     )
 
 
-def call(kernel, outs, *, scratch=(), flops=0, specs=None, room=48, **options):
+def call(kernel, outs, *, scratch=(), flops=0, specs=None, out_spec=VMEM, room=48, **options):
     return pl.pallas_call(
         kernel,
         out_shape=outs,
         in_specs=specs,
-        out_specs=jax.tree.map(lambda _: VMEM, outs),
+        out_specs=jax.tree.map(lambda _: out_spec, outs),
         scratch_shapes=list(scratch),
         compiler_params=pltpu.CompilerParams(vmem_limit_bytes=room * 1024 * 1024),
         cost_estimate=pl.CostEstimate(flops=flops, bytes_accessed=4 << 20, transcendentals=0),
@@ -70,33 +70,32 @@
     out[...] = dot(chosen, stacked).astype(BF16)
 
 
-def quarters_kernel(
-    plane, shrink, gain, expand, q0, q1, q2, q3, taken, weights, gain_in, in_sem, put_sem
-):
+def quarters_kernel(shifts, plane, shrink, gain, expand, *refs):
+    number = len(shifts)
+    outs = refs[:number]
+    taken, weights, gain_in, in_sem, put_sem = refs[number:]
     rank = shrink.shape[0]
-    outs = (q0, q1, q2, q3)
-    part = q0.shape[1]
+    part = outs[0].shape[1]
     columns = [
-        pl.ds(pl.multiple_of(lax.rem(plane[0] + k, 4) * part, part), part) for k in range(4)
+        pl.ds(pl.multiple_of(lax.rem(plane[0] + k, 4) * part, part), part) for k in shifts
     ]
-    load = pltpu.make_async_copy(gain, weights, gain_in)
-    load.start()
-    ins = [
-        pltpu.make_async_copy(shrink.at[:, columns[k]], taken.at[k], in_sem.at[k])
-        for k in range(4)
-    ]
-    puts = [
-        pltpu.make_async_copy(
-            expand.at[:, columns[k]], outs[k].at[pl.ds(rank, rank)], put_sem.at[k]
+    loads, ins, puts = [], [], []
+    for at in range(number):
+        loads.append(
+            pltpu.make_async_copy(gain.at[:, columns[at]], weights.at[at], gain_in.at[at])
         )
-        for k in range(4)
-    ]
-    for copy in ins + puts:
+        ins.append(pltpu.make_async_copy(shrink.at[:, columns[at]], taken.at[at], in_sem.at[at]))
+        puts.append(
+            pltpu.make_async_copy(
+                expand.at[:, columns[at]], outs[at].at[pl.ds(rank, rank)], put_sem.at[at]
+            )
+        )
+    for copy in loads + ins + puts:
         copy.start()
-    load.wait()
-    for k in range(4):
-        ins[k].wait()
-        outs[k][:rank] = (taken[k].astype(F32) * weights[:, columns[k]]).astype(BF16)
+    for at in range(number):
+        loads[at].wait()
+        ins[at].wait()
+        outs[at][:rank] = (taken[at].astype(F32) * weights[at]).astype(BF16)
     for copy in puts:
         copy.wait()
 
@@ -178,7 +177,7 @@
 
 
 def sections_kernel(
-    features, order, s0, s1, s2, s3, plain, f0, f1, f2, f3, out, stack, expand
+    features, order, s0, s1, s2, s3, plain, f0, f1, f2, f3, out, stack, expand, made, sent
 ):
     pair = f0.shape[0]
     rank = pair // 2
@@ -229,16 +228,22 @@
             y[later] = y[later] + added[:, at * pair : (at + 1) * pair]
         ends = added[:, added.shape[1] - rank :]
         square = square + jnp.sum(value * (2.0 * y[s][:, rank:] + ends), axis=1, keepdims=True)
-    for g in range(GROUPS):
-        columns = slice(g * cols, (g + 1) * cols)
-        current = plain[:, columns].astype(F32)
-        for s in range(4):
-            current = current + dot(lowers[s], expand[s * rank : (s + 1) * rank, columns])
-            stack[s, g * count : (g + 1) * count] = current.astype(BF16)
     size = GROUPS * count
     moved = one_hot(block_places((1, size), 1, count), (size, size), 0)
+    current = [plain[:, g * cols : (g + 1) * cols].astype(F32) for g in range(GROUPS)]
+    sends = []
     for s in range(4):
-        out[s * size : (s + 1) * size] = dot(moved, stack[s]).astype(BF16)
+        for g in range(GROUPS):
+            columns = slice(g * cols, (g + 1) * cols)
+            current[g] = current[g] + dot(lowers[s], expand[s * rank : (s + 1) * rank, columns])
+            stack[s, g * count : (g + 1) * count] = current[g].astype(BF16)
+        made[s] = dot(moved, stack[s]).astype(BF16)
+        sends.append(
+            pltpu.make_async_copy(made.at[s], out.at[pl.ds(s * size, size)], sent.at[s])
+        )
+        sends[-1].start()
+    for copy in sends:
+        copy.wait()
 
 
 def unpack_kernel(places, back, out):
@@ -268,20 +273,25 @@
     block = depth * GROUPS
     size = peers * block
 
-    quarters = call(
-        quarters_kernel,
-        tuple(jax.ShapeDtypeStruct((pair, part), BF16) for _ in range(sections)),
-        scratch=[
-            pltpu.VMEM((sections, rank, part), BF16),
-            pltpu.VMEM((1, width), F32),
-            pltpu.SemaphoreType.DMA,
-            pltpu.SemaphoreType.DMA((sections,)),
-            pltpu.SemaphoreType.DMA((sections,)),
-        ],
-        specs=[SMEM, ANY, ANY, ANY],
-        room=60,
-        name="quarters",
-    )(plane.reshape(1), shrink_tiles[0, 0].T, gains, expand_tiles[0, 0])
+    def quarters_of(*shifts):
+        number = len(shifts)
+        return call(
+            lambda *refs: quarters_kernel(shifts, *refs),
+            tuple(jax.ShapeDtypeStruct((pair, part), BF16) for _ in shifts),
+            scratch=[
+                pltpu.VMEM((number, rank, part), BF16),
+                pltpu.VMEM((number, 1, part), F32),
+                pltpu.SemaphoreType.DMA((number,)),
+                pltpu.SemaphoreType.DMA((number,)),
+                pltpu.SemaphoreType.DMA((number,)),
+            ],
+            specs=[SMEM, ANY, ANY, ANY],
+            room=60,
+            name="quarters",
+        )(plane.reshape(1), shrink_tiles[0, 0].T, gains, expand_tiles[0, 0])
+
+    near, behind = quarters_of(1, 3)
+    far, kept = quarters_of(2, 0)
 
     adapter_ids = request_adapter[:, 0]
     catalog = jnp.arange(total, dtype=jnp.int32)
@@ -301,9 +311,8 @@
         specs=[VMEM, VMEM],
         name="pack",
     )(homes[None, :], mine)
-    held = [quarters[0]] + [
-        shifted(quarters[steps], "segment", steps) for steps in range(1, sections)
-    ]
+    sent = ((1, near), (2, far), (3, behind))
+    held = [kept] + [shifted(quarter, "segment", steps) for steps, quarter in sent]
 
     arrived = lax.all_to_all(
         packed.reshape(chips, 2 * block, cols), "chip", split_axis=0, concat_axis=0, tiled=True
@@ -344,8 +353,11 @@
         scratch=[
             pltpu.VMEM((sections, size, cols), BF16),
             pltpu.VMEM((sections * rank, part), BF16),
+            pltpu.VMEM((sections, size, cols), BF16),
+            pltpu.SemaphoreType.DMA((sections,)),
         ],
         specs=[SMEM] + [VMEM] * 9,
+        out_spec=ANY,
         name="sections",
     )(section_order, *all_sums, plain, *held)
 

time: 133 us -> 134 us (level)
    pallas_call x1 -> x2, Pallas kernels: 3 us -> 4.6 us  [quarters_of(): call(lambda *refs: quarters_kernel(shifts, *refs), tuple((jax.ShapeDtypeS...]
  transfers between devices with their start and end apart: 9 -> 9, of which waited for: 6 -> 7; matrix products, arithmetic and copies ran while one was open for 0% -> 0% of each run, Pallas kernels for 2% -> 3%
where the time goes in v8:
time: 134 us
  waiting for transfers between devices  81.2 us (61%)
  starting transfers between devices  35 us (26%)
  Pallas kernels  16.1 us (12%)
    all_to_all x1, waiting for transfers between devices, local(): lax.all_to_all(results.reshape(sections * peers, block, cols), ('segment'...  54.7 us
    ppermute x6, waiting for transfers between devices, shifted(): lax.ppermute(value, axis, [(source, (source + steps) % count) for source...  23.3 us
    all_to_all x1, starting transfers between devices, local(): lax.all_to_all(packed.reshape(chips, 2 * block, cols), 'chip', split_axis...  11 us
    all_to_all x1, starting transfers between devices, local(): lax.all_to_all(results.reshape(sections * peers, block, cols), ('segment'...  9.57 us
    ppermute x6, starting transfers between devices, shifted(): lax.ppermute(value, axis, [(source, (source + steps) % count) for source...  8.92 us
    ppermute x1, starting transfers between devices, local(): lax.ppermute(theirs, 'core', [(0, 1), (1, 0)]).reshape(chips * block, cols)  5.5 us
    pallas_call x1, Pallas kernels, local(): call(lambda *refs: sections_kernel(width, *refs), jax.ShapeDtypeStruct((s...  5 us
    pallas_call x2, Pallas kernels, quarters_of(): call(lambda *refs: quarters_kernel(shifts, *refs), tuple((jax.ShapeDtypeS...  4.6 us
  transfers between devices with their start and end apart: 9, of which 7 were waited for; matrix products, arithmetic and copies ran while one was open for 0% of the time, Pallas kernels for 3%

profile of v8, /device:TPU:1, one launch (start us, length us, event | category | flops | bytes accessed | tf_op | source)
XLA Modules:
  0.0 133.9 jit_solution(13543357948706280953)
XLA Ops:
  0.0 2.3 %quarters.3 = (bf16[128,2048]{1,0:T(8,128)(2,1)}, bf16[128,2048]{1,0:T(8,128)(2,1)}) custom-call(s32[1]{0:T(128)} %bitcast.3.refs_0_, bf16[64,8192]{1,0:T(8,128)(2,1)} %bitcast.17, f32[1,8192]{1,0:T(1,128)} %refs_2_.3, bf16[64,8192]{1,0:T(8,128)(2,1)} %bitcast.19), custom_call_target="tpu_custom_call" | custom-call | bytes 4194304 | tf_op jit(solution)/shard_map/quarters/pallas_call | solution.py:278
  2.3 2.2 %collective-permute-start = (bf16[128,2048]{1,0:T(8,128)(2,1)}, bf16[128,2048]{1,0:T(8,128)(2,1)S(1)}, u32[]{:S(2)}, u32[]{:S(2)}) collective-permute-start(bf16[128,2048]{1,0:T(8,128)(2,1)} %get-tuple-element.14), channel_id=1, source_target_pairs={{0,64},{64,128},{128,192},{192,0},{1,65},{65,129},{129,193},{193,1... | collective-permute-start | bytes 1572872 | tf_op jit(solution)/shard_map/ppermute | solution.py:20
  4.6 2.3 %quarters.2 = (bf16[128,2048]{1,0:T(8,128)(2,1)}, bf16[128,2048]{1,0:T(8,128)(2,1)}) custom-call(s32[1]{0:T(128)} %bitcast.3.refs_0_, bf16[64,8192]{1,0:T(8,128)(2,1)} %bitcast.18, f32[1,8192]{1,0:T(1,128)} %refs_2_.3, bf16[64,8192]{1,0:T(8,128)(2,1)} %bitcast.20), custom_call_target="tpu_custom_call" | custom-call | bytes 4194304 | tf_op jit(solution)/shard_map/quarters/pallas_call | solution.py:278
  6.8 2.7 %collective-permute-start.1 = (bf16[128,2048]{1,0:T(8,128)(2,1)}, bf16[128,2048]{1,0:T(8,128)(2,1)S(1)}, u32[]{:S(2)}, u32[]{:S(2)}) collective-permute-start(bf16[128,2048]{1,0:T(8,128)(2,1)} %get-tuple-element.15), channel_id=1, source_target_pairs={{0,128},{64,192},{128,0},{192,64},{1,129},{65,193},{129,1},{193,65... | collective-permute-start | bytes 1572872 | tf_op jit(solution)/shard_map/ppermute | solution.py:20
  9.5 1.1 collective-permute-start.2
  10.6 0.2 select_reduce_fusion
  10.8 0.1 broadcast_add_fusion
  10.9 0.1 add.58.places
  11.0 0.3 pack.1
  11.3 0.0 copy-start.2
  11.3 0.8 copy-done.2
  12.1 11.0 %all-to-all-start = ((bf16[32,16,512]{2,1,0:T(8,128)(2,1)}), bf16[32,16,512]{2,1,0:T(8,128)(2,1)S(1)}, u32[]{:S(2)}, u32[]{:S(2)}) async-start(bf16[32,16,512]{2,1,0:T(8,128)(2,1)} %bitcast.15), calls=%async_computation | async-start | bytes 1048576 | tf_op jit(solution)/shard_map/all_to_all | solution.py:317
  23.2 0.1 pad_add_fusion.order.refs_0_
  23.2 0.0 collective-permute-done.first.refs_7_
  23.2 6.7 %collective-permute-done.1.second.refs_8_ = bf16[128,2048]{1,0:T(8,128)(2,1)S(1)} collective-permute-done((bf16[128,2048]{1,0:T(8,128)(2,1)}, bf16[128,2048]{1,0:T(8,128)(2,1)S(1)}, u32[]{:S(2)}, u32[]{:S(2)}) %collective-permute-start.1) | collective-permute-done | bytes 524320 | tf_op jit(solution)/shard_map/ppermute | solution.py:20
  29.9 1.9 %collective-permute-done.2.third.refs_9_ = bf16[128,2048]{1,0:T(8,128)(2,1)} collective-permute-done((bf16[128,2048]{1,0:T(8,128)(2,1)}, bf16[128,2048]{1,0:T(8,128)(2,1)}, u32[]{:S(2)}, u32[]{:S(2)}) %collective-permute-start.2) | collective-permute-done | bytes 524320 | tf_op jit(solution)/shard_map/ppermute | solution.py:20
  31.9 2.0 %factors.1.tiles = f32[384,128]{1,0:T(8,128)S(1)} custom-call(s32[5]{0:T(128)S(1)} %pad_add_fusion.order.refs_0_, bf16[128,2048]{1,0:T(8,128)(2,1)S(1)} %copy-done.1, bf16[128,2048]{1,0:T(8,128)(2,1)S(1)} %collective-permute-done.first.refs_7_, bf16[128,2048]{1,0:T(8,128)(2,1)S(1)} %collective-permute-done.1.second.refs_8_, ...), custom_call_target="tpu_custom_call" | custom-call | flops 40000000000 | bytes 4194304 | tf_op jit(solution)/shard_map/factors/pallas_call | solution.py:323
  33.9 2.1 %all-to-all-done = bf16[32,16,512]{2,1,0:T(8,128)(2,1)S(1)} async-done(((bf16[32,16,512]{2,1,0:T(8,128)(2,1)}), bf16[32,16,512]{2,1,0:T(8,128)(2,1)S(1)}, u32[]{:S(2)}, u32[]{:S(2)}) %all-to-all-start) | async-done | bytes 524320 | tf_op jit(solution)/shard_map/all_to_all | solution.py:317
  36.1 5.5 %collective-permute-start.3 = (bf16[32,8,512]{2,1,0:T(8,128)(2,1)S(1)}, bf16[32,8,512]{2,1,0:T(8,128)(2,1)S(1)}, u32[]{:S(2)}, u32[]{:S(2)}) collective-permute-start(bf16[32,8,512]{2,1,0:T(8,128)(2,1)S(1)} %constant_dynamic-slice_fusion), channel_id=1, source_target_pairs={{0,1},{1,0},{2,3},{3,2},{4,5},{5,4},{6,7},{7,6},{8,9},{9,8},{10,11... | collective-permute-start | bytes 786440 | tf_op jit(solution)/shard_map/ppermute | solution.py:337
  41.6 1.2 collective-permute-done.3
  42.7 2.4 %products.1 = (bf16[128,1280]{1,0:T(8,128)(2,1)S(1)}, bf16[128,2048]{1,0:T(8,128)(2,1)S(1)}) custom-call(s32[5]{0:T(128)S(1)} %pad_add_fusion.order.refs_0_, bf16[512,512]{1,0:T(8,128)(2,1)S(1)} %bitcast.14, bf16[256,512]{1,0:T(8,128)(2,1)S(1)} %bitcast.16, f32[384,128]{1,0:T(8,128)S(1)} %factors.1.tiles, bf16[128,2048]{1,0:T(8,128)(2,1)S(1)} %copy-done.1, ...), custom_call_target="tpu_custom_call" | custom-call | bytes 4194304 | tf_op jit(solution)/shard_map/products/pallas_call | solution.py:338
  45.2 0.5 collective-permute-start.4
  45.6 0.7 collective-permute-start.5
  46.4 1.8 %collective-permute-start.6 = (bf16[128,1280]{1,0:T(8,128)(2,1)S(1)}, bf16[128,1280]{1,0:T(8,128)(2,1)S(1)}, u32[]{:S(2)}, u32[]{:S(2)}) collective-permute-start(bf16[128,1280]{1,0:T(8,128)(2,1)S(1)} %get-tuple-element.19.refs_1_), channel_id=1, source_target_pairs={{0,192},{64,0},{128,64},{192,128},{1,193},{65,1},{129,65},{193,129... | collective-permute-start | bytes 983048 | tf_op jit(solution)/shard_map/ppermute | solution.py:20
  48.1 14.3 %collective-permute-done.4.refs_2_ = bf16[128,1280]{1,0:T(8,128)(2,1)S(1)} collective-permute-done((bf16[128,1280]{1,0:T(8,128)(2,1)S(1)}, bf16[128,1280]{1,0:T(8,128)(2,1)S(1)}, u32[]{:S(2)}, u32[]{:S(2)}) %collective-permute-start.4) | collective-permute-done | bytes 327712 | tf_op jit(solution)/shard_map/ppermute | solution.py:20
  62.4 0.0 collective-permute-done.5.refs_3_
  62.4 0.3 collective-permute-done.6.refs_4_
  62.8 5.0 %sections.1 = bf16[2048,512]{1,0:T(8,128)(2,1)} custom-call(s32[5]{0:T(128)S(1)} %pad_add_fusion.order.refs_0_, bf16[128,1280]{1,0:T(8,128)(2,1)S(1)} %get-tuple-element.19.refs_1_, bf16[128,1280]{1,0:T(8,128)(2,1)S(1)} %collective-permute-done.4.refs_2_, bf16[128,1280]{1,0:T(8,128)(2,1)S(1)} %collective-permute-done.5.refs_3_, ...), custom_call_target="tpu_custom_call" | custom-call | bytes 4194304 | tf_op jit(solution)/shard_map/sections/pallas_call | solution.py:350
  67.8 9.6 %all-to-all-start.1 = ((bf16[256,8,512]{2,1,0:T(8,128)(2,1)}), bf16[256,8,512]{2,1,0:T(8,128)(2,1)S(1)}, u32[]{:S(2)}, u32[]{:S(2)}) async-start(bf16[256,8,512]{2,1,0:T(8,128)(2,1)} %bitcast.10), calls=%async_computation.1 | async-start | bytes 4194304 | tf_op jit(solution)/shard_map/all_to_all | solution.py:364
  77.4 0.1 add.61.places
  77.5 54.7 %all-to-all-done.1 = bf16[256,8,512]{2,1,0:T(8,128)(2,1)S(1)} async-done(((bf16[256,8,512]{2,1,0:T(8,128)(2,1)}), bf16[256,8,512]{2,1,0:T(8,128)(2,1)S(1)}, u32[]{:S(2)}, u32[]{:S(2)}) %all-to-all-start.1) | async-done | bytes 2097184 | tf_op jit(solution)/shard_map/all_to_all | solution.py:364
  132.2 1.7 %unpack.1 = bf16[64,8192]{1,0:T(8,128)(2,1)} custom-call(s32[256,1]{1,0:T(8,128)S(1)} %add.61.places, bf16[4,512,512]{2,1,0:T(8,128)(2,1)S(1)} %bitcast.13), custom_call_target="tpu_custom_call" | custom-call | bytes 4194304 | tf_op jit(solution)/shard_map/unpack/pallas_call | solution.py:371
  (13 shorter events, 0.1 us)
Async XLA Ops:
  0.0 11.0 %copy-start = (bf16[64,8192]{1,0:T(8,128)(2,1)S(1)}, bf16[64,8192]{1,0:T(8,128)(2,1)}, u32[]{:S(2)}) copy-start(bf16[64,8192]{1,0:T(8,128)(2,1)} %param.6) | copy-start | bytes 3145732
  0.0 10.6 %copy-start.3 = (s32[64,1]{0,1:T(1,128)S(1)}, s32[64,1]{0,1:T(1,128)}, u32[]{:S(2)}) copy-start(s32[64,1]{0,1:T(1,128)} %param.7) | copy-start | bytes 772
  0.0 10.6 %copy-start.4 = (s32[64]{0:T(128)S(1)}, s32[64]{0:T(128)}, u32[]{:S(2)}) copy-start(s32[64]{0:T(128)} %param.8) | copy-start | bytes 772
  2.3 20.9 %collective-permute-start = (bf16[128,2048]{1,0:T(8,128)(2,1)}, bf16[128,2048]{1,0:T(8,128)(2,1)S(1)}, u32[]{:S(2)}, u32[]{:S(2)}) collective-permute-start(bf16[128,2048]{1,0:T(8,128)(2,1)} %get-tuple-element.14), channel_id=1, source_target_pairs={{0,64},{64,128},{128,192},{192,0},{1,65},{65,129},{129,193},{193,1... | collective-permute-start | bytes 1572872 | tf_op jit(solution)/shard_map/ppermute | solution.py:20
  6.8 25.1 %copy-start.1 = (bf16[128,2048]{1,0:T(8,128)(2,1)S(1)}, bf16[128,2048]{1,0:T(8,128)(2,1)}, u32[]{:S(2)}) copy-start(bf16[128,2048]{1,0:T(8,128)(2,1)} %get-tuple-element.13.own.refs_6_) | copy-start | bytes 1572868
  6.8 23.1 %collective-permute-start.1 = (bf16[128,2048]{1,0:T(8,128)(2,1)}, bf16[128,2048]{1,0:T(8,128)(2,1)S(1)}, u32[]{:S(2)}, u32[]{:S(2)}) collective-permute-start(bf16[128,2048]{1,0:T(8,128)(2,1)} %get-tuple-element.15), channel_id=1, source_target_pairs={{0,128},{64,192},{128,0},{192,64},{1,129},{65,193},{129,1},{193,65... | collective-permute-start | bytes 1572872 | tf_op jit(solution)/shard_map/ppermute | solution.py:20
  9.5 22.3 %collective-permute-start.2 = (bf16[128,2048]{1,0:T(8,128)(2,1)}, bf16[128,2048]{1,0:T(8,128)(2,1)}, u32[]{:S(2)}, u32[]{:S(2)}) collective-permute-start(bf16[128,2048]{1,0:T(8,128)(2,1)} %get-tuple-element.16), channel_id=1, source_target_pairs={{0,192},{64,0},{128,64},{192,128},{1,193},{65,1},{129,65},{193,129... | collective-permute-start | bytes 1572872 | tf_op jit(solution)/shard_map/ppermute | solution.py:20
  11.3 0.8 copy-start.2
  12.1 24.0 %all-to-all-start = ((bf16[32,16,512]{2,1,0:T(8,128)(2,1)}), bf16[32,16,512]{2,1,0:T(8,128)(2,1)S(1)}, u32[]{:S(2)}, u32[]{:S(2)}) async-start(bf16[32,16,512]{2,1,0:T(8,128)(2,1)} %bitcast.15), calls=%async_computation | async-start | bytes 1048576 | tf_op jit(solution)/shard_map/all_to_all | solution.py:317
  36.1 6.7 %collective-permute-start.3 = (bf16[32,8,512]{2,1,0:T(8,128)(2,1)S(1)}, bf16[32,8,512]{2,1,0:T(8,128)(2,1)S(1)}, u32[]{:S(2)}, u32[]{:S(2)}) collective-permute-start(bf16[32,8,512]{2,1,0:T(8,128)(2,1)S(1)} %constant_dynamic-slice_fusion), channel_id=1, source_target_pairs={{0,1},{1,0},{2,3},{3,2},{4,5},{5,4},{6,7},{7,6},{8,9},{9,8},{10,11... | collective-permute-start | bytes 786440 | tf_op jit(solution)/shard_map/ppermute | solution.py:337
  45.2 17.2 %collective-permute-start.4 = (bf16[128,1280]{1,0:T(8,128)(2,1)S(1)}, bf16[128,1280]{1,0:T(8,128)(2,1)S(1)}, u32[]{:S(2)}, u32[]{:S(2)}) collective-permute-start(bf16[128,1280]{1,0:T(8,128)(2,1)S(1)} %get-tuple-element.19.refs_1_), channel_id=1, source_target_pairs={{0,64},{64,128},{128,192},{192,0},{1,65},{65,129},{129,193},{193,1... | collective-permute-start | bytes 983048 | tf_op jit(solution)/shard_map/ppermute | solution.py:20
  45.6 16.8 %collective-permute-start.5 = (bf16[128,1280]{1,0:T(8,128)(2,1)S(1)}, bf16[128,1280]{1,0:T(8,128)(2,1)S(1)}, u32[]{:S(2)}, u32[]{:S(2)}) collective-permute-start(bf16[128,1280]{1,0:T(8,128)(2,1)S(1)} %get-tuple-element.19.refs_1_), channel_id=1, source_target_pairs={{0,128},{64,192},{128,0},{192,64},{1,129},{65,193},{129,1},{193,65... | collective-permute-start | bytes 983048 | tf_op jit(solution)/shard_map/ppermute | solution.py:20
  46.4 16.4 %collective-permute-start.6 = (bf16[128,1280]{1,0:T(8,128)(2,1)S(1)}, bf16[128,1280]{1,0:T(8,128)(2,1)S(1)}, u32[]{:S(2)}, u32[]{:S(2)}) collective-permute-start(bf16[128,1280]{1,0:T(8,128)(2,1)S(1)} %get-tuple-element.19.refs_1_), channel_id=1, source_target_pairs={{0,192},{64,0},{128,64},{192,128},{1,193},{65,1},{129,65},{193,129... | collective-permute-start | bytes 983048 | tf_op jit(solution)/shard_map/ppermute | solution.py:20
  67.8 64.4 %all-to-all-start.1 = ((bf16[256,8,512]{2,1,0:T(8,128)(2,1)}), bf16[256,8,512]{2,1,0:T(8,128)(2,1)S(1)}, u32[]{:S(2)}, u32[]{:S(2)}) async-start(bf16[256,8,512]{2,1,0:T(8,128)(2,1)} %bitcast.10), calls=%async_computation.1 | async-start | bytes 4194304 | tf_op jit(solution)/shard_map/all_to_all | solution.py:364

commit v9 on v6

--- a/solution.py
+++ b/solution.py
@@ -26,12 +26,12 @@
     )
 
 
-def call(kernel, outs, *, scratch=(), flops=0, specs=None, room=48, **options):
+def call(kernel, outs, *, scratch=(), flops=0, specs=None, out_spec=VMEM, room=48, **options):
     return pl.pallas_call(
         kernel,
         out_shape=outs,
         in_specs=specs,
-        out_specs=jax.tree.map(lambda _: VMEM, outs),
+        out_specs=jax.tree.map(lambda _: out_spec, outs),
         scratch_shapes=list(scratch),
         compiler_params=pltpu.CompilerParams(vmem_limit_bytes=room * 1024 * 1024),
         cost_estimate=pl.CostEstimate(flops=flops, bytes_accessed=4 << 20, transcendentals=0),
@@ -155,30 +155,16 @@
     values = rows.astype(F32)
     squares = jnp.sum(values * values, axis=1, keepdims=True)
     lanes = lax.broadcasted_iota(jnp.int32, (count, pair), 1)
-    low = []
-    for s in range(3):
-        high, rest = rounded(product[:, s * pair : (s + 1) * pair])
-        sums[:, s * pair : (s + 1) * pair] = high
-        low.append(rest)
+    sums[:, : 3 * pair] = product[:, : 3 * pair].astype(BF16)
     high, rest = rounded(squares)
     ends = jnp.where(lanes < half, product[:, 3 * pair :], high.astype(F32))
     sums[:, 3 * pair : 4 * pair] = jnp.where(lanes < half + half // 2, ends, rest).astype(BF16)
-    tile_low = []
     for at in range(3):
-        high, rest = rounded(tiles[at * pair : (at + 1) * pair])
-        sums[:, (6 + at) * pair : (7 + at) * pair] = high
-        tile_low.append(rest)
-
-    def both(left, right):
-        return jnp.where(lanes < half, pltpu.roll(left, half, 1), right).astype(BF16)
-
-    sums[:, 4 * pair : 5 * pair] = both(low[1], low[0])
-    sums[:, 5 * pair : 6 * pair] = both(tile_low[2], low[2])
-    sums[:, 9 * pair :] = both(tile_low[1], tile_low[0])
+        sums[:, (4 + at) * pair : (5 + at) * pair] = tiles[at * pair : (at + 1) * pair].astype(BF16)
 
 
 def sections_kernel(
-    features, order, s0, s1, s2, s3, plain, f0, f1, f2, f3, out, stack, expand
+    features, order, s0, s1, s2, s3, plain, f0, f1, f2, f3, out, stack, expand, made, sent
 ):
     pair = f0.shape[0]
     rank = pair // 2
@@ -187,23 +173,15 @@
     for steps, ref in enumerate((f0, f1, f2, f3)):
         section = order[steps]
         expand[pl.ds(pl.multiple_of(section * rank, rank), rank), :] = ref[rank:]
-    lanes = lax.broadcasted_iota(jnp.int32, (count, pair), 1)
 
     def summed(at):
         columns = slice(at * pair, (at + 1) * pair)
         parts = [ref[:, columns].astype(F32) for ref in (s0, s1, s2, s3)]
         return (parts[0] + parts[1]) + (parts[2] + parts[3])
 
-    def right(value):
-        return jnp.where(lanes < rank, 0.0, value)
-
-    def left(value):
-        return right(pltpu.roll(value, rank, 1))
-
-    low, mixed, tile_low = summed(4), summed(5), summed(9)
-    y = [summed(0) + right(low), summed(1) + left(low), summed(2) + right(mixed), summed(3)]
+    y = [summed(s) for s in range(4)]
     square = y[3][:, rank : rank + 1] + y[3][:, pair - 1 :]
-    stacks = [summed(6) + right(tile_low), summed(7) + left(tile_low), summed(8) + left(mixed)]
+    stacks = [summed(4 + at) for at in range(3)]
 
     def thirds(place):
         at = (place % 2) * rank
@@ -229,16 +207,22 @@
             y[later] = y[later] + added[:, at * pair : (at + 1) * pair]
         ends = added[:, added.shape[1] - rank :]
         square = square + jnp.sum(value * (2.0 * y[s][:, rank:] + ends), axis=1, keepdims=True)
-    for g in range(GROUPS):
-        columns = slice(g * cols, (g + 1) * cols)
-        current = plain[:, columns].astype(F32)
-        for s in range(4):
-            current = current + dot(lowers[s], expand[s * rank : (s + 1) * rank, columns])
-            stack[s, g * count : (g + 1) * count] = current.astype(BF16)
     size = GROUPS * count
     moved = one_hot(block_places((1, size), 1, count), (size, size), 0)
+    current = [plain[:, g * cols : (g + 1) * cols].astype(F32) for g in range(GROUPS)]
+    sends = []
     for s in range(4):
-        out[s * size : (s + 1) * size] = dot(moved, stack[s]).astype(BF16)
+        for g in range(GROUPS):
+            columns = slice(g * cols, (g + 1) * cols)
+            current[g] = current[g] + dot(lowers[s], expand[s * rank : (s + 1) * rank, columns])
+            stack[s, g * count : (g + 1) * count] = current[g].astype(BF16)
+        made[s] = dot(moved, stack[s]).astype(BF16)
+        sends.append(
+            pltpu.make_async_copy(made.at[s], out.at[pl.ds(s * size, size)], sent.at[s])
+        )
+        sends[-1].start()
+    for copy in sends:
+        copy.wait()
 
 
 def unpack_kernel(places, back, out):
@@ -329,7 +313,7 @@
     sums, plain = call(
         products_kernel,
         (
-            jax.ShapeDtypeStruct((peers * depth, 10 * pair), BF16),
+            jax.ShapeDtypeStruct((peers * depth, 7 * pair), BF16),
             jax.ShapeDtypeStruct((peers * depth, part), BF16),
         ),
         scratch=[pltpu.VMEM((peers * depth, sections * pair), F32)],
@@ -344,8 +328,11 @@
         scratch=[
             pltpu.VMEM((sections, size, cols), BF16),
             pltpu.VMEM((sections * rank, part), BF16),
+            pltpu.VMEM((sections, size, cols), BF16),
+            pltpu.SemaphoreType.DMA((sections,)),
         ],
         specs=[SMEM] + [VMEM] * 9,
+        out_spec=ANY,
         name="sections",
     )(section_order, *all_sums, plain, *held)
 

time: 133 us -> 128 us (0.962)
  waiting for transfers between devices: 81.2 us -> 77 us
    ppermute x6, waiting for transfers between devices: 23.7 us -> 19.5 us  [shifted(): lax.ppermute(value, axis, [(source, (source + steps) % count) for source...]
where the time goes in v9:
time: 128 us
  waiting for transfers between devices  77 us (60%)
  starting transfers between devices  34.9 us (27%)
  Pallas kernels  14.4 us (11%)
    all_to_all x1, waiting for transfers between devices, local(): lax.all_to_all(results.reshape(sections * peers, block, cols), ('segment'...  54.7 us
    ppermute x6, waiting for transfers between devices, shifted(): lax.ppermute(value, axis, [(source, (source + steps) % count) for source...  19.5 us
    all_to_all x1, starting transfers between devices, local(): lax.all_to_all(packed.reshape(chips, 2 * block, cols), 'chip', split_axis...  11 us
    all_to_all x1, starting transfers between devices, local(): lax.all_to_all(results.reshape(sections * peers, block, cols), ('segment'...  9.59 us
    ppermute x6, starting transfers between devices, shifted(): lax.ppermute(value, axis, [(source, (source + steps) % count) for source...  8.86 us
    ppermute x1, starting transfers between devices, local(): lax.ppermute(theirs, 'core', [(0, 1), (1, 0)]).reshape(chips * block, cols)  5.47 us
    pallas_call x1, Pallas kernels, local(): call(lambda *refs: sections_kernel(width, *refs), jax.ShapeDtypeStruct((s...  4.97 us
    pallas_call x1, Pallas kernels, local(): call(quarters_kernel, tuple((jax.ShapeDtypeStruct((pair, part), BF16) for...  3 us
  transfers between devices with their start and end apart: 9, of which 6 were waited for; matrix products, arithmetic and copies ran while one was open for 0% of the time, Pallas kernels for 2%

profile of v9, /device:TPU:1, one launch (start us, length us, event | category | flops | bytes accessed | tf_op | source)
XLA Modules:
  0.0 127.9 jit_solution(9044320064483328269)
XLA Ops:
  0.0 0.0 copy-start
  0.0 3.0 %quarters.1 = (bf16[128,2048]{1,0:T(8,128)(2,1)}, bf16[128,2048]{1,0:T(8,128)(2,1)}, bf16[128,2048]{1,0:T(8,128)(2,1)}, bf16[128,2048]{1,0:T(8,128)(2,1)}) custom-call(s32[1]{0:T(128)} %bitcast.3.plane, bf16[64,8192]{1,0:T(8,128)(2,1)} %bitcast.17, f32[1,8192]{1,0:T(1,128)} %gain.1, bf16[64,8192]{1,0:T(8,128)(2,1)} %bitcast.18), custom_call_target="tpu_custom_call" | custom-call | bytes 4194304 | tf_op jit(solution)/shard_map/quarters/pallas_call | solution.py:255
  3.0 2.2 %collective-permute-start = (bf16[128,2048]{1,0:T(8,128)(2,1)}, bf16[128,2048]{1,0:T(8,128)(2,1)S(1)}, u32[]{:S(2)}, u32[]{:S(2)}) collective-permute-start(bf16[128,2048]{1,0:T(8,128)(2,1)} %get-tuple-element.14), channel_id=1, source_target_pairs={{0,64},{64,128},{128,192},{192,0},{1,65},{65,129},{129,193},{193,1... | collective-permute-start | bytes 1572872 | tf_op jit(solution)/shard_map/ppermute | solution.py:20
  5.2 2.6 %collective-permute-start.1 = (bf16[128,2048]{1,0:T(8,128)(2,1)}, bf16[128,2048]{1,0:T(8,128)(2,1)S(1)}, u32[]{:S(2)}, u32[]{:S(2)}) collective-permute-start(bf16[128,2048]{1,0:T(8,128)(2,1)} %get-tuple-element.15), channel_id=1, source_target_pairs={{0,128},{64,192},{128,0},{192,64},{1,129},{65,193},{129,1},{193,65... | collective-permute-start | bytes 1572872 | tf_op jit(solution)/shard_map/ppermute | solution.py:20
  7.9 1.1 collective-permute-start.2
  8.9 0.2 select_reduce_fusion
  9.1 0.1 broadcast_add_fusion
  9.2 0.1 add.58.places
  9.3 0.3 pack.1
  9.6 0.0 copy-start.2
  9.6 0.8 copy-done.2
  10.4 11.0 %all-to-all-start = ((bf16[32,16,512]{2,1,0:T(8,128)(2,1)}), bf16[32,16,512]{2,1,0:T(8,128)(2,1)S(1)}, u32[]{:S(2)}, u32[]{:S(2)}) async-start(bf16[32,16,512]{2,1,0:T(8,128)(2,1)} %bitcast.15), calls=%async_computation | async-start | bytes 1048576 | tf_op jit(solution)/shard_map/all_to_all | solution.py:292
  21.5 0.1 pad_add_fusion.order.refs_0_
  21.6 0.0 collective-permute-done.first.refs_7_
  21.6 9.1 %collective-permute-done.1.second.refs_8_ = bf16[128,2048]{1,0:T(8,128)(2,1)S(1)} collective-permute-done((bf16[128,2048]{1,0:T(8,128)(2,1)}, bf16[128,2048]{1,0:T(8,128)(2,1)S(1)}, u32[]{:S(2)}, u32[]{:S(2)}) %collective-permute-start.1) | collective-permute-done | bytes 524320 | tf_op jit(solution)/shard_map/ppermute | solution.py:20
  30.6 0.0 collective-permute-done.2.third.refs_9_
  30.6 2.0 %factors.1.tiles = f32[384,128]{1,0:T(8,128)S(1)} custom-call(s32[5]{0:T(128)S(1)} %pad_add_fusion.order.refs_0_, bf16[128,2048]{1,0:T(8,128)(2,1)S(1)} %copy-done.1, bf16[128,2048]{1,0:T(8,128)(2,1)S(1)} %collective-permute-done.first.refs_7_, bf16[128,2048]{1,0:T(8,128)(2,1)S(1)} %collective-permute-done.1.second.refs_8_, ...), custom_call_target="tpu_custom_call" | custom-call | flops 40000000000 | bytes 4194304 | tf_op jit(solution)/shard_map/factors/pallas_call | solution.py:298
  32.7 1.7 %all-to-all-done = bf16[32,16,512]{2,1,0:T(8,128)(2,1)S(1)} async-done(((bf16[32,16,512]{2,1,0:T(8,128)(2,1)}), bf16[32,16,512]{2,1,0:T(8,128)(2,1)S(1)}, u32[]{:S(2)}, u32[]{:S(2)}) %all-to-all-start) | async-done | bytes 524320 | tf_op jit(solution)/shard_map/all_to_all | solution.py:292
  34.4 5.5 %collective-permute-start.3 = (bf16[32,8,512]{2,1,0:T(8,128)(2,1)S(1)}, bf16[32,8,512]{2,1,0:T(8,128)(2,1)S(1)}, u32[]{:S(2)}, u32[]{:S(2)}) collective-permute-start(bf16[32,8,512]{2,1,0:T(8,128)(2,1)S(1)} %constant_dynamic-slice_fusion), channel_id=1, source_target_pairs={{0,1},{1,0},{2,3},{3,2},{4,5},{5,4},{6,7},{7,6},{8,9},{9,8},{10,11... | collective-permute-start | bytes 786440 | tf_op jit(solution)/shard_map/ppermute | solution.py:312
  39.9 1.2 collective-permute-done.3
  41.0 2.4 %products.1 = (bf16[128,896]{1,0:T(8,128)(2,1)S(1)}, bf16[128,2048]{1,0:T(8,128)(2,1)S(1)}) custom-call(s32[5]{0:T(128)S(1)} %pad_add_fusion.order.refs_0_, bf16[512,512]{1,0:T(8,128)(2,1)S(1)} %bitcast.14, bf16[256,512]{1,0:T(8,128)(2,1)S(1)} %bitcast.16, f32[384,128]{1,0:T(8,128)S(1)} %factors.1.tiles, bf16[128,2048]{1,0:T(8,128)(2,1)S(1)} %copy-done.1, ...), custom_call_target="tpu_custom_call" | custom-call | bytes 4194304 | tf_op jit(solution)/shard_map/products/pallas_call | solution.py:313
  43.4 0.5 collective-permute-start.4
  43.9 0.7 collective-permute-start.5
  44.6 1.8 %collective-permute-start.6 = (bf16[128,896]{1,0:T(8,128)(2,1)S(1)}, bf16[128,896]{1,0:T(8,128)(2,1)S(1)}, u32[]{:S(2)}, u32[]{:S(2)}) collective-permute-start(bf16[128,896]{1,0:T(8,128)(2,1)S(1)} %get-tuple-element.19.refs_1_), channel_id=1, source_target_pairs={{0,192},{64,0},{128,64},{192,128},{1,193},{65,1},{129,65},{193,129... | collective-permute-start | bytes 688136 | tf_op jit(solution)/shard_map/ppermute | solution.py:20
  46.4 10.1 %collective-permute-done.4.refs_2_ = bf16[128,896]{1,0:T(8,128)(2,1)S(1)} collective-permute-done((bf16[128,896]{1,0:T(8,128)(2,1)S(1)}, bf16[128,896]{1,0:T(8,128)(2,1)S(1)}, u32[]{:S(2)}, u32[]{:S(2)}) %collective-permute-start.4) | collective-permute-done | bytes 229408 | tf_op jit(solution)/shard_map/ppermute | solution.py:20
  56.5 0.0 collective-permute-done.5.refs_3_
  56.5 0.4 collective-permute-done.6.refs_4_
  56.8 5.0 %sections.1 = bf16[2048,512]{1,0:T(8,128)(2,1)} custom-call(s32[5]{0:T(128)S(1)} %pad_add_fusion.order.refs_0_, bf16[128,896]{1,0:T(8,128)(2,1)S(1)} %get-tuple-element.19.refs_1_, bf16[128,896]{1,0:T(8,128)(2,1)S(1)} %collective-permute-done.4.refs_2_, bf16[128,896]{1,0:T(8,128)(2,1)S(1)} %collective-permute-done.5.refs_3_, ...), custom_call_target="tpu_custom_call" | custom-call | bytes 4194304 | tf_op jit(solution)/shard_map/sections/pallas_call | solution.py:325
  61.8 9.6 %all-to-all-start.1 = ((bf16[256,8,512]{2,1,0:T(8,128)(2,1)}), bf16[256,8,512]{2,1,0:T(8,128)(2,1)S(1)}, u32[]{:S(2)}, u32[]{:S(2)}) async-start(bf16[256,8,512]{2,1,0:T(8,128)(2,1)} %bitcast.9), calls=%async_computation.1 | async-start | bytes 4194304 | tf_op jit(solution)/shard_map/all_to_all | solution.py:339
  71.4 0.1 add.61.places
  71.5 54.7 %all-to-all-done.1 = bf16[256,8,512]{2,1,0:T(8,128)(2,1)S(1)} async-done(((bf16[256,8,512]{2,1,0:T(8,128)(2,1)}), bf16[256,8,512]{2,1,0:T(8,128)(2,1)S(1)}, u32[]{:S(2)}, u32[]{:S(2)}) %all-to-all-start.1) | async-done | bytes 2097184 | tf_op jit(solution)/shard_map/all_to_all | solution.py:339
  126.2 1.7 %unpack.1 = bf16[64,8192]{1,0:T(8,128)(2,1)} custom-call(s32[256,1]{1,0:T(8,128)S(1)} %add.61.places, bf16[4,512,512]{2,1,0:T(8,128)(2,1)S(1)} %bitcast.13), custom_call_target="tpu_custom_call" | custom-call | bytes 4194304 | tf_op jit(solution)/shard_map/unpack/pallas_call | solution.py:346
  (12 shorter events, 0.1 us)
Async XLA Ops:
  0.0 9.3 %copy-start = (bf16[64,8192]{1,0:T(8,128)(2,1)S(1)}, bf16[64,8192]{1,0:T(8,128)(2,1)}, u32[]{:S(2)}) copy-start(bf16[64,8192]{1,0:T(8,128)(2,1)} %param.6) | copy-start | bytes 3145732
  0.0 8.9 %copy-start.3 = (s32[64,1]{0,1:T(1,128)S(1)}, s32[64,1]{0,1:T(1,128)}, u32[]{:S(2)}) copy-start(s32[64,1]{0,1:T(1,128)} %param.7) | copy-start | bytes 772
  0.0 8.9 %copy-start.4 = (s32[64]{0:T(128)S(1)}, s32[64]{0:T(128)}, u32[]{:S(2)}) copy-start(s32[64]{0:T(128)} %param.8) | copy-start | bytes 772
  3.0 27.6 %copy-start.1 = (bf16[128,2048]{1,0:T(8,128)(2,1)S(1)}, bf16[128,2048]{1,0:T(8,128)(2,1)}, u32[]{:S(2)}) copy-start(bf16[128,2048]{1,0:T(8,128)(2,1)} %get-tuple-element.13.own.refs_6_) | copy-start | bytes 1572868
  3.0 18.5 %collective-permute-start = (bf16[128,2048]{1,0:T(8,128)(2,1)}, bf16[128,2048]{1,0:T(8,128)(2,1)S(1)}, u32[]{:S(2)}, u32[]{:S(2)}) collective-permute-start(bf16[128,2048]{1,0:T(8,128)(2,1)} %get-tuple-element.14), channel_id=1, source_target_pairs={{0,64},{64,128},{128,192},{192,0},{1,65},{65,129},{129,193},{193,1... | collective-permute-start | bytes 1572872 | tf_op jit(solution)/shard_map/ppermute | solution.py:20
  5.2 25.4 %collective-permute-start.1 = (bf16[128,2048]{1,0:T(8,128)(2,1)}, bf16[128,2048]{1,0:T(8,128)(2,1)S(1)}, u32[]{:S(2)}, u32[]{:S(2)}) collective-permute-start(bf16[128,2048]{1,0:T(8,128)(2,1)} %get-tuple-element.15), channel_id=1, source_target_pairs={{0,128},{64,192},{128,0},{192,64},{1,129},{65,193},{129,1},{193,65... | collective-permute-start | bytes 1572872 | tf_op jit(solution)/shard_map/ppermute | solution.py:20
  7.9 22.8 %collective-permute-start.2 = (bf16[128,2048]{1,0:T(8,128)(2,1)}, bf16[128,2048]{1,0:T(8,128)(2,1)}, u32[]{:S(2)}, u32[]{:S(2)}) collective-permute-start(bf16[128,2048]{1,0:T(8,128)(2,1)} %get-tuple-element.16), channel_id=1, source_target_pairs={{0,192},{64,0},{128,64},{192,128},{1,193},{65,1},{129,65},{193,129... | collective-permute-start | bytes 1572872 | tf_op jit(solution)/shard_map/ppermute | solution.py:20
  9.6 0.8 copy-start.2
  10.4 24.0 %all-to-all-start = ((bf16[32,16,512]{2,1,0:T(8,128)(2,1)}), bf16[32,16,512]{2,1,0:T(8,128)(2,1)S(1)}, u32[]{:S(2)}, u32[]{:S(2)}) async-start(bf16[32,16,512]{2,1,0:T(8,128)(2,1)} %bitcast.15), calls=%async_computation | async-start | bytes 1048576 | tf_op jit(solution)/shard_map/all_to_all | solution.py:292
  34.4 6.6 %collective-permute-start.3 = (bf16[32,8,512]{2,1,0:T(8,128)(2,1)S(1)}, bf16[32,8,512]{2,1,0:T(8,128)(2,1)S(1)}, u32[]{:S(2)}, u32[]{:S(2)}) collective-permute-start(bf16[32,8,512]{2,1,0:T(8,128)(2,1)S(1)} %constant_dynamic-slice_fusion), channel_id=1, source_target_pairs={{0,1},{1,0},{2,3},{3,2},{4,5},{5,4},{6,7},{7,6},{8,9},{9,8},{10,11... | collective-permute-start | bytes 786440 | tf_op jit(solution)/shard_map/ppermute | solution.py:312
  43.4 13.0 %collective-permute-start.4 = (bf16[128,896]{1,0:T(8,128)(2,1)S(1)}, bf16[128,896]{1,0:T(8,128)(2,1)S(1)}, u32[]{:S(2)}, u32[]{:S(2)}) collective-permute-start(bf16[128,896]{1,0:T(8,128)(2,1)S(1)} %get-tuple-element.19.refs_1_), channel_id=1, source_target_pairs={{0,64},{64,128},{128,192},{192,0},{1,65},{65,129},{129,193},{193,1... | collective-permute-start | bytes 688136 | tf_op jit(solution)/shard_map/ppermute | solution.py:20
  43.9 12.6 %collective-permute-start.5 = (bf16[128,896]{1,0:T(8,128)(2,1)S(1)}, bf16[128,896]{1,0:T(8,128)(2,1)S(1)}, u32[]{:S(2)}, u32[]{:S(2)}) collective-permute-start(bf16[128,896]{1,0:T(8,128)(2,1)S(1)} %get-tuple-element.19.refs_1_), channel_id=1, source_target_pairs={{0,128},{64,192},{128,0},{192,64},{1,129},{65,193},{129,1},{193,65... | collective-permute-start | bytes 688136 | tf_op jit(solution)/shard_map/ppermute | solution.py:20
  44.6 12.2 %collective-permute-start.6 = (bf16[128,896]{1,0:T(8,128)(2,1)S(1)}, bf16[128,896]{1,0:T(8,128)(2,1)S(1)}, u32[]{:S(2)}, u32[]{:S(2)}) collective-permute-start(bf16[128,896]{1,0:T(8,128)(2,1)S(1)} %get-tuple-element.19.refs_1_), channel_id=1, source_target_pairs={{0,192},{64,0},{128,64},{192,128},{1,193},{65,1},{129,65},{193,129... | collective-permute-start | bytes 688136 | tf_op jit(solution)/shard_map/ppermute | solution.py:20
  61.8 64.4 %all-to-all-start.1 = ((bf16[256,8,512]{2,1,0:T(8,128)(2,1)}), bf16[256,8,512]{2,1,0:T(8,128)(2,1)S(1)}, u32[]{:S(2)}, u32[]{:S(2)}) async-start(bf16[256,8,512]{2,1,0:T(8,128)(2,1)} %bitcast.9), calls=%async_computation.1 | async-start | bytes 4194304 | tf_op jit(solution)/shard_map/all_to_all | solution.py:339

commit v10 on v9

--- a/solution.py
+++ b/solution.py
@@ -71,7 +71,7 @@
 
 
 def quarters_kernel(
-    plane, shrink, gain, expand, q0, q1, q2, q3, taken, weights, gain_in, in_sem, put_sem
+    plane, shrink, gain, expand, q0, q1, q2, q3, made, weights, gain_in, in_sem, put_sem, out_sem
 ):
     rank = shrink.shape[0]
     outs = (q0, q1, q2, q3)
@@ -81,24 +81,26 @@
     ]
     load = pltpu.make_async_copy(gain, weights, gain_in)
     load.start()
-    ins = [
-        pltpu.make_async_copy(shrink.at[:, columns[k]], taken.at[k], in_sem.at[k])
-        for k in range(4)
-    ]
-    puts = [
-        pltpu.make_async_copy(
-            expand.at[:, columns[k]], outs[k].at[pl.ds(rank, rank)], put_sem.at[k]
+    order = (2, 1, 3, 0)
+    ins, puts, sends = {}, {}, {}
+    for k in order:
+        ins[k] = pltpu.make_async_copy(
+            shrink.at[:, columns[k]], made.at[k, pl.ds(0, rank)], in_sem.at[k]
         )
-        for k in range(4)
-    ]
-    for copy in ins + puts:
-        copy.start()
+        puts[k] = pltpu.make_async_copy(
+            expand.at[:, columns[k]], made.at[k, pl.ds(rank, rank)], put_sem.at[k]
+        )
+        ins[k].start()
+        puts[k].start()
     load.wait()
-    for k in range(4):
+    for k in order:
         ins[k].wait()
-        outs[k][:rank] = (taken[k].astype(F32) * weights[:, columns[k]]).astype(BF16)
-    for copy in puts:
-        copy.wait()
+        made[k, :rank] = (made[k, :rank].astype(F32) * weights[:, columns[k]]).astype(BF16)
+        puts[k].wait()
+        sends[k] = pltpu.make_async_copy(made.at[k], outs[k], out_sem.at[k])
+        sends[k].start()
+    for k in order:
+        sends[k].wait()
 
 
 def factors_kernel(order, own, first, second, third, tiles, every, expand):
@@ -191,30 +193,28 @@
         return jnp.concatenate([high, middle, rest.astype(BF16)], axis=0)
 
     uses = (((1, 0), (2, 1), (3, 3)), ((2, 2), (3, 4)), ((3, 5),))
-    lowers = []
-    for s in range(4):
-        scale = lax.rsqrt(jnp.maximum(square, 0.0) / features + 1e-05)
-        lower = (y[s][:, :rank] * scale).astype(BF16)
-        lowers.append(lower)
-        if s == 3:
-            break
-        added = dot(
-            jnp.concatenate([lower] * 3, axis=1),
-            jnp.concatenate([thirds(place) for _, place in uses[s]], axis=1),
-        )
-        value = lower.astype(F32)
-        for at, (later, _) in enumerate(uses[s]):
-            y[later] = y[later] + added[:, at * pair : (at + 1) * pair]
-        ends = added[:, added.shape[1] - rank :]
-        square = square + jnp.sum(value * (2.0 * y[s][:, rank:] + ends), axis=1, keepdims=True)
     size = GROUPS * count
     moved = one_hot(block_places((1, size), 1, count), (size, size), 0)
     current = [plain[:, g * cols : (g + 1) * cols].astype(F32) for g in range(GROUPS)]
     sends = []
     for s in range(4):
+        scale = lax.rsqrt(jnp.maximum(square, 0.0) / features + 1e-05)
+        lower = (y[s][:, :rank] * scale).astype(BF16)
+        if s < 3:
+            added = dot(
+                jnp.concatenate([lower] * 3, axis=1),
+                jnp.concatenate([thirds(place) for _, place in uses[s]], axis=1),
+            )
+            value = lower.astype(F32)
+            for at, (later, _) in enumerate(uses[s]):
+                y[later] = y[later] + added[:, at * pair : (at + 1) * pair]
+            ends = added[:, added.shape[1] - rank :]
+            square = square + jnp.sum(
+                value * (2.0 * y[s][:, rank:] + ends), axis=1, keepdims=True
+            )
         for g in range(GROUPS):
             columns = slice(g * cols, (g + 1) * cols)
-            current[g] = current[g] + dot(lowers[s], expand[s * rank : (s + 1) * rank, columns])
+            current[g] = current[g] + dot(lower, expand[s * rank : (s + 1) * rank, columns])
             stack[s, g * count : (g + 1) * count] = current[g].astype(BF16)
         made[s] = dot(moved, stack[s]).astype(BF16)
         sends.append(
@@ -225,15 +225,24 @@
         copy.wait()
 
 
-def unpack_kernel(places, back, out):
+def unpack_kernel(places, back, out, made, sent):
     size, cols = places.shape[0], back.shape[2]
     count = size // GROUPS
+    part = GROUPS * cols
     chosen = one_hot(places[...], (size, back.shape[1]), 1)
+    sends = []
     for plane in range(back.shape[0]):
         found = dot(chosen, back[plane]).astype(BF16)
         for g in range(GROUPS):
-            start = (plane * GROUPS + g) * cols
-            out[:, start : start + cols] = found[g * count : (g + 1) * count]
+            made[plane, :, g * cols : (g + 1) * cols] = found[g * count : (g + 1) * count]
+        sends.append(
+            pltpu.make_async_copy(
+                made.at[plane], out.at[:, pl.ds(plane * part, part)], sent.at[plane]
+            )
+        )
+        sends[-1].start()
+    for copy in sends:
+        copy.wait()
 
 
 def local(hidden_in, request_adapter, home_slot, gains, shrink_tiles, expand_tiles):
@@ -256,12 +265,14 @@
         quarters_kernel,
         tuple(jax.ShapeDtypeStruct((pair, part), BF16) for _ in range(sections)),
         scratch=[
-            pltpu.VMEM((sections, rank, part), BF16),
+            pltpu.VMEM((sections, pair, part), BF16),
             pltpu.VMEM((1, width), F32),
             pltpu.SemaphoreType.DMA,
             pltpu.SemaphoreType.DMA((sections,)),
             pltpu.SemaphoreType.DMA((sections,)),
+            pltpu.SemaphoreType.DMA((sections,)),
         ],
+        out_spec=ANY,
         specs=[SMEM, ANY, ANY, ANY],
         room=60,
         name="quarters",
@@ -346,7 +357,12 @@
     rows = call(
         unpack_kernel,
         jax.ShapeDtypeStruct((count, width), BF16),
+        scratch=[
+            pltpu.VMEM((sections, count, part), BF16),
+            pltpu.SemaphoreType.DMA((sections,)),
+        ],
         specs=[VMEM, VMEM],
+        out_spec=ANY,
         name="unpack",
     )(homes[:, None], back.reshape(sections, size, cols))
     return rows[None]

time: 128 us -> 127 us (level)
  no operation moved by 1% of the time
where the time goes in v10:
time: 127 us
  waiting for transfers between devices  77 us (61%)
  starting transfers between devices  35 us (28%)
  Pallas kernels  13.3 us (10%)
    all_to_all x1, waiting for transfers between devices, local(): lax.all_to_all(results.reshape(sections * peers, block, cols), ('segment'...  54.7 us
    ppermute x6, waiting for transfers between devices, shifted(): lax.ppermute(value, axis, [(source, (source + steps) % count) for source...  19.5 us
    all_to_all x1, starting transfers between devices, local(): lax.all_to_all(packed.reshape(chips, 2 * block, cols), 'chip', split_axis...  11 us
    all_to_all x1, starting transfers between devices, local(): lax.all_to_all(results.reshape(sections * peers, block, cols), ('segment'...  9.62 us
    ppermute x6, starting transfers between devices, shifted(): lax.ppermute(value, axis, [(source, (source + steps) % count) for source...  8.85 us
    ppermute x1, starting transfers between devices, local(): lax.ppermute(theirs, 'core', [(0, 1), (1, 0)]).reshape(chips * block, cols)  5.5 us
    pallas_call x1, Pallas kernels, local(): call(lambda *refs: sections_kernel(width, *refs), jax.ShapeDtypeStruct((s...  4.24 us
    pallas_call x1, Pallas kernels, local(): call(quarters_kernel, tuple((jax.ShapeDtypeStruct((pair, part), BF16) for...  2.87 us
  transfers between devices with their start and end apart: 9, of which 6 were waited for; matrix products, arithmetic and copies ran while one was open for 0% of the time, Pallas kernels for 2%

profile of v10, /device:TPU:1, one launch (start us, length us, event | category | flops | bytes accessed | tf_op | source)
XLA Modules:
  0.0 126.8 jit_solution(16574263855416281472)
XLA Ops:
  0.0 0.0 copy-start
  0.0 2.9 %quarters.1 = (bf16[128,2048]{1,0:T(8,128)(2,1)}, bf16[128,2048]{1,0:T(8,128)(2,1)}, bf16[128,2048]{1,0:T(8,128)(2,1)}, bf16[128,2048]{1,0:T(8,128)(2,1)}) custom-call(s32[1]{0:T(128)} %bitcast.3.plane, bf16[64,8192]{1,0:T(8,128)(2,1)} %bitcast.17, f32[1,8192]{1,0:T(1,128)} %gain.1, bf16[64,8192]{1,0:T(8,128)(2,1)} %bitcast.18), custom_call_target="tpu_custom_call" | custom-call | bytes 4194304 | tf_op jit(solution)/shard_map/quarters/pallas_call | solution.py:264
  2.9 2.2 %collective-permute-start = (bf16[128,2048]{1,0:T(8,128)(2,1)}, bf16[128,2048]{1,0:T(8,128)(2,1)S(1)}, u32[]{:S(2)}, u32[]{:S(2)}) collective-permute-start(bf16[128,2048]{1,0:T(8,128)(2,1)} %get-tuple-element.14), channel_id=1, source_target_pairs={{0,64},{64,128},{128,192},{192,0},{1,65},{65,129},{129,193},{193,1... | collective-permute-start | bytes 1572872 | tf_op jit(solution)/shard_map/ppermute | solution.py:20
  5.1 2.6 %collective-permute-start.1 = (bf16[128,2048]{1,0:T(8,128)(2,1)}, bf16[128,2048]{1,0:T(8,128)(2,1)S(1)}, u32[]{:S(2)}, u32[]{:S(2)}) collective-permute-start(bf16[128,2048]{1,0:T(8,128)(2,1)} %get-tuple-element.15), channel_id=1, source_target_pairs={{0,128},{64,192},{128,0},{192,64},{1,129},{65,193},{129,1},{193,65... | collective-permute-start | bytes 1572872 | tf_op jit(solution)/shard_map/ppermute | solution.py:20
  7.7 1.1 collective-permute-start.2
  8.8 0.2 select_reduce_fusion
  9.0 0.1 broadcast_add_fusion
  9.1 0.1 add.58.places
  9.2 0.3 pack.1
  9.5 0.0 copy-start.2
  9.5 0.8 copy-done.2
  10.3 11.0 %all-to-all-start = ((bf16[32,16,512]{2,1,0:T(8,128)(2,1)}), bf16[32,16,512]{2,1,0:T(8,128)(2,1)S(1)}, u32[]{:S(2)}, u32[]{:S(2)}) async-start(bf16[32,16,512]{2,1,0:T(8,128)(2,1)} %bitcast.15), calls=%async_computation | async-start | bytes 1048576 | tf_op jit(solution)/shard_map/all_to_all | solution.py:303
  21.3 0.1 pad_add_fusion.order.refs_0_
  21.4 0.0 collective-permute-done.first.refs_7_
  21.4 9.1 %collective-permute-done.1.second.refs_8_ = bf16[128,2048]{1,0:T(8,128)(2,1)S(1)} collective-permute-done((bf16[128,2048]{1,0:T(8,128)(2,1)}, bf16[128,2048]{1,0:T(8,128)(2,1)S(1)}, u32[]{:S(2)}, u32[]{:S(2)}) %collective-permute-start.1) | collective-permute-done | bytes 524320 | tf_op jit(solution)/shard_map/ppermute | solution.py:20
  30.5 0.0 collective-permute-done.2.third.refs_9_
  30.5 2.0 %factors.1.tiles = f32[384,128]{1,0:T(8,128)S(1)} custom-call(s32[5]{0:T(128)S(1)} %pad_add_fusion.order.refs_0_, bf16[128,2048]{1,0:T(8,128)(2,1)S(1)} %copy-done.1, bf16[128,2048]{1,0:T(8,128)(2,1)S(1)} %collective-permute-done.first.refs_7_, bf16[128,2048]{1,0:T(8,128)(2,1)S(1)} %collective-permute-done.1.second.refs_8_, ...), custom_call_target="tpu_custom_call" | custom-call | flops 40000000000 | bytes 4194304 | tf_op jit(solution)/shard_map/factors/pallas_call | solution.py:309
  32.6 1.7 %all-to-all-done = bf16[32,16,512]{2,1,0:T(8,128)(2,1)S(1)} async-done(((bf16[32,16,512]{2,1,0:T(8,128)(2,1)}), bf16[32,16,512]{2,1,0:T(8,128)(2,1)S(1)}, u32[]{:S(2)}, u32[]{:S(2)}) %all-to-all-start) | async-done | bytes 524320 | tf_op jit(solution)/shard_map/all_to_all | solution.py:303
  34.3 5.5 %collective-permute-start.3 = (bf16[32,8,512]{2,1,0:T(8,128)(2,1)S(1)}, bf16[32,8,512]{2,1,0:T(8,128)(2,1)S(1)}, u32[]{:S(2)}, u32[]{:S(2)}) collective-permute-start(bf16[32,8,512]{2,1,0:T(8,128)(2,1)S(1)} %constant_dynamic-slice_fusion), channel_id=1, source_target_pairs={{0,1},{1,0},{2,3},{3,2},{4,5},{5,4},{6,7},{7,6},{8,9},{9,8},{10,11... | collective-permute-start | bytes 786440 | tf_op jit(solution)/shard_map/ppermute | solution.py:323
  39.8 1.2 collective-permute-done.3
  40.9 2.4 %products.1 = (bf16[128,896]{1,0:T(8,128)(2,1)S(1)}, bf16[128,2048]{1,0:T(8,128)(2,1)S(1)}) custom-call(s32[5]{0:T(128)S(1)} %pad_add_fusion.order.refs_0_, bf16[512,512]{1,0:T(8,128)(2,1)S(1)} %bitcast.14, bf16[256,512]{1,0:T(8,128)(2,1)S(1)} %bitcast.16, f32[384,128]{1,0:T(8,128)S(1)} %factors.1.tiles, bf16[128,2048]{1,0:T(8,128)(2,1)S(1)} %copy-done.1, ...), custom_call_target="tpu_custom_call" | custom-call | bytes 4194304 | tf_op jit(solution)/shard_map/products/pallas_call | solution.py:324
  43.3 0.5 collective-permute-start.4
  43.8 0.7 collective-permute-start.5
  44.5 1.8 %collective-permute-start.6 = (bf16[128,896]{1,0:T(8,128)(2,1)S(1)}, bf16[128,896]{1,0:T(8,128)(2,1)S(1)}, u32[]{:S(2)}, u32[]{:S(2)}) collective-permute-start(bf16[128,896]{1,0:T(8,128)(2,1)S(1)} %get-tuple-element.19.refs_1_), channel_id=1, source_target_pairs={{0,192},{64,0},{128,64},{192,128},{1,193},{65,1},{129,65},{193,129... | collective-permute-start | bytes 688136 | tf_op jit(solution)/shard_map/ppermute | solution.py:20
  46.3 10.0 %collective-permute-done.4.refs_2_ = bf16[128,896]{1,0:T(8,128)(2,1)S(1)} collective-permute-done((bf16[128,896]{1,0:T(8,128)(2,1)S(1)}, bf16[128,896]{1,0:T(8,128)(2,1)S(1)}, u32[]{:S(2)}, u32[]{:S(2)}) %collective-permute-start.4) | collective-permute-done | bytes 229408 | tf_op jit(solution)/shard_map/ppermute | solution.py:20
  56.3 0.0 collective-permute-done.5.refs_3_
  56.3 0.3 collective-permute-done.6.refs_4_
  56.6 4.2 %sections.1 = bf16[2048,512]{1,0:T(8,128)(2,1)} custom-call(s32[5]{0:T(128)S(1)} %pad_add_fusion.order.refs_0_, bf16[128,896]{1,0:T(8,128)(2,1)S(1)} %get-tuple-element.19.refs_1_, bf16[128,896]{1,0:T(8,128)(2,1)S(1)} %collective-permute-done.4.refs_2_, bf16[128,896]{1,0:T(8,128)(2,1)S(1)} %collective-permute-done.5.refs_3_, ...), custom_call_target="tpu_custom_call" | custom-call | bytes 4194304 | tf_op jit(solution)/shard_map/sections/pallas_call | solution.py:336
  60.9 9.6 %all-to-all-start.1 = ((bf16[256,8,512]{2,1,0:T(8,128)(2,1)}), bf16[256,8,512]{2,1,0:T(8,128)(2,1)S(1)}, u32[]{:S(2)}, u32[]{:S(2)}) async-start(bf16[256,8,512]{2,1,0:T(8,128)(2,1)} %bitcast.9), calls=%async_computation.1 | async-start | bytes 4194304 | tf_op jit(solution)/shard_map/all_to_all | solution.py:350
  70.5 0.1 add.61.places
  70.7 54.7 %all-to-all-done.1 = bf16[256,8,512]{2,1,0:T(8,128)(2,1)S(1)} async-done(((bf16[256,8,512]{2,1,0:T(8,128)(2,1)}), bf16[256,8,512]{2,1,0:T(8,128)(2,1)S(1)}, u32[]{:S(2)}, u32[]{:S(2)}) %all-to-all-start.1) | async-done | bytes 2097184 | tf_op jit(solution)/shard_map/all_to_all | solution.py:350
  125.3 1.5 %unpack.1 = bf16[64,8192]{1,0:T(8,128)(2,1)} custom-call(s32[256,1]{1,0:T(8,128)S(1)} %add.61.places, bf16[4,512,512]{2,1,0:T(8,128)(2,1)S(1)} %bitcast.13), custom_call_target="tpu_custom_call" | custom-call | bytes 4194304 | tf_op jit(solution)/shard_map/unpack/pallas_call | solution.py:357
  (12 shorter events, 0.1 us)
Async XLA Ops:
  0.0 9.2 %copy-start = (bf16[64,8192]{1,0:T(8,128)(2,1)S(1)}, bf16[64,8192]{1,0:T(8,128)(2,1)}, u32[]{:S(2)}) copy-start(bf16[64,8192]{1,0:T(8,128)(2,1)} %param.6) | copy-start | bytes 3145732
  0.0 8.8 %copy-start.3 = (s32[64,1]{0,1:T(1,128)S(1)}, s32[64,1]{0,1:T(1,128)}, u32[]{:S(2)}) copy-start(s32[64,1]{0,1:T(1,128)} %param.7) | copy-start | bytes 772
  0.0 8.8 %copy-start.4 = (s32[64]{0:T(128)S(1)}, s32[64]{0:T(128)}, u32[]{:S(2)}) copy-start(s32[64]{0:T(128)} %param.8) | copy-start | bytes 772
  2.9 27.6 %copy-start.1 = (bf16[128,2048]{1,0:T(8,128)(2,1)S(1)}, bf16[128,2048]{1,0:T(8,128)(2,1)}, u32[]{:S(2)}) copy-start(bf16[128,2048]{1,0:T(8,128)(2,1)} %get-tuple-element.13.own.refs_6_) | copy-start | bytes 1572868
  2.9 18.5 %collective-permute-start = (bf16[128,2048]{1,0:T(8,128)(2,1)}, bf16[128,2048]{1,0:T(8,128)(2,1)S(1)}, u32[]{:S(2)}, u32[]{:S(2)}) collective-permute-start(bf16[128,2048]{1,0:T(8,128)(2,1)} %get-tuple-element.14), channel_id=1, source_target_pairs={{0,64},{64,128},{128,192},{192,0},{1,65},{65,129},{129,193},{193,1... | collective-permute-start | bytes 1572872 | tf_op jit(solution)/shard_map/ppermute | solution.py:20
  5.1 25.4 %collective-permute-start.1 = (bf16[128,2048]{1,0:T(8,128)(2,1)}, bf16[128,2048]{1,0:T(8,128)(2,1)S(1)}, u32[]{:S(2)}, u32[]{:S(2)}) collective-permute-start(bf16[128,2048]{1,0:T(8,128)(2,1)} %get-tuple-element.15), channel_id=1, source_target_pairs={{0,128},{64,192},{128,0},{192,64},{1,129},{65,193},{129,1},{193,65... | collective-permute-start | bytes 1572872 | tf_op jit(solution)/shard_map/ppermute | solution.py:20
  7.7 22.8 %collective-permute-start.2 = (bf16[128,2048]{1,0:T(8,128)(2,1)}, bf16[128,2048]{1,0:T(8,128)(2,1)}, u32[]{:S(2)}, u32[]{:S(2)}) collective-permute-start(bf16[128,2048]{1,0:T(8,128)(2,1)} %get-tuple-element.16), channel_id=1, source_target_pairs={{0,192},{64,0},{128,64},{192,128},{1,193},{65,1},{129,65},{193,129... | collective-permute-start | bytes 1572872 | tf_op jit(solution)/shard_map/ppermute | solution.py:20
  9.5 0.8 copy-start.2
  10.3 24.0 %all-to-all-start = ((bf16[32,16,512]{2,1,0:T(8,128)(2,1)}), bf16[32,16,512]{2,1,0:T(8,128)(2,1)S(1)}, u32[]{:S(2)}, u32[]{:S(2)}) async-start(bf16[32,16,512]{2,1,0:T(8,128)(2,1)} %bitcast.15), calls=%async_computation | async-start | bytes 1048576 | tf_op jit(solution)/shard_map/all_to_all | solution.py:303
  34.3 6.7 %collective-permute-start.3 = (bf16[32,8,512]{2,1,0:T(8,128)(2,1)S(1)}, bf16[32,8,512]{2,1,0:T(8,128)(2,1)S(1)}, u32[]{:S(2)}, u32[]{:S(2)}) collective-permute-start(bf16[32,8,512]{2,1,0:T(8,128)(2,1)S(1)} %constant_dynamic-slice_fusion), channel_id=1, source_target_pairs={{0,1},{1,0},{2,3},{3,2},{4,5},{5,4},{6,7},{7,6},{8,9},{9,8},{10,11... | collective-permute-start | bytes 786440 | tf_op jit(solution)/shard_map/ppermute | solution.py:323
  43.3 13.0 %collective-permute-start.4 = (bf16[128,896]{1,0:T(8,128)(2,1)S(1)}, bf16[128,896]{1,0:T(8,128)(2,1)S(1)}, u32[]{:S(2)}, u32[]{:S(2)}) collective-permute-start(bf16[128,896]{1,0:T(8,128)(2,1)S(1)} %get-tuple-element.19.refs_1_), channel_id=1, source_target_pairs={{0,64},{64,128},{128,192},{192,0},{1,65},{65,129},{129,193},{193,1... | collective-permute-start | bytes 688136 | tf_op jit(solution)/shard_map/ppermute | solution.py:20
  43.8 12.5 %collective-permute-start.5 = (bf16[128,896]{1,0:T(8,128)(2,1)S(1)}, bf16[128,896]{1,0:T(8,128)(2,1)S(1)}, u32[]{:S(2)}, u32[]{:S(2)}) collective-permute-start(bf16[128,896]{1,0:T(8,128)(2,1)S(1)} %get-tuple-element.19.refs_1_), channel_id=1, source_target_pairs={{0,128},{64,192},{128,0},{192,64},{1,129},{65,193},{129,1},{193,65... | collective-permute-start | bytes 688136 | tf_op jit(solution)/shard_map/ppermute | solution.py:20
  44.5 12.1 %collective-permute-start.6 = (bf16[128,896]{1,0:T(8,128)(2,1)S(1)}, bf16[128,896]{1,0:T(8,128)(2,1)S(1)}, u32[]{:S(2)}, u32[]{:S(2)}) collective-permute-start(bf16[128,896]{1,0:T(8,128)(2,1)S(1)} %get-tuple-element.19.refs_1_), channel_id=1, source_target_pairs={{0,192},{64,0},{128,64},{192,128},{1,193},{65,1},{129,65},{193,129... | collective-permute-start | bytes 688136 | tf_op jit(solution)/shard_map/ppermute | solution.py:20
  60.9 64.5 %all-to-all-start.1 = ((bf16[256,8,512]{2,1,0:T(8,128)(2,1)}), bf16[256,8,512]{2,1,0:T(8,128)(2,1)S(1)}, u32[]{:S(2)}, u32[]{:S(2)}) async-start(bf16[256,8,512]{2,1,0:T(8,128)(2,1)} %bitcast.9), calls=%async_computation.1 | async-start | bytes 4194304 | tf_op jit(solution)/shard_map/all_to_all | solution.py:350

commit v11 on v10

--- a/solution.py
+++ b/solution.py
@@ -7,7 +7,7 @@
 from jax.sharding import PartitionSpec as P
 
 GROUPS = 4
-FACTOR_FLOPS = 40_000_000_000
+LANDED_FLOPS = 40_000_000_000
 VMEM = pl.BlockSpec(memory_space=pltpu.VMEM)
 ANY = pl.BlockSpec(memory_space=pl.ANY)
 SMEM = pl.BlockSpec(memory_space=pltpu.SMEM)
@@ -131,13 +131,19 @@
     return high, value - high.astype(F32)
 
 
+def landed_kernel(first, second, third, token):
+    del first, second, third
+    token[...] = jnp.zeros_like(token)
+
+
 def products_kernel(
-    order, blocks, others, tiles, own, first, second, third, sums, plain, product
+    order, token, blocks, others, tiles, own, first, second, third, sums, plain, product
 ):
     count, width = plain.shape
     cols = width // GROUPS
     size = count * GROUPS
     core = order[4]
+    del token
     stacked = dot(
         one_hot(block_places((size, 1), 0, count, core, True), (size, blocks.shape[0]), 1),
         blocks[...],
@@ -314,10 +320,16 @@
             pltpu.VMEM((sections * rank, part), BF16),
         ],
         specs=[SMEM] + [VMEM] * 4,
-        flops=FACTOR_FLOPS,
         name="factors",
     )(section_order, *held)
-    arrived, tiles = lax.optimization_barrier((arrived, tiles))
+    token = call(
+        landed_kernel,
+        jax.ShapeDtypeStruct((8, 128), F32),
+        specs=[ANY] * 3,
+        flops=LANDED_FLOPS,
+        name="landed",
+    )(*held[1:])
+    arrived, token = lax.optimization_barrier((arrived, token))
 
     theirs = lax.dynamic_slice(arrived, (0, (1 - core) * block, 0), (chips, block, cols))
     others = lax.ppermute(theirs, "core", [(0, 1), (1, 0)]).reshape(chips * block, cols)
@@ -328,9 +340,9 @@
             jax.ShapeDtypeStruct((peers * depth, part), BF16),
         ),
         scratch=[pltpu.VMEM((peers * depth, sections * pair), F32)],
-        specs=[SMEM] + [VMEM] * 7,
+        specs=[SMEM, ANY] + [VMEM] * 7,
         name="products",
-    )(section_order, arrived.reshape(size, cols), others, tiles, *held)
+    )(section_order, token, arrived.reshape(size, cols), others, tiles, *held)
     all_sums = [sums] + [shifted(sums, "segment", steps) for steps in range(1, sections)]
 
     results = call(

time: 127 us -> 127 us (level)
  waiting for transfers between devices: 77 us -> 78.3 us
    all_to_all x1, waiting for transfers between devices: 1.68 us -> 3.76 us  [local(): lax.all_to_all(packed.reshape(chips, 2 * block, cols), 'chip', split_axis...]
  transfers between devices with their start and end apart: 9 -> 9, of which waited for: 6 -> 5; matrix products, arithmetic and copies ran while one was open for 0% -> 0% of each run, Pallas kernels for 2% -> 2%
where the time goes in v11:
time: 127 us
  waiting for transfers between devices  78.3 us (62%)
  starting transfers between devices  33.9 us (27%)
  Pallas kernels  13.1 us (10%)
    all_to_all x1, waiting for transfers between devices, local(): lax.all_to_all(results.reshape(sections * peers, block, cols), ('segment'...  54.7 us
    ppermute x6, waiting for transfers between devices, shifted(): lax.ppermute(value, axis, [(source, (source + steps) % count) for source...  19.9 us
    all_to_all x1, starting transfers between devices, local(): lax.all_to_all(packed.reshape(chips, 2 * block, cols), 'chip', split_axis...  11.2 us
    ppermute x6, starting transfers between devices, shifted(): lax.ppermute(value, axis, [(source, (source + steps) % count) for source...  8.87 us
    all_to_all x1, starting transfers between devices, local(): lax.all_to_all(results.reshape(sections * peers, block, cols), ('segment'...  8.43 us
    ppermute x1, starting transfers between devices, local(): lax.ppermute(theirs, 'core', [(0, 1), (1, 0)]).reshape(chips * block, cols)  5.47 us
    all_to_all x1, waiting for transfers between devices, local(): lax.all_to_all(packed.reshape(chips, 2 * block, cols), 'chip', split_axis...  3.76 us
    pallas_call x1, Pallas kernels, local(): call(lambda *refs: sections_kernel(width, *refs), jax.ShapeDtypeStruct((s...  3.72 us
  transfers between devices with their start and end apart: 9, of which 5 were waited for; matrix products, arithmetic and copies ran while one was open for 0% of the time, Pallas kernels for 2%

profile of v11, /device:TPU:1, one launch (start us, length us, event | category | flops | bytes accessed | tf_op | source)
XLA Modules:
  0.0 127.0 jit_solution(15354744931386029709)
XLA Ops:
  0.0 0.0 copy-start
  0.0 2.9 %quarters.1 = (bf16[128,2048]{1,0:T(8,128)(2,1)}, bf16[128,2048]{1,0:T(8,128)(2,1)}, bf16[128,2048]{1,0:T(8,128)(2,1)}, bf16[128,2048]{1,0:T(8,128)(2,1)}) custom-call(s32[1]{0:T(128)} %bitcast.3.plane, bf16[64,8192]{1,0:T(8,128)(2,1)} %bitcast.15, f32[1,8192]{1,0:T(1,128)} %gain.1, bf16[64,8192]{1,0:T(8,128)(2,1)} %bitcast.16), custom_call_target="tpu_custom_call" | custom-call | bytes 4194304 | tf_op jit(solution)/shard_map/quarters/pallas_call | solution.py:270
  2.9 2.2 %collective-permute-start = (bf16[128,2048]{1,0:T(8,128)(2,1)}, bf16[128,2048]{1,0:T(8,128)(2,1)S(1)}, u32[]{:S(2)}, u32[]{:S(2)}) collective-permute-start(bf16[128,2048]{1,0:T(8,128)(2,1)} %get-tuple-element.13), channel_id=1, source_target_pairs={{0,64},{64,128},{128,192},{192,0},{1,65},{65,129},{129,193},{193,1... | collective-permute-start | bytes 1572872 | tf_op jit(solution)/shard_map/ppermute | solution.py:20
  5.1 2.6 %collective-permute-start.1 = (bf16[128,2048]{1,0:T(8,128)(2,1)}, bf16[128,2048]{1,0:T(8,128)(2,1)S(1)}, u32[]{:S(2)}, u32[]{:S(2)}) collective-permute-start(bf16[128,2048]{1,0:T(8,128)(2,1)} %get-tuple-element.14), channel_id=1, source_target_pairs={{0,128},{64,192},{128,0},{192,64},{1,129},{65,193},{129,1},{193,65... | collective-permute-start | bytes 1572872 | tf_op jit(solution)/shard_map/ppermute | solution.py:20
  7.7 1.1 collective-permute-start.2
  8.8 0.2 select_reduce_fusion
  9.0 0.1 broadcast_add_fusion
  9.1 0.1 add.58.places
  9.2 1.1 pack.1
  10.3 11.2 %all-to-all-start = ((bf16[32,16,512]{2,1,0:T(8,128)(2,1)}), bf16[32,16,512]{2,1,0:T(8,128)(2,1)}, u32[]{:S(2)}, u32[]{:S(2)}) async-start(bf16[32,16,512]{2,1,0:T(8,128)(2,1)} %bitcast.2), calls=%async_computation | async-start | bytes 1048576 | tf_op jit(solution)/shard_map/all_to_all | solution.py:309
  21.5 0.0 copy-start.1
  21.5 0.0 collective-permute-done.first.refs_7_
  21.5 9.1 %collective-permute-done.1.second.refs_8_ = bf16[128,2048]{1,0:T(8,128)(2,1)S(1)} collective-permute-done((bf16[128,2048]{1,0:T(8,128)(2,1)}, bf16[128,2048]{1,0:T(8,128)(2,1)S(1)}, u32[]{:S(2)}, u32[]{:S(2)}) %collective-permute-start.1) | collective-permute-done | bytes 524320 | tf_op jit(solution)/shard_map/ppermute | solution.py:20
  30.6 0.0 collective-permute-done.2.third.refs_9_
  30.6 3.8 %all-to-all-done = bf16[32,16,512]{2,1,0:T(8,128)(2,1)} async-done(((bf16[32,16,512]{2,1,0:T(8,128)(2,1)}), bf16[32,16,512]{2,1,0:T(8,128)(2,1)}, u32[]{:S(2)}, u32[]{:S(2)}) %all-to-all-start) | async-done | bytes 524320 | tf_op jit(solution)/shard_map/all_to_all | solution.py:309
  34.4 1.0 constant_dynamic-slice_fusion
  35.3 5.5 %collective-permute-start.3 = (bf16[32,8,512]{2,1,0:T(8,128)(2,1)S(1)}, bf16[32,8,512]{2,1,0:T(8,128)(2,1)S(1)}, u32[]{:S(2)}, u32[]{:S(2)}) collective-permute-start(bf16[32,8,512]{2,1,0:T(8,128)(2,1)S(1)} %constant_dynamic-slice_fusion), channel_id=1, source_target_pairs={{0,1},{1,0},{2,3},{3,2},{4,5},{5,4},{6,7},{7,6},{8,9},{9,8},{10,11... | collective-permute-start | bytes 786440 | tf_op jit(solution)/shard_map/ppermute | solution.py:335
  40.8 0.1 pad_add_fusion.order.refs_0_
  40.9 1.5 %factors.1.tiles = f32[384,128]{1,0:T(8,128)S(1)} custom-call(s32[5]{0:T(128)S(1)} %pad_add_fusion.order.refs_0_, bf16[128,2048]{1,0:T(8,128)(2,1)S(1)} %copy-done.1, bf16[128,2048]{1,0:T(8,128)(2,1)S(1)} %collective-permute-done.first.refs_7_, bf16[128,2048]{1,0:T(8,128)(2,1)S(1)} %collective-permute-done.1.second.refs_8_, ...), custom_call_target="tpu_custom_call" | custom-call | bytes 4194304 | tf_op jit(solution)/shard_map/factors/pallas_call | solution.py:315
  42.4 0.0 collective-permute-done.3
  42.4 2.4 %products.1 = (bf16[128,896]{1,0:T(8,128)(2,1)S(1)}, bf16[128,2048]{1,0:T(8,128)(2,1)S(1)}) custom-call(s32[5]{0:T(128)S(1)} %pad_add_fusion.order.refs_0_, f32[8,128]{1,0:T(8,128)S(1)} %landed.1.token, bf16[512,512]{1,0:T(8,128)(2,1)} %bitcast.7.blocks, bf16[256,512]{1,0:T(8,128)(2,1)S(1)} %bitcast.14, f32[384,128]{1,0:T(8,128)S(1)} %factors.1.tiles, ...), custom_call_target="tpu_custom_call" | custom-call | bytes 4194304 | tf_op jit(solution)/shard_map/products/pallas_call | solution.py:336
  44.8 0.5 collective-permute-start.4
  45.3 0.7 collective-permute-start.5
  46.1 1.7 %collective-permute-start.6 = (bf16[128,896]{1,0:T(8,128)(2,1)S(1)}, bf16[128,896]{1,0:T(8,128)(2,1)S(1)}, u32[]{:S(2)}, u32[]{:S(2)}) collective-permute-start(bf16[128,896]{1,0:T(8,128)(2,1)S(1)} %get-tuple-element.19.refs_1_), channel_id=1, source_target_pairs={{0,192},{64,0},{128,64},{192,128},{1,193},{65,1},{129,65},{193,129... | collective-permute-start | bytes 688136 | tf_op jit(solution)/shard_map/ppermute | solution.py:20
  47.8 10.4 %collective-permute-done.4.refs_2_ = bf16[128,896]{1,0:T(8,128)(2,1)S(1)} collective-permute-done((bf16[128,896]{1,0:T(8,128)(2,1)S(1)}, bf16[128,896]{1,0:T(8,128)(2,1)S(1)}, u32[]{:S(2)}, u32[]{:S(2)}) %collective-permute-start.4) | collective-permute-done | bytes 229408 | tf_op jit(solution)/shard_map/ppermute | solution.py:20
  58.3 0.0 collective-permute-done.5.refs_3_
  58.3 0.3 collective-permute-done.6.refs_4_
  58.6 3.7 %sections.1 = bf16[2048,512]{1,0:T(8,128)(2,1)} custom-call(s32[5]{0:T(128)S(1)} %pad_add_fusion.order.refs_0_, bf16[128,896]{1,0:T(8,128)(2,1)S(1)} %get-tuple-element.19.refs_1_, bf16[128,896]{1,0:T(8,128)(2,1)S(1)} %collective-permute-done.4.refs_2_, bf16[128,896]{1,0:T(8,128)(2,1)S(1)} %collective-permute-done.5.refs_3_, ...), custom_call_target="tpu_custom_call" | custom-call | bytes 4194304 | tf_op jit(solution)/shard_map/sections/pallas_call | solution.py:348
  62.3 8.4 %all-to-all-start.1 = ((bf16[256,8,512]{2,1,0:T(8,128)(2,1)}), bf16[256,8,512]{2,1,0:T(8,128)(2,1)S(1)}, u32[]{:S(2)}, u32[]{:S(2)}) async-start(bf16[256,8,512]{2,1,0:T(8,128)(2,1)} %bitcast.9), calls=%async_computation.1 | async-start | bytes 4194304 | tf_op jit(solution)/shard_map/all_to_all | solution.py:362
  70.7 0.1 add.61.places
  70.9 54.7 %all-to-all-done.1 = bf16[256,8,512]{2,1,0:T(8,128)(2,1)S(1)} async-done(((bf16[256,8,512]{2,1,0:T(8,128)(2,1)}), bf16[256,8,512]{2,1,0:T(8,128)(2,1)S(1)}, u32[]{:S(2)}, u32[]{:S(2)}) %all-to-all-start.1) | async-done | bytes 2097184 | tf_op jit(solution)/shard_map/all_to_all | solution.py:362
  125.5 1.5 %unpack.1 = bf16[64,8192]{1,0:T(8,128)(2,1)} custom-call(s32[256,1]{1,0:T(8,128)S(1)} %add.61.places, bf16[4,512,512]{2,1,0:T(8,128)(2,1)S(1)} %bitcast.13), custom_call_target="tpu_custom_call" | custom-call | bytes 4194304 | tf_op jit(solution)/shard_map/unpack/pallas_call | solution.py:369
  (11 shorter events, 0.1 us)
Async XLA Ops:
  0.0 9.2 %copy-start = (bf16[64,8192]{1,0:T(8,128)(2,1)S(1)}, bf16[64,8192]{1,0:T(8,128)(2,1)}, u32[]{:S(2)}) copy-start(bf16[64,8192]{1,0:T(8,128)(2,1)} %param.6) | copy-start | bytes 3145732
  0.0 8.8 %copy-start.2 = (s32[64,1]{0,1:T(1,128)S(1)}, s32[64,1]{0,1:T(1,128)}, u32[]{:S(2)}) copy-start(s32[64,1]{0,1:T(1,128)} %param.7) | copy-start | bytes 772
  0.0 8.8 %copy-start.3 = (s32[64]{0:T(128)S(1)}, s32[64]{0:T(128)}, u32[]{:S(2)}) copy-start(s32[64]{0:T(128)} %param.8) | copy-start | bytes 772
  2.9 18.6 %collective-permute-start = (bf16[128,2048]{1,0:T(8,128)(2,1)}, bf16[128,2048]{1,0:T(8,128)(2,1)S(1)}, u32[]{:S(2)}, u32[]{:S(2)}) collective-permute-start(bf16[128,2048]{1,0:T(8,128)(2,1)} %get-tuple-element.13), channel_id=1, source_target_pairs={{0,64},{64,128},{128,192},{192,0},{1,65},{65,129},{129,193},{193,1... | collective-permute-start | bytes 1572872 | tf_op jit(solution)/shard_map/ppermute | solution.py:20
  5.1 25.5 %collective-permute-start.1 = (bf16[128,2048]{1,0:T(8,128)(2,1)}, bf16[128,2048]{1,0:T(8,128)(2,1)S(1)}, u32[]{:S(2)}, u32[]{:S(2)}) collective-permute-start(bf16[128,2048]{1,0:T(8,128)(2,1)} %get-tuple-element.14), channel_id=1, source_target_pairs={{0,128},{64,192},{128,0},{192,64},{1,129},{65,193},{129,1},{193,65... | collective-permute-start | bytes 1572872 | tf_op jit(solution)/shard_map/ppermute | solution.py:20
  7.7 22.9 %collective-permute-start.2 = (bf16[128,2048]{1,0:T(8,128)(2,1)}, bf16[128,2048]{1,0:T(8,128)(2,1)S(1)}, u32[]{:S(2)}, u32[]{:S(2)}) collective-permute-start(bf16[128,2048]{1,0:T(8,128)(2,1)} %get-tuple-element.15), channel_id=1, source_target_pairs={{0,192},{64,0},{128,64},{192,128},{1,193},{65,1},{129,65},{193,129... | collective-permute-start | bytes 1572872 | tf_op jit(solution)/shard_map/ppermute | solution.py:20
  10.3 24.1 %all-to-all-start = ((bf16[32,16,512]{2,1,0:T(8,128)(2,1)}), bf16[32,16,512]{2,1,0:T(8,128)(2,1)}, u32[]{:S(2)}, u32[]{:S(2)}) async-start(bf16[32,16,512]{2,1,0:T(8,128)(2,1)} %bitcast.2), calls=%async_computation | async-start | bytes 1048576 | tf_op jit(solution)/shard_map/all_to_all | solution.py:309
  21.5 19.4 %copy-start.1 = (bf16[128,2048]{1,0:T(8,128)(2,1)S(1)}, bf16[128,2048]{1,0:T(8,128)(2,1)}, u32[]{:S(2)}) copy-start(bf16[128,2048]{1,0:T(8,128)(2,1)} %get-tuple-element.18.own.refs_6_) | copy-start | bytes 1572868
  35.3 7.1 %collective-permute-start.3 = (bf16[32,8,512]{2,1,0:T(8,128)(2,1)S(1)}, bf16[32,8,512]{2,1,0:T(8,128)(2,1)S(1)}, u32[]{:S(2)}, u32[]{:S(2)}) collective-permute-start(bf16[32,8,512]{2,1,0:T(8,128)(2,1)S(1)} %constant_dynamic-slice_fusion), channel_id=1, source_target_pairs={{0,1},{1,0},{2,3},{3,2},{4,5},{5,4},{6,7},{7,6},{8,9},{9,8},{10,11... | collective-permute-start | bytes 786440 | tf_op jit(solution)/shard_map/ppermute | solution.py:335
  44.8 13.4 %collective-permute-start.4 = (bf16[128,896]{1,0:T(8,128)(2,1)S(1)}, bf16[128,896]{1,0:T(8,128)(2,1)S(1)}, u32[]{:S(2)}, u32[]{:S(2)}) collective-permute-start(bf16[128,896]{1,0:T(8,128)(2,1)S(1)} %get-tuple-element.19.refs_1_), channel_id=1, source_target_pairs={{0,64},{64,128},{128,192},{192,0},{1,65},{65,129},{129,193},{193,1... | collective-permute-start | bytes 688136 | tf_op jit(solution)/shard_map/ppermute | solution.py:20
  45.3 12.9 %collective-permute-start.5 = (bf16[128,896]{1,0:T(8,128)(2,1)S(1)}, bf16[128,896]{1,0:T(8,128)(2,1)S(1)}, u32[]{:S(2)}, u32[]{:S(2)}) collective-permute-start(bf16[128,896]{1,0:T(8,128)(2,1)S(1)} %get-tuple-element.19.refs_1_), channel_id=1, source_target_pairs={{0,128},{64,192},{128,0},{192,64},{1,129},{65,193},{129,1},{193,65... | collective-permute-start | bytes 688136 | tf_op jit(solution)/shard_map/ppermute | solution.py:20
  46.1 12.5 %collective-permute-start.6 = (bf16[128,896]{1,0:T(8,128)(2,1)S(1)}, bf16[128,896]{1,0:T(8,128)(2,1)S(1)}, u32[]{:S(2)}, u32[]{:S(2)}) collective-permute-start(bf16[128,896]{1,0:T(8,128)(2,1)S(1)} %get-tuple-element.19.refs_1_), channel_id=1, source_target_pairs={{0,192},{64,0},{128,64},{192,128},{1,193},{65,1},{129,65},{193,129... | collective-permute-start | bytes 688136 | tf_op jit(solution)/shard_map/ppermute | solution.py:20
  62.3 63.3 %all-to-all-start.1 = ((bf16[256,8,512]{2,1,0:T(8,128)(2,1)}), bf16[256,8,512]{2,1,0:T(8,128)(2,1)S(1)}, u32[]{:S(2)}, u32[]{:S(2)}) async-start(bf16[256,8,512]{2,1,0:T(8,128)(2,1)} %bitcast.9), calls=%async_computation.1 | async-start | bytes 4194304 | tf_op jit(solution)/shard_map/all_to_all | solution.py:362

commit v12 on v11

--- a/solution.py
+++ b/solution.py
@@ -44,7 +44,7 @@
     return jnp.where(lines == places, 1.0, 0.0).astype(BF16)
 
 
-def block_places(shape, axis, count, core=None, only=None):
+def block_places(shape, axis, count, core=None, own=None):
     line = lax.broadcasted_iota(jnp.int32, shape, axis)
     group = line // count
     row = line % count
@@ -52,13 +52,8 @@
     peer = row // 2
     if core is None:
         return peer * (2 * GROUPS) + within
-    if only:
-        return jnp.where(peer % 2 == core, peer * (2 * GROUPS) + within, -1)
-    return jnp.where(peer % 2 == core, -1, (peer // 2) * (2 * GROUPS) + within)
-
-
-def quarter_columns(plane, steps, part, planes=4):
-    return pl.ds(pl.multiple_of(lax.rem(plane + steps, planes) * part, part), part)
+    held = peer % 2 == (core if own else 1 - core)
+    return jnp.where(held, (peer - peer % 2 + core) * (2 * GROUPS) + within, -1)
 
 
 def pack_kernel(places, hidden, out):
@@ -331,8 +326,7 @@
     )(*held[1:])
     arrived, token = lax.optimization_barrier((arrived, token))
 
-    theirs = lax.dynamic_slice(arrived, (0, (1 - core) * block, 0), (chips, block, cols))
-    others = lax.ppermute(theirs, "core", [(0, 1), (1, 0)]).reshape(chips * block, cols)
+    others = lax.ppermute(arrived, "core", [(0, 1), (1, 0)]).reshape(size, cols)
     sums, plain = call(
         products_kernel,
         (

time: 127 us -> 127 us (level)
  transfers between devices with their start and end apart: 9 -> 9, of which waited for: 5 -> 6; matrix products, arithmetic and copies ran while one was open for 0% -> 0% of each run, Pallas kernels for 2% -> 2%
where the time goes in v12:
time: 127 us
  waiting for transfers between devices  78.2 us (62%)
  starting transfers between devices  34.2 us (27%)
  Pallas kernels  13.4 us (11%)
    all_to_all x1, waiting for transfers between devices, local(): lax.all_to_all(results.reshape(sections * peers, block, cols), ('segment'...  54.7 us
    ppermute x6, waiting for transfers between devices, shifted(): lax.ppermute(value, axis, [(source, (source + steps) % count) for source...  19.5 us
    all_to_all x1, starting transfers between devices, local(): lax.all_to_all(packed.reshape(chips, 2 * block, cols), 'chip', split_axis...  11.2 us
    ppermute x6, starting transfers between devices, shifted(): lax.ppermute(value, axis, [(source, (source + steps) % count) for source...  8.86 us
    all_to_all x1, starting transfers between devices, local(): lax.all_to_all(results.reshape(sections * peers, block, cols), ('segment'...  8.79 us
    ppermute x1, starting transfers between devices, local(): others = lax.ppermute(arrived, 'core', [(0, 1), (1, 0)]).reshape(size, cols)  5.38 us
    all_to_all x1, waiting for transfers between devices, local(): lax.all_to_all(packed.reshape(chips, 2 * block, cols), 'chip', split_axis...  3.76 us
    pallas_call x1, Pallas kernels, local(): call(lambda *refs: sections_kernel(width, *refs), jax.ShapeDtypeStruct((s...  3.72 us
  transfers between devices with their start and end apart: 9, of which 6 were waited for; matrix products, arithmetic and copies ran while one was open for 0% of the time, Pallas kernels for 2%

profile of v12, /device:TPU:1, one launch (start us, length us, event | category | flops | bytes accessed | tf_op | source)
XLA Modules:
  0.0 126.5 jit_solution(8981438746033157666)
XLA Ops:
  0.0 0.0 copy-start
  0.0 2.9 %quarters.1 = (bf16[128,2048]{1,0:T(8,128)(2,1)}, bf16[128,2048]{1,0:T(8,128)(2,1)}, bf16[128,2048]{1,0:T(8,128)(2,1)}, bf16[128,2048]{1,0:T(8,128)(2,1)}) custom-call(s32[1]{0:T(128)} %bitcast.3.plane, bf16[64,8192]{1,0:T(8,128)(2,1)} %bitcast.14, f32[1,8192]{1,0:T(1,128)} %gain.1, bf16[64,8192]{1,0:T(8,128)(2,1)} %bitcast.15), custom_call_target="tpu_custom_call" | custom-call | bytes 4194304 | tf_op jit(solution)/shard_map/quarters/pallas_call | solution.py:265
  2.9 2.2 %collective-permute-start = (bf16[128,2048]{1,0:T(8,128)(2,1)}, bf16[128,2048]{1,0:T(8,128)(2,1)S(1)}, u32[]{:S(2)}, u32[]{:S(2)}) collective-permute-start(bf16[128,2048]{1,0:T(8,128)(2,1)} %get-tuple-element.13), channel_id=1, source_target_pairs={{0,64},{64,128},{128,192},{192,0},{1,65},{65,129},{129,193},{193,1... | collective-permute-start | bytes 1572872 | tf_op jit(solution)/shard_map/ppermute | solution.py:20
  5.1 2.6 %collective-permute-start.1 = (bf16[128,2048]{1,0:T(8,128)(2,1)}, bf16[128,2048]{1,0:T(8,128)(2,1)S(1)}, u32[]{:S(2)}, u32[]{:S(2)}) collective-permute-start(bf16[128,2048]{1,0:T(8,128)(2,1)} %get-tuple-element.14), channel_id=1, source_target_pairs={{0,128},{64,192},{128,0},{192,64},{1,129},{65,193},{129,1},{193,65... | collective-permute-start | bytes 1572872 | tf_op jit(solution)/shard_map/ppermute | solution.py:20
  7.7 1.1 collective-permute-start.2
  8.8 0.2 select_reduce_fusion
  9.0 0.1 broadcast_add_fusion
  9.1 0.1 add.55.places
  9.2 1.1 pack.1
  10.3 11.2 %all-to-all-start = ((bf16[32,16,512]{2,1,0:T(8,128)(2,1)}), bf16[32,16,512]{2,1,0:T(8,128)(2,1)}, u32[]{:S(2)}, u32[]{:S(2)}) async-start(bf16[32,16,512]{2,1,0:T(8,128)(2,1)} %bitcast.2), calls=%async_computation | async-start | bytes 1048576 | tf_op jit(solution)/shard_map/all_to_all | solution.py:304
  21.5 0.0 copy-start.1
  21.5 0.0 collective-permute-done.first.refs_7_
  21.5 9.1 %collective-permute-done.1.second.refs_8_ = bf16[128,2048]{1,0:T(8,128)(2,1)S(1)} collective-permute-done((bf16[128,2048]{1,0:T(8,128)(2,1)}, bf16[128,2048]{1,0:T(8,128)(2,1)S(1)}, u32[]{:S(2)}, u32[]{:S(2)}) %collective-permute-start.1) | collective-permute-done | bytes 524320 | tf_op jit(solution)/shard_map/ppermute | solution.py:20
  30.6 0.0 collective-permute-done.2.third.refs_9_
  30.6 3.8 %all-to-all-done = bf16[32,16,512]{2,1,0:T(8,128)(2,1)} async-done(((bf16[32,16,512]{2,1,0:T(8,128)(2,1)}), bf16[32,16,512]{2,1,0:T(8,128)(2,1)}, u32[]{:S(2)}, u32[]{:S(2)}) %all-to-all-start) | async-done | bytes 524320 | tf_op jit(solution)/shard_map/all_to_all | solution.py:304
  34.4 5.4 %collective-permute-start.3 = (bf16[32,16,512]{2,1,0:T(8,128)(2,1)}, bf16[32,16,512]{2,1,0:T(8,128)(2,1)}, u32[]{:S(2)}, u32[]{:S(2)}) collective-permute-start(bf16[32,16,512]{2,1,0:T(8,128)(2,1)} %all-to-all-done), channel_id=1, source_target_pairs={{0,1},{1,0},{2,3},{3,2},{4,5},{5,4},{6,7},{7,6},{8,9},{9,8},{10,11... | collective-permute-start | bytes 1572872 | tf_op jit(solution)/shard_map/ppermute | solution.py:329
  39.8 0.1 pad_add_fusion.order.refs_0_
  39.8 0.0 copy-done.1
  39.8 1.5 %factors.1.tiles = f32[384,128]{1,0:T(8,128)S(1)} custom-call(s32[5]{0:T(128)S(1)} %pad_add_fusion.order.refs_0_, bf16[128,2048]{1,0:T(8,128)(2,1)S(1)} %copy-done.1, bf16[128,2048]{1,0:T(8,128)(2,1)S(1)} %collective-permute-done.first.refs_7_, bf16[128,2048]{1,0:T(8,128)(2,1)S(1)} %collective-permute-done.1.second.refs_8_, ...), custom_call_target="tpu_custom_call" | custom-call | bytes 4194304 | tf_op jit(solution)/shard_map/factors/pallas_call | solution.py:310
  41.4 0.2 collective-permute-done.3
  41.6 2.7 %products.1 = (bf16[128,896]{1,0:T(8,128)(2,1)S(1)}, bf16[128,2048]{1,0:T(8,128)(2,1)S(1)}) custom-call(s32[5]{0:T(128)S(1)} %pad_add_fusion.order.refs_0_, f32[8,128]{1,0:T(8,128)S(1)} %landed.1.token, bf16[512,512]{1,0:T(8,128)(2,1)} %bitcast.7.blocks, bf16[512,512]{1,0:T(8,128)(2,1)} %bitcast.8.others, f32[384,128]{1,0:T(8,128)S(1)} %factors.1.tiles, ...), custom_call_target="tpu_custom_call" | custom-call | bytes 4194304 | tf_op jit(solution)/shard_map/products/pallas_call | solution.py:330
  44.3 0.5 collective-permute-start.4
  44.8 0.8 collective-permute-start.5
  45.5 1.7 %collective-permute-start.6 = (bf16[128,896]{1,0:T(8,128)(2,1)S(1)}, bf16[128,896]{1,0:T(8,128)(2,1)S(1)}, u32[]{:S(2)}, u32[]{:S(2)}) collective-permute-start(bf16[128,896]{1,0:T(8,128)(2,1)S(1)} %get-tuple-element.19.refs_1_), channel_id=1, source_target_pairs={{0,192},{64,0},{128,64},{192,128},{1,193},{65,1},{129,65},{193,129... | collective-permute-start | bytes 688136 | tf_op jit(solution)/shard_map/ppermute | solution.py:20
  47.3 10.1 %collective-permute-done.4.refs_2_ = bf16[128,896]{1,0:T(8,128)(2,1)S(1)} collective-permute-done((bf16[128,896]{1,0:T(8,128)(2,1)S(1)}, bf16[128,896]{1,0:T(8,128)(2,1)S(1)}, u32[]{:S(2)}, u32[]{:S(2)}) %collective-permute-start.4) | collective-permute-done | bytes 229408 | tf_op jit(solution)/shard_map/ppermute | solution.py:20
  57.3 0.0 collective-permute-done.5.refs_3_
  57.3 0.3 collective-permute-done.6.refs_4_
  57.7 3.7 %sections.1 = bf16[2048,512]{1,0:T(8,128)(2,1)} custom-call(s32[5]{0:T(128)S(1)} %pad_add_fusion.order.refs_0_, bf16[128,896]{1,0:T(8,128)(2,1)S(1)} %get-tuple-element.19.refs_1_, bf16[128,896]{1,0:T(8,128)(2,1)S(1)} %collective-permute-done.4.refs_2_, bf16[128,896]{1,0:T(8,128)(2,1)S(1)} %collective-permute-done.5.refs_3_, ...), custom_call_target="tpu_custom_call" | custom-call | bytes 4194304 | tf_op jit(solution)/shard_map/sections/pallas_call | solution.py:342
  61.4 8.8 %all-to-all-start.1 = ((bf16[256,8,512]{2,1,0:T(8,128)(2,1)}), bf16[256,8,512]{2,1,0:T(8,128)(2,1)S(1)}, u32[]{:S(2)}, u32[]{:S(2)}) async-start(bf16[256,8,512]{2,1,0:T(8,128)(2,1)} %bitcast.9), calls=%async_computation.1 | async-start | bytes 4194304 | tf_op jit(solution)/shard_map/all_to_all | solution.py:356
  70.2 0.1 add.57.places
  70.3 54.7 %all-to-all-done.1 = bf16[256,8,512]{2,1,0:T(8,128)(2,1)S(1)} async-done(((bf16[256,8,512]{2,1,0:T(8,128)(2,1)}), bf16[256,8,512]{2,1,0:T(8,128)(2,1)S(1)}, u32[]{:S(2)}, u32[]{:S(2)}) %all-to-all-start.1) | async-done | bytes 2097184 | tf_op jit(solution)/shard_map/all_to_all | solution.py:356
  125.0 1.5 %unpack.1 = bf16[64,8192]{1,0:T(8,128)(2,1)} custom-call(s32[256,1]{1,0:T(8,128)S(1)} %add.57.places, bf16[4,512,512]{2,1,0:T(8,128)(2,1)S(1)} %bitcast.13), custom_call_target="tpu_custom_call" | custom-call | bytes 4194304 | tf_op jit(solution)/shard_map/unpack/pallas_call | solution.py:363
  (10 shorter events, 0.0 us)
Async XLA Ops:
  0.0 9.2 %copy-start = (bf16[64,8192]{1,0:T(8,128)(2,1)S(1)}, bf16[64,8192]{1,0:T(8,128)(2,1)}, u32[]{:S(2)}) copy-start(bf16[64,8192]{1,0:T(8,128)(2,1)} %param.6) | copy-start | bytes 3145732
  0.0 8.8 %copy-start.2 = (s32[64,1]{0,1:T(1,128)S(1)}, s32[64,1]{0,1:T(1,128)}, u32[]{:S(2)}) copy-start(s32[64,1]{0,1:T(1,128)} %param.7) | copy-start | bytes 772
  0.0 8.8 %copy-start.3 = (s32[64]{0:T(128)S(1)}, s32[64]{0:T(128)}, u32[]{:S(2)}) copy-start(s32[64]{0:T(128)} %param.8) | copy-start | bytes 772
  2.9 18.6 %collective-permute-start = (bf16[128,2048]{1,0:T(8,128)(2,1)}, bf16[128,2048]{1,0:T(8,128)(2,1)S(1)}, u32[]{:S(2)}, u32[]{:S(2)}) collective-permute-start(bf16[128,2048]{1,0:T(8,128)(2,1)} %get-tuple-element.13), channel_id=1, source_target_pairs={{0,64},{64,128},{128,192},{192,0},{1,65},{65,129},{129,193},{193,1... | collective-permute-start | bytes 1572872 | tf_op jit(solution)/shard_map/ppermute | solution.py:20
  5.1 25.5 %collective-permute-start.1 = (bf16[128,2048]{1,0:T(8,128)(2,1)}, bf16[128,2048]{1,0:T(8,128)(2,1)S(1)}, u32[]{:S(2)}, u32[]{:S(2)}) collective-permute-start(bf16[128,2048]{1,0:T(8,128)(2,1)} %get-tuple-element.14), channel_id=1, source_target_pairs={{0,128},{64,192},{128,0},{192,64},{1,129},{65,193},{129,1},{193,65... | collective-permute-start | bytes 1572872 | tf_op jit(solution)/shard_map/ppermute | solution.py:20
  7.7 22.9 %collective-permute-start.2 = (bf16[128,2048]{1,0:T(8,128)(2,1)}, bf16[128,2048]{1,0:T(8,128)(2,1)S(1)}, u32[]{:S(2)}, u32[]{:S(2)}) collective-permute-start(bf16[128,2048]{1,0:T(8,128)(2,1)} %get-tuple-element.15), channel_id=1, source_target_pairs={{0,192},{64,0},{128,64},{192,128},{1,193},{65,1},{129,65},{193,129... | collective-permute-start | bytes 1572872 | tf_op jit(solution)/shard_map/ppermute | solution.py:20
  10.3 24.1 %all-to-all-start = ((bf16[32,16,512]{2,1,0:T(8,128)(2,1)}), bf16[32,16,512]{2,1,0:T(8,128)(2,1)}, u32[]{:S(2)}, u32[]{:S(2)}) async-start(bf16[32,16,512]{2,1,0:T(8,128)(2,1)} %bitcast.2), calls=%async_computation | async-start | bytes 1048576 | tf_op jit(solution)/shard_map/all_to_all | solution.py:304
  21.5 18.4 %copy-start.1 = (bf16[128,2048]{1,0:T(8,128)(2,1)S(1)}, bf16[128,2048]{1,0:T(8,128)(2,1)}, u32[]{:S(2)}) copy-start(bf16[128,2048]{1,0:T(8,128)(2,1)} %get-tuple-element.18.own.refs_6_) | copy-start | bytes 1572868
  34.4 7.3 %collective-permute-start.3 = (bf16[32,16,512]{2,1,0:T(8,128)(2,1)}, bf16[32,16,512]{2,1,0:T(8,128)(2,1)}, u32[]{:S(2)}, u32[]{:S(2)}) collective-permute-start(bf16[32,16,512]{2,1,0:T(8,128)(2,1)} %all-to-all-done), channel_id=1, source_target_pairs={{0,1},{1,0},{2,3},{3,2},{4,5},{5,4},{6,7},{7,6},{8,9},{9,8},{10,11... | collective-permute-start | bytes 1572872 | tf_op jit(solution)/shard_map/ppermute | solution.py:329
  44.3 13.0 %collective-permute-start.4 = (bf16[128,896]{1,0:T(8,128)(2,1)S(1)}, bf16[128,896]{1,0:T(8,128)(2,1)S(1)}, u32[]{:S(2)}, u32[]{:S(2)}) collective-permute-start(bf16[128,896]{1,0:T(8,128)(2,1)S(1)} %get-tuple-element.19.refs_1_), channel_id=1, source_target_pairs={{0,64},{64,128},{128,192},{192,0},{1,65},{65,129},{129,193},{193,1... | collective-permute-start | bytes 688136 | tf_op jit(solution)/shard_map/ppermute | solution.py:20
  44.8 12.6 %collective-permute-start.5 = (bf16[128,896]{1,0:T(8,128)(2,1)S(1)}, bf16[128,896]{1,0:T(8,128)(2,1)S(1)}, u32[]{:S(2)}, u32[]{:S(2)}) collective-permute-start(bf16[128,896]{1,0:T(8,128)(2,1)S(1)} %get-tuple-element.19.refs_1_), channel_id=1, source_target_pairs={{0,128},{64,192},{128,0},{192,64},{1,129},{65,193},{129,1},{193,65... | collective-permute-start | bytes 688136 | tf_op jit(solution)/shard_map/ppermute | solution.py:20
  45.5 12.1 %collective-permute-start.6 = (bf16[128,896]{1,0:T(8,128)(2,1)S(1)}, bf16[128,896]{1,0:T(8,128)(2,1)S(1)}, u32[]{:S(2)}, u32[]{:S(2)}) collective-permute-start(bf16[128,896]{1,0:T(8,128)(2,1)S(1)} %get-tuple-element.19.refs_1_), channel_id=1, source_target_pairs={{0,192},{64,0},{128,64},{192,128},{1,193},{65,1},{129,65},{193,129... | collective-permute-start | bytes 688136 | tf_op jit(solution)/shard_map/ppermute | solution.py:20
  61.4 63.6 %all-to-all-start.1 = ((bf16[256,8,512]{2,1,0:T(8,128)(2,1)}), bf16[256,8,512]{2,1,0:T(8,128)(2,1)S(1)}, u32[]{:S(2)}, u32[]{:S(2)}) async-start(bf16[256,8,512]{2,1,0:T(8,128)(2,1)} %bitcast.9), calls=%async_computation.1 | async-start | bytes 4194304 | tf_op jit(solution)/shard_map/all_to_all | solution.py:356
